TPU v7x, 32 devices: a whole 2x2x4 slice. The times are simulated.
32 devices in a mesh: replica: 16 (over z, y, core), fsdp: 2 (over x).
Axes of the slice: x: 2, y: 2, z: 4, core: 2. Of those that a mesh axis runs over, the one named last changes fastest.
Arguments:
- inputs: bfloat16 [16384, 1024], P(('replica', 'fsdp')), may hold values from -6 to 6
- segments: int32 [16, 1024], P('replica', 'fsdp'), may hold values from 0 to 66, as said below
- cotangent: bfloat16 [16384, 1024], P(('replica', 'fsdp')), may hold values from -6 to 6
- mixer_gain: bfloat16 [1024], P('fsdp'), may hold values from 0.5 to 1.5
- query_map: bfloat16 [1024, 512], P('fsdp'), may hold values from -0.1875 to 0.1875
- key_map: bfloat16 [1024, 512], P('fsdp'), may hold values from -0.1875 to 0.1875
- value_map: bfloat16 [1024, 1024], P('fsdp'), may hold values from -0.1875 to 0.1875
- swish_map: bfloat16 [1024, 1024], P('fsdp'), may hold values from -0.1875 to 0.1875
- squeeze: bfloat16 [1024, 16], P('fsdp'), may hold values from -0.1875 to 0.1875
- expand: bfloat16 [16, 512], P(None, 'fsdp'), may hold values from -1.5 to 1.5
- forget_bias: bfloat16 [512], P('fsdp'), may hold values from -2 to 6
- head_gain: bfloat16 [256], P('fsdp'), may hold values from 0.5 to 1.5
- readout: bfloat16 [1024, 1024], P('fsdp'), may hold values from -0.25 to 0.25
- feed_gain: bfloat16 [1024], P('fsdp'), may hold values from 0.5 to 1.5
- gate_map: bfloat16 [1024, 2816], P('fsdp'), may hold values from -0.1875 to 0.1875
- up_map: bfloat16 [1024, 2816], P('fsdp'), may hold values from -0.1875 to 0.1875
- down_map: bfloat16 [2816, 1024], P('fsdp'), may hold values from -0.21875 to 0.21875
Outputs:
- output: bfloat16 [16384, 1024], P(('replica', 'fsdp'))
- grad_input: bfloat16 [16384, 1024], P(('replica', 'fsdp'))
- grad_mixer: float32 [1024], P('fsdp')
- grad_query: float32 [1024, 512], P('fsdp')
- grad_key: float32 [1024, 512], P('fsdp')
- grad_value: float32 [1024, 1024], P('fsdp')
- grad_swish: float32 [1024, 1024], P('fsdp')
- grad_squeeze: float32 [1024, 16], P('fsdp')
- grad_expand: float32 [16, 512], P(None, 'fsdp')
- grad_bias: float32 [512], P('fsdp')
- grad_heads: float32 [256], P('fsdp')
- grad_readout: float32 [1024, 1024], P('fsdp')
- grad_feed: float32 [1024], P('fsdp')
- grad_gate: float32 [1024, 2816], P('fsdp')
- grad_up: float32 [1024, 2816], P('fsdp')
- grad_down: float32 [2816, 1024], P('fsdp')
Inputs may be any that keep to these rules, and one draw needn't show every extreme that they name: `segments`: along each sequence the document numbers start at 0 and rise by 0 or 1 from token to token; in every sequence one document begins among the first 512 tokens and ends among the last 512, and the last token's number is 66.
All inputs are finite; a program needn't handle non-finite values.
Results may differ from a plain program's by a relative error of at most 0.035.
Values may be sent and summed in bfloat16 or wider, within the bound.
No kernel may reach another device: no remote copies, remote signals or barrier semaphores. Data moves between devices by JAX's collectives and lax.ppermute only.
A program may use at most 192 MiB of HBM per device.

v0:
```python
import jax
import jax.numpy as jnp
from jax import lax
from jax.sharding import PartitionSpec as P

HEADS = 4
DK = 128
DV = 256
SPAN = 64


EPSILON = 1e-06
HEAD_FLOOR = 16.0
GATE_NORM = 16.0
HIGH = lax.Precision.HIGHEST


def carried_in(x, axis, join, neutral):
    place = lax.axis_index(axis)
    gathered = jax.tree.map(
        lambda a, kind: lax.all_gather(a.astype(kind), axis),
        x,
        (jnp.bfloat16, jnp.bfloat16, jnp.bfloat16, jnp.bfloat16),
    )
    state = jax.tree.map(lambda a, e: jnp.zeros_like(a) + jnp.asarray(e, a.dtype), x, neutral)

    def carried_one(turn, state):
        return join(
            state,
            jax.tree.map(
                lambda a, own: lax.dynamic_index_in_dim(a, turn, 0, False).astype(own.dtype),
                gathered,
                x,
            ),
        )

    return lax.fori_loop(0, place, carried_one, state)


def entering(x, axis, join, neutral):
    count = lax.axis_size(axis)
    place = lax.axis_index(axis)
    ahead = count - 1 - place
    gathered = jax.tree.map(
        lambda a, kind: lax.all_gather(a.astype(kind), axis),
        x,
        jax.tree.map(lambda a: jnp.bfloat16 if a.dtype == jnp.float32 else a.dtype, x),
    )
    state = jax.tree.map(lambda a, e: jnp.zeros_like(a) + jnp.asarray(e, a.dtype), x, neutral)

    def entering_one(turn, state):
        source = count - 1 - turn
        return join(
            state,
            jax.tree.map(
                lambda a, own: lax.dynamic_index_in_dim(a, source, 0, False).astype(own.dtype),
                gathered,
                x,
            ),
        )

    return lax.fori_loop(0, ahead, entering_one, state)


def product(form, left, right):
    return jnp.einsum(form, left, right, preferred_element_type=jnp.float32)


def rms_scale(values, gain):
    mean_sq = jnp.mean(values * values, axis=-1, keepdims=True)
    return values * lax.rsqrt(mean_sq + EPSILON) * gain


def head_scale(values, gain):
    mean_sq = jnp.mean(values * values, axis=-1, keepdims=True)
    return values * lax.rsqrt(mean_sq + HEAD_FLOOR) * gain


def block_step(carry, block):
    state, last = carry
    queries, keys, values, decay, marks = block
    cumul = jnp.cumsum(decay, axis=0)
    width = marks.shape[0]
    places = jnp.arange(width)
    causal = (places[:, None] >= places[None, :]) & (marks[:, None] == marks[None, :])
    lifted = queries * jnp.exp(cumul)
    lowered = keys * jnp.exp(-cumul)
    scores = jnp.einsum("thc,shc->hts", lifted, lowered, precision=HIGH)
    scores = jnp.where(causal[None], scores, 0.0)
    within = jnp.einsum("hts,shv->thv", scores, values, precision=HIGH)
    carried = jnp.where((marks == last)[:, None, None], lifted, 0.0)
    across = jnp.einsum("thc,hcv->thv", carried, state, precision=HIGH)
    tail = jnp.where(
        (marks == marks[-1])[:, None, None], jnp.exp(cumul[-1][None] - cumul) * keys, 0.0
    )
    keeping = jnp.where(marks[-1] == last, jnp.exp(cumul[-1]), 0.0)
    state = keeping[:, :, None] * state + jnp.einsum("shc,shv->hcv", tail, values, precision=HIGH)
    return ((state, marks[-1]), within + across)


def recurrence(queries, keys, values, decay, marks):
    length = marks.shape[0]
    count = length // SPAN
    blocks = (
        queries.reshape(count, SPAN, HEADS, DK),
        keys.reshape(count, SPAN, HEADS, DK),
        values.reshape(count, SPAN, HEADS, DV),
        decay.reshape(count, SPAN, HEADS, DK),
        marks.reshape(count, SPAN),
    )
    start = (jnp.zeros((HEADS, DK, DV), jnp.float32), marks[0])
    final, mixed = lax.scan(jax.checkpoint(block_step), start, blocks)
    passing = jnp.where(marks[0] == marks[-1], jnp.exp(jnp.sum(decay, axis=0)), 0.0)
    return (mixed.reshape(length, HEADS, DV), final[0], passing)


def carried_term(queries, decay, marks, state, last):
    cumul = jnp.cumsum(decay, axis=0)
    carried = jnp.where((marks == last)[:, None, None], queries * jnp.exp(cumul), 0.0)
    return jnp.einsum("thc,hcv->thv", carried, state, precision=HIGH)


def chain_join(earlier, later):
    factor_early, state_early, first_early, last_early = earlier
    factor_late, state_late, first_late, last_late = later
    joined = (first_late == last_early) | (last_early < 0) | (first_late < 0)
    linked = jnp.where(joined, factor_late, 0.0)
    return (
        linked * factor_early,
        linked[..., None] * state_early + state_late,
        jnp.where(first_early < 0, first_late, first_early),
        jnp.where(last_late < 0, last_early, last_late),
    )


def grad_join(earlier, later):
    factor_early, grad_early = earlier
    factor_late, grad_late = later
    return (factor_late * factor_early, grad_late + factor_late[..., None] * grad_early)


def gate_piece(mixed, swish_pre, gain):
    return head_scale(mixed, gain) * jax.nn.silu(swish_pre)


def act_piece(gate, upward):
    return jax.nn.silu(gate) * upward


def decay_piece(decay_pre):
    return jax.nn.log_sigmoid(decay_pre) / GATE_NORM


def on_device(
    inputs,
    segments,
    cotangent,
    mixer_gain,
    query_map,
    key_map,
    value_map,
    swish_map,
    squeeze,
    expand,
    forget_bias,
    head_gain,
    readout,
    feed_gain,
    gate_map,
    up_map,
    down_map,
):
    weights = (
        lax.all_gather(mixer_gain, "fsdp", axis=0, tiled=True),
        lax.all_gather(query_map, "fsdp", axis=0, tiled=True),
        lax.all_gather(key_map, "fsdp", axis=0, tiled=True),
        lax.all_gather(value_map, "fsdp", axis=0, tiled=True),
        lax.all_gather(swish_map, "fsdp", axis=0, tiled=True),
        lax.all_gather(squeeze, "fsdp", axis=0, tiled=True),
        lax.all_gather(expand, "fsdp", axis=1, tiled=True),
        lax.all_gather(forget_bias, "fsdp", axis=0, tiled=True),
        lax.all_gather(head_gain, "fsdp", axis=0, tiled=True),
        lax.all_gather(readout, "fsdp", axis=0, tiled=True),
        lax.all_gather(feed_gain, "fsdp", axis=0, tiled=True),
        lax.all_gather(gate_map, "fsdp", axis=0, tiled=True),
        lax.all_gather(up_map, "fsdp", axis=0, tiled=True),
        lax.all_gather(down_map, "fsdp", axis=0, tiled=True),
    )
    length = inputs.shape[0]
    tokens = inputs.astype(jnp.float32)
    marks = segments[0].astype(jnp.float32)
    mixer_float = weights[0].astype(jnp.float32)
    normed_float, mixer_back = jax.vjp(rms_scale, tokens, mixer_float)
    normed = normed_float.astype(jnp.bfloat16)
    queries = product("td,dk->tk", normed, weights[1]).astype(jnp.bfloat16)
    keys = product("td,dk->tk", normed, weights[2]).astype(jnp.bfloat16)
    values = product("td,dk->tk", normed, weights[3]).astype(jnp.bfloat16)
    swish_pre = product("td,dk->tk", normed, weights[4]).reshape(length, HEADS, DV)
    narrow = product("td,dr->tr", normed, weights[5]).astype(jnp.bfloat16)
    decay_pre = product("tr,rk->tk", narrow, weights[6]) + weights[7].astype(jnp.float32)
    decay_flat, decay_back = jax.vjp(decay_piece, decay_pre)
    decay = decay_flat.reshape(length, HEADS, DK)
    query_float = queries.astype(jnp.float32).reshape(length, HEADS, DK)
    key_float = keys.astype(jnp.float32).reshape(length, HEADS, DK)
    value_float = values.astype(jnp.float32).reshape(length, HEADS, DV)

    def local_piece(query_part, key_part, value_part, decay_part):
        return recurrence(query_part, key_part, value_part, decay_part, marks)

    (local_mixed, local_state, passing), local_back = jax.vjp(
        local_piece, query_float, key_float, value_float, decay
    )
    minus_one = -jnp.ones((1,), jnp.float32)
    chained = carried_in(
        (passing, local_state, marks[:1], marks[-1:]),
        "fsdp",
        chain_join,
        (jnp.ones_like(passing), jnp.zeros_like(local_state), minus_one, minus_one),
    )
    state_in = chained[1]
    last_in = chained[3][0]

    def carry_piece(query_part, decay_part, state_part):
        return carried_term(query_part, decay_part, marks, state_part, last_in)

    carried, carry_back = jax.vjp(carry_piece, query_float, decay, state_in)
    mixed = local_mixed + carried
    head_float = weights[8].astype(jnp.float32)
    gated_float, gate_back = jax.vjp(gate_piece, mixed, swish_pre, head_float)
    gated = gated_float.reshape(length, HEADS * DV).astype(jnp.bfloat16)
    hidden = tokens + product("tv,vd->td", gated, weights[9])
    feed_float = weights[10].astype(jnp.float32)
    second_float, feed_back = jax.vjp(rms_scale, hidden, feed_float)
    second = second_float.astype(jnp.bfloat16)
    gate = product("td,df->tf", second, weights[11])
    upward = product("td,df->tf", second, weights[12])
    inner_float, act_back = jax.vjp(act_piece, gate, upward)
    inner = inner_float.astype(jnp.bfloat16)
    output = (hidden + product("tf,fd->td", inner, weights[13])).astype(jnp.bfloat16)
    grad_down = product("tf,td->fd", inner, cotangent)
    grad_inner = product("td,fd->tf", cotangent, weights[13])
    grad_gate_float, grad_up_float = act_back(grad_inner)
    gate_low = grad_gate_float.astype(jnp.bfloat16)
    up_low = grad_up_float.astype(jnp.bfloat16)
    grad_gate = product("td,tf->df", second, gate_low)
    grad_up = product("td,tf->df", second, up_low)
    grad_second = product("tf,df->td", gate_low, weights[11]) + product(
        "tf,df->td", up_low, weights[12]
    )
    grad_hidden_norm, grad_feed = feed_back(grad_second)
    grad_hidden = cotangent.astype(jnp.float32) + grad_hidden_norm
    hidden_low = grad_hidden.astype(jnp.bfloat16)
    grad_readout = product("tv,td->vd", gated, hidden_low)
    grad_gated = product("td,vd->tv", hidden_low, weights[9]).reshape(length, HEADS, DV)
    grad_mixed, grad_swish_pre, grad_heads = gate_back(grad_gated)
    swish_low = grad_swish_pre.reshape(length, HEADS * DV).astype(jnp.bfloat16)
    grad_query_carry, grad_decay_carry, grad_state_local = carry_back(grad_mixed)
    linked = jnp.where(marks[0] == last_in, passing, 0.0)
    later = entering(
        (linked, grad_state_local),
        "fsdp",
        grad_join,
        (jnp.ones_like(linked), jnp.zeros_like(grad_state_local)),
    )
    grad_out_state = later[1]
    grad_passing = jnp.where(marks[0] == last_in, jnp.sum(grad_out_state * state_in, axis=-1), 0.0)
    grad_query_local, grad_key_float, grad_value_float, grad_decay_local = local_back(
        (grad_mixed, grad_out_state, grad_passing)
    )
    query_low = (
        (grad_query_carry + grad_query_local).reshape(length, HEADS * DK).astype(jnp.bfloat16)
    )
    key_low = grad_key_float.reshape(length, HEADS * DK).astype(jnp.bfloat16)
    value_low = grad_value_float.reshape(length, HEADS * DV).astype(jnp.bfloat16)
    grad_decay = (grad_decay_carry + grad_decay_local).reshape(length, HEADS * DK)
    grad_decay_pre = decay_back(grad_decay)[0]
    grad_bias = jnp.sum(grad_decay_pre, axis=0)
    pre_low = grad_decay_pre.astype(jnp.bfloat16)
    grad_expand = product("tr,tk->rk", narrow, pre_low)
    narrow_low = product("tk,rk->tr", pre_low, weights[6]).astype(jnp.bfloat16)
    grad_squeeze = product("td,tr->dr", normed, narrow_low)
    grad_query = product("td,tk->dk", normed, query_low)
    grad_key = product("td,tk->dk", normed, key_low)
    grad_value = product("td,tk->dk", normed, value_low)
    grad_swish = product("td,tk->dk", normed, swish_low)
    grad_normed = (
        product("tk,dk->td", query_low, weights[1])
        + product("tk,dk->td", key_low, weights[2])
        + product("tk,dk->td", value_low, weights[3])
        + product("tk,dk->td", swish_low, weights[4])
        + product("tr,dr->td", narrow_low, weights[5])
    )
    grad_tokens_norm, grad_mixer = mixer_back(grad_normed)
    grad_input = (grad_hidden + grad_tokens_norm).astype(jnp.bfloat16)
    parts = (
        lax.psum_scatter(
            grad_mixer.astype(jnp.bfloat16), "fsdp", scatter_dimension=0, tiled=True
        ).astype(jnp.float32),
        lax.psum_scatter(
            grad_query.astype(jnp.bfloat16), "fsdp", scatter_dimension=0, tiled=True
        ).astype(jnp.float32),
        lax.psum_scatter(
            grad_key.astype(jnp.bfloat16), "fsdp", scatter_dimension=0, tiled=True
        ).astype(jnp.float32),
        lax.psum_scatter(
            grad_value.astype(jnp.bfloat16), "fsdp", scatter_dimension=0, tiled=True
        ).astype(jnp.float32),
        lax.psum_scatter(
            grad_swish.astype(jnp.bfloat16), "fsdp", scatter_dimension=0, tiled=True
        ).astype(jnp.float32),
        lax.psum_scatter(
            grad_squeeze.astype(jnp.bfloat16), "fsdp", scatter_dimension=0, tiled=True
        ).astype(jnp.float32),
        lax.psum_scatter(
            grad_expand.astype(jnp.bfloat16), "fsdp", scatter_dimension=1, tiled=True
        ).astype(jnp.float32),
        lax.psum_scatter(
            grad_bias.astype(jnp.bfloat16), "fsdp", scatter_dimension=0, tiled=True
        ).astype(jnp.float32),
        lax.psum_scatter(
            grad_heads.astype(jnp.bfloat16), "fsdp", scatter_dimension=0, tiled=True
        ).astype(jnp.float32),
        lax.psum_scatter(
            grad_readout.astype(jnp.bfloat16), "fsdp", scatter_dimension=0, tiled=True
        ).astype(jnp.float32),
        lax.psum_scatter(
            grad_feed.astype(jnp.bfloat16), "fsdp", scatter_dimension=0, tiled=True
        ).astype(jnp.float32),
        lax.psum_scatter(
            grad_gate.astype(jnp.bfloat16), "fsdp", scatter_dimension=0, tiled=True
        ).astype(jnp.float32),
        lax.psum_scatter(
            grad_up.astype(jnp.bfloat16), "fsdp", scatter_dimension=0, tiled=True
        ).astype(jnp.float32),
        lax.psum_scatter(
            grad_down.astype(jnp.bfloat16), "fsdp", scatter_dimension=0, tiled=True
        ).astype(jnp.float32),
    )
    summed = (
        lax.psum(parts[0].astype(jnp.bfloat16), "replica").astype(jnp.float32),
        lax.psum(parts[1].astype(jnp.bfloat16), "replica").astype(jnp.float32),
        lax.psum(parts[2].astype(jnp.bfloat16), "replica").astype(jnp.float32),
        lax.psum(parts[3].astype(jnp.bfloat16), "replica").astype(jnp.float32),
        lax.psum(parts[4].astype(jnp.bfloat16), "replica").astype(jnp.float32),
        lax.psum(parts[5].astype(jnp.bfloat16), "replica").astype(jnp.float32),
        lax.psum(parts[6].astype(jnp.bfloat16), "replica").astype(jnp.float32),
        lax.psum(parts[7].astype(jnp.bfloat16), "replica").astype(jnp.float32),
        lax.psum(parts[8].astype(jnp.bfloat16), "replica").astype(jnp.float32),
        lax.psum(parts[9].astype(jnp.bfloat16), "replica").astype(jnp.float32),
        lax.psum(parts[10].astype(jnp.bfloat16), "replica").astype(jnp.float32),
        lax.psum(parts[11].astype(jnp.bfloat16), "replica").astype(jnp.float32),
        lax.psum(parts[12].astype(jnp.bfloat16), "replica").astype(jnp.float32),
        lax.psum(parts[13].astype(jnp.bfloat16), "replica").astype(jnp.float32),
    )
    return (
        output,
        grad_input,
        summed[0],
        summed[1],
        summed[2],
        summed[3],
        summed[4],
        summed[5],
        summed[6],
        summed[7],
        summed[8],
        summed[9],
        summed[10],
        summed[11],
        summed[12],
        summed[13],
    )


def solution(mesh):
    placed = (
        P(("replica", "fsdp"), None),
        P("replica", "fsdp"),
        P(("replica", "fsdp"), None),
        P("fsdp"),
        P("fsdp", None),
        P("fsdp", None),
        P("fsdp", None),
        P("fsdp", None),
        P("fsdp", None),
        P(None, "fsdp"),
        P("fsdp"),
        P("fsdp"),
        P("fsdp", None),
        P("fsdp"),
        P("fsdp", None),
        P("fsdp", None),
        P("fsdp", None),
    )
    return jax.shard_map(
        on_device,
        mesh=mesh,
        in_specs=placed,
        out_specs=(
            P(("replica", "fsdp"), None),
            P(("replica", "fsdp"), None),
            P("fsdp"),
            P("fsdp", None),
            P("fsdp", None),
            P("fsdp", None),
            P("fsdp", None),
            P("fsdp", None),
            P(None, "fsdp"),
            P("fsdp"),
            P("fsdp"),
            P("fsdp", None),
            P("fsdp"),
            P("fsdp", None),
            P("fsdp", None),
            P("fsdp", None),
        ),
        check_vma=False,
    )
```

profile of v0, /device:TPU:0, one launch (start us, length us, event | category | flops | bytes accessed | tf_op | source)
XLA Modules:
  0.0 1264.0 jit_solution(18037148518937544234)
XLA Ops:
  13.5 5.2 all-gather.2
  62.1 5.3 all-reduce.11
  80.3 11.5 all-gather.17.cloned.1.call-done
  101.3 67.4 %while.75 = (s32[]{:T(128)}, f32[4,128,256]{2,1,0:T(8,128)S(1)}, f32[]{:T(128)}, f32[8,64,4,256]{3,1,0,2:T(8,128)}, f32[8,4,128,256]{3,2,1,0:T(8,128)}, /*index=...) while((s32[]{:T(128)}, f32[4,128,256]{2,1,0:T(8,128)S(1)}, ...), condition=%wide.region_3.4_spmd.clone, body=%wide.region_1.3_spmd.clone.sunk | while | flops 279868032 | bytes 5856199 | solution.py:112
  172.5 14.9 %all-gather = bf16[8,128,256]{2,1,0:T(8,128)(2,1)S(1)} all-gather(bf16[4,128,256]{2,1,0:T(8,128)(2,1)S(1)} %convert_element_type.327), channel_id=2, replica_groups=mesh['replica'=16,'fsdp'=2] {'fsdp'}, dimensions={0}, use_global_device_ids=true | all-gather | bytes 786432 | tf_op jit(solution)/shard_map/all_gather | solution.py:21
  192.4 6.0 multiply_convert_fusion.3
  198.4 19.4 %all_gather.91 = bf16[2,4,128]{2,1,0:T(4,128)(2,1)S(1)} all-gather(bf16[1,4,128]{2,1,0:T(4,128)(2,1)S(1)} %fusion.124), channel_id=1, replica_groups=mesh['replica'=16,'fsdp'=2] {'fsdp'}, dimensions={0}, use_global_device_ids=true | all-gather | bytes 3072 | tf_op jit(solution)/shard_map/all_gather | solution.py:45
  223.9 18.6 %all-gather.25.cloned.1.call-done = bf16[1024,2816]{1,0:T(8,128)(2,1)} async-done(((bf16[512,2816]{1,0:T(8,128)(2,1)}), bf16[1024,2816]{1,0:T(8,128)(2,1)}) %all-gather.25.cloned.1.call-update) | async-done | bytes 5767184 | tf_op jit(solution)/shard_map/all_gather | solution.py:185
  242.4 8.9 fusion.143
  251.3 67.2 %all-gather.27.cloned.1.call-done = bf16[1024,2816]{1,0:T(8,128)(2,1)} async-done(((bf16[512,2816]{1,0:T(8,128)(2,1)}), bf16[1024,2816]{1,0:T(8,128)(2,1)}) %all-gather.27.cloned.1.call-update) | async-done | bytes 5767184 | tf_op jit(solution)/shard_map/all_gather | solution.py:186
  318.5 8.9 fusion.144
  327.3 67.2 %all-gather.29.cloned.1.call-done = bf16[2816,1024]{1,0:T(8,128)(2,1)} async-done(((bf16[1408,1024]{1,0:T(8,128)(2,1)}), bf16[2816,1024]{1,0:T(8,128)(2,1)}) %all-gather.29.cloned.1.call-update) | async-done | bytes 5767184 | tf_op jit(solution)/shard_map/all_gather | solution.py:187
  394.5 11.3 multiply_convert_fusion
  405.8 7.3 fusion.145
  431.9 8.7 all-gather.1
  445.1 142.2 %while.74 = (s32[]{:T(128)}, f32[4,128,256]{2,1,0:T(8,128)S(1)}, f32[8,64,4,128]{3,1,0,2:T(8,128)}, bf16[8,64,4,128]{3,2,1,0:T(4,128)(2,1)}, bf16[8,64,4,256]{3,...) while((s32[]{:T(128)}, f32[4,128,256]{2,1,0:T(8,128)S(1)}, ...), condition=%wide.region_20.21_spmd, body=%wide.region_15.20_spmd.sunk | while | flops 584790656 | bytes 14526128 | solution.py:112
  587.3 7.1 bitcast_multiply_fusion.10
  615.1 6.8 convolution_convert_fusion.2
  622.0 6.8 convolution_convert_fusion.1
  630.0 6.8 convolution_convert_fusion
  637.2 7.0 fusion.107
  650.7 23.0 %reduce-scatter.23.cloned.1.call-done = bf16[512,1024]{1,0:T(8,128)(2,1)} async-done(((bf16[1024,1024]{1,0:T(8,128)(2,1)}), bf16[512,1024]{1,0:T(8,128)(2,1)}) %reduce-scatter.23.cloned.1.call-update) | async-done | bytes 1048592 | tf_op jit(solution)/shard_map/reduce_scatter | solution.py:323
  673.7 34.7 %reduce-scatter.15.cloned.1.call-done = bf16[512,1024]{1,0:T(8,128)(2,1)} async-done(((bf16[1024,1024]{1,0:T(8,128)(2,1)}), bf16[512,1024]{1,0:T(8,128)(2,1)}) %reduce-scatter.15.cloned.1.call-update) | async-done | bytes 1048592 | tf_op jit(solution)/shard_map/reduce_scatter | solution.py:305
  708.4 34.1 %reduce-scatter.17.cloned.1.call-done = bf16[512,1024]{1,0:T(8,128)(2,1)} async-done(((bf16[1024,1024]{1,0:T(8,128)(2,1)}), bf16[512,1024]{1,0:T(8,128)(2,1)}) %reduce-scatter.17.cloned.1.call-update) | async-done | bytes 1048592 | tf_op jit(solution)/shard_map/reduce_scatter | solution.py:308
  742.5 74.2 %reduce-scatter.25.cloned.1.call-done = bf16[512,2816]{1,0:T(8,128)(2,1)} async-done(((bf16[1024,2816]{1,0:T(8,128)(2,1)}), bf16[512,2816]{1,0:T(8,128)(2,1)}) %reduce-scatter.25.cloned.1.call-update) | async-done | bytes 2883600 | tf_op jit(solution)/shard_map/reduce_scatter | solution.py:329
  816.7 74.1 %reduce-scatter.27.cloned.1.call-done = bf16[512,2816]{1,0:T(8,128)(2,1)} async-done(((bf16[1024,2816]{1,0:T(8,128)(2,1)}), bf16[512,2816]{1,0:T(8,128)(2,1)}) %reduce-scatter.27.cloned.1.call-update) | async-done | bytes 2883600 | tf_op jit(solution)/shard_map/reduce_scatter | solution.py:332
  890.8 74.2 %reduce-scatter.29.cloned.1.call-done = bf16[1408,1024]{1,0:T(8,128)(2,1)} async-done(((bf16[2816,1024]{1,0:T(8,128)(2,1)}), bf16[1408,1024]{1,0:T(8,128)(2,1)}) %reduce-scatter.29.cloned.1.call-update) | async-done | bytes 2883600 | tf_op jit(solution)/shard_map/reduce_scatter | solution.py:335
  976.1 5.0 all-reduce.10
  985.3 6.8 add_convert_fusion
  992.1 63.0 %all-reduce.8 = (bf16[512]{0:T(512)(128)(2,1)S(1)}, bf16[512,16]{0,1:T(8,128)(2,1)S(1)}, bf16[16,256]{1,0:T(8,128)(2,1)S(1)}, bf16[256]{0:T(256)(128)(2,1)S(1)},...) all-reduce(bf16[512]{0:T(512)(128)(2,1)S(1)} %dynamic-slice.3, ...), channel_id=1, replica_groups=mesh['replica'=16,'fsdp'=2] {'replica'}, use_global_device_ids=true, to_apply=%region_27.28 | all-reduce | flops 13696 | bytes 54784 | tf_op jit(solution)/shard_map/psum | solution.py:340
  1058.5 180.7 %all-reduce.14.cloned.1.call-done = (bf16[512,512]{1,0:T(8,128)(2,1)}, bf16[512,512]{1,0:T(8,128)(2,1)}, bf16[512,1024]{1,0:T(8,128)(2,1)}, bf16[512,1024]{1,0:T...) async-done(((bf16[512,512]{1,0:T(8,128)(2,1)}, bf16[512,512]{1,0:T(8,128)(2,1)}, ...) | async-done | bytes 12845072 | tf_op jit(solution)/shard_map/psum | solution.py:341
  1239.2 4.9 convert_element_type.377
  (631 shorter events, 350.5 us)
Async XLA Ops:
  7.2 60.3 %all-gather.19.cloned.1.call-start = ((), (), s32[]{:S(2)}) async-start(), calls=%async_computation.12 | async-start | bytes 1572864 | tf_op jit(solution)/shard_map/all_gather | solution.py:175
  7.9 65.6 %all-gather.15.cloned.1.call-start = ((), (), s32[]{:S(2)}) async-start(), calls=%async_computation.10 | async-start | bytes 1572864 | tf_op jit(solution)/shard_map/all_gather | solution.py:176
  8.7 83.1 %all-gather.17.cloned.1.call-start = ((), (), s32[]{:S(2)}) async-start(), calls=%async_computation.11 | async-start | bytes 3145728 | tf_op jit(solution)/shard_map/all_gather | solution.py:177
  9.4 183.0 %all-gather.21.cloned.1.call-start = ((), (), s32[]{:S(2)}) async-start(), calls=%async_computation.13 | async-start | bytes 3145728 | tf_op jit(solution)/shard_map/all_gather | solution.py:178
  10.0 207.8 %all-gather.23.cloned.1.call-start = ((), (), s32[]{:S(2)}) async-start(), calls=%async_computation.14 | async-start | bytes 3145728 | tf_op jit(solution)/shard_map/all_gather | solution.py:183
  10.6 231.9 %all-gather.25.cloned.1.call-start = ((), (), s32[]{:S(2)}) async-start(), calls=%async_computation.15 | async-start | bytes 8650752 | tf_op jit(solution)/shard_map/all_gather | solution.py:185
  11.1 307.3 %all-gather.27.cloned.1.call-start = ((), (), s32[]{:S(2)}) async-start(), calls=%async_computation.16 | async-start | bytes 8650752 | tf_op jit(solution)/shard_map/all_gather | solution.py:186
  11.9 6.8 copy-start.46
  11.9 11.2 copy-start.47
  11.9 16.0 %copy-start.53 = (bf16[256]{0:T(256)(128)(2,1)S(1)}, bf16[256]{0:T(256)(128)(2,1)}, u32[]{:S(2)}) copy-start(bf16[256]{0:T(256)(128)(2,1)} %param.35) | copy-start | bytes 1540
  12.0 382.6 %all-gather.29.cloned.1.call-start = ((), (), s32[]{:S(2)}) async-start(), calls=%async_computation.17 | async-start | bytes 8650752 | tf_op jit(solution)/shard_map/all_gather | solution.py:187
  12.7 638.0 %reduce-scatter.11.cloned.1.call-start = ((), (), s32[]{:S(2)}) async-start(), calls=%async_computation.18 | async-start | bytes 1572864 | tf_op jit(solution)/shard_map/reduce_scatter | solution.py:299
  13.4 19.3 %copy-start.41 = (f32[512]{0:T(512)}, f32[512]{0:T(512)S(1)}, u32[]{:S(2)}) copy-start(f32[512]{0:T(512)S(1)} %fusion.80) | copy-start | bytes 6148
  23.1 11.4 copy-start.37
  49.9 10.1 copy-start.48
  192.3 227.3 %copy-start.1 = (f32[512,4,256]{0,2,1:T(8,128)}, f32[512,4,256]{0,2,1:T(8,128)S(1)}, u32[]{:S(2)}) copy-start(f32[512,4,256]{0,2,1:T(8,128)S(1)} %get-tuple-element.928) | copy-start | bytes 6291460
  405.8 7.4 copy-start.57
  405.8 7.4 copy-start.55
  405.8 7.4 copy-start.6
  405.8 7.4 copy-start.51
  587.3 7.4 copy-start.4
  596.6 54.1 %reduce-scatter.13.cloned.1.call-start = ((), (), s32[]{:S(2)}) async-start(), calls=%async_computation.19 | async-start | bytes 1572864 | tf_op jit(solution)/shard_map/reduce_scatter | solution.py:302
  599.6 74.1 %reduce-scatter.23.cloned.1.call-start = ((), (), s32[]{:S(2)}) async-start(), calls=%async_computation.24 | async-start | bytes 3145728 | tf_op jit(solution)/shard_map/reduce_scatter | solution.py:323
  603.9 104.5 %reduce-scatter.15.cloned.1.call-start = ((), (), s32[]{:S(2)}) async-start(), calls=%async_computation.20 | async-start | bytes 3145728 | tf_op jit(solution)/shard_map/reduce_scatter | solution.py:305
  609.8 132.6 %reduce-scatter.17.cloned.1.call-start = ((), (), s32[]{:S(2)}) async-start(), calls=%async_computation.21 | async-start | bytes 3145728 | tf_op jit(solution)/shard_map/reduce_scatter | solution.py:308
  613.9 202.8 %reduce-scatter.25.cloned.1.call-start = ((), (), s32[]{:S(2)}) async-start(), calls=%async_computation.25 | async-start | bytes 8650752 | tf_op jit(solution)/shard_map/reduce_scatter | solution.py:329
  621.9 268.9 %reduce-scatter.27.cloned.1.call-start = ((), (), s32[]{:S(2)}) async-start(), calls=%async_computation.26 | async-start | bytes 8650752 | tf_op jit(solution)/shard_map/reduce_scatter | solution.py:332
  628.8 336.2 %reduce-scatter.29.cloned.1.call-start = ((), (), s32[]{:S(2)}) async-start(), calls=%async_computation.27 | async-start | bytes 8650752 | tf_op jit(solution)/shard_map/reduce_scatter | solution.py:335
  636.9 355.2 %reduce-scatter.21.cloned.1.call-start = ((), (), s32[]{:S(2)}) async-start(), calls=%async_computation.23 | async-start | bytes 24576 | tf_op jit(solution)/shard_map/reduce_scatter | solution.py:314
  649.3 342.8 %reduce-scatter.19.cloned.1.call-start = ((), (), s32[]{:S(2)}) async-start(), calls=%async_computation.22 | async-start | bytes 49152 | tf_op jit(solution)/shard_map/reduce_scatter | solution.py:311
  650.4 588.8 %all-reduce.14.cloned.1.call-start = ((), (), s32[]{:S(2)}) async-start(), calls=%async_computation.28 | async-start | bytes 25690112 | tf_op jit(solution)/shard_map/psum | solution.py:341
  973.6 7.7 copy-start.42
  (45 other events, 101.7 us)
Sparse Core Ops, SparseCore 0:
  9.6 24.3 all-gather.18
  35.5 21.4 all-gather.14
  58.6 33.1 all-gather.16
  93.2 33.1 all-gather.20
  127.7 33.1 all-gather.22
  162.3 80.1 all-gather.24
  244.0 74.4 all-gather.26
  320.0 74.4 all-gather.28
  596.7 20.3 reduce-scatter.10
  619.3 20.3 reduce-scatter.12
  641.9 31.8 reduce-scatter.22
  676.5 31.8 reduce-scatter.14
  710.6 31.8 reduce-scatter.16
  745.3 71.3 reduce-scatter.24
  819.4 71.3 reduce-scatter.26
  893.7 71.3 reduce-scatter.28
  967.7 9.7 reduce-scatter.20
  980.1 9.8 reduce-scatter.18
  995.5 243.6 all-reduce.13
where the time goes:
time: 1270 us; the launch traced here: 1260 us
  waiting for transfers between devices  665 us (52%)
  matrix products  186 us (15%)
  blocking collectives  148 us (12%)
  local copies, waits for them, and re-layouts  115 us (9%)
  other arithmetic  106 us (8%)
  loops' own time  22.9 us (2%)
  between operations  21.3 us (2%)
    psum x1, waiting for transfers between devices, on_device(): lax.psum(parts[1].astype(jnp.bfloat16), 'replica').astype(jnp.float32)  181 us
    dot_general x30, matrix products, product(): return jnp.einsum(form, left, right, preferred_element_type=jnp.float32)  113 us
    reduce_scatter x1, waiting for transfers between devices, on_device(): lax.psum_scatter(grad_gate.astype(jnp.bfloat16), 'fsdp', scatter_dimensio...  74.2 us
    reduce_scatter x1, waiting for transfers between devices, on_device(): lax.psum_scatter(grad_down.astype(jnp.bfloat16), 'fsdp', scatter_dimensio...  74.2 us
    reduce_scatter x1, waiting for transfers between devices, on_device(): lax.psum_scatter(grad_up.astype(jnp.bfloat16), 'fsdp', scatter_dimension=...  74.1 us
    all_gather x1, waiting for transfers between devices, on_device(): lax.all_gather(down_map, 'fsdp', axis=0, tiled=True)  67.2 us
    all_gather x1, waiting for transfers between devices, on_device(): lax.all_gather(up_map, 'fsdp', axis=0, tiled=True)  67.2 us
    psum x1, blocking collectives, on_device(): lax.psum(parts[0].astype(jnp.bfloat16), 'replica').astype(jnp.float32)  63 us
  transfers between devices with their start and end apart: 19, of which 11 were waited for; matrix products, arithmetic and copies ran while one was open for 16% of the time, Pallas kernels for 0%

commit v1 on v0

v1 whole, which is shorter than its diff:
```python
import functools

import jax
import jax.numpy as jnp
from jax import lax
from jax.experimental import pallas as pl
from jax.experimental.pallas import tpu as pltpu
from jax.sharding import PartitionSpec as P

HEADS = 4
DK = 128
DV = 256
SPAN = 64
WIDE = 2 * SPAN

EPSILON = 1e-06
HEAD_FLOOR = 16.0
GATE_NORM = 16.0

F32 = jnp.float32
BF16 = jnp.bfloat16
VMEM_BYTES = 56 * 1024 * 1024

ROW_EXPAND = 16
ROW_MIXER = 32
ROW_FEED = 33
ROW_MIXED = 34
SMALL_ROWS = 48
LANE_EXPAND = 16
LANE_MIXER = 32
LANE_FEED = 33
LANE_BIAS = 34
LANE_HEADS = 35


def nn(a, b):
    return lax.dot_general(a, b, (((1,), (0,)), ((), ())), preferred_element_type=F32)


def nt(a, b):
    return lax.dot_general(a, b, (((1,), (1,)), ((), ())), preferred_element_type=F32)


def tn(a, b):
    return lax.dot_general(a, b, (((0,), (0,)), ((), ())), preferred_element_type=F32)


def sigmoid(v):
    return 1.0 / (1.0 + jnp.exp(-v))


def call(kernel, out_shape, **kw):
    return pl.pallas_call(
        kernel,
        out_shape=out_shape,
        compiler_params=pltpu.CompilerParams(vmem_limit_bytes=VMEM_BYTES),
        **kw,
    )


def sds(shape, dtype):
    return jax.ShapeDtypeStruct(shape, dtype)


SMEM = pl.BlockSpec(memory_space=pltpu.SMEM)
VMEM = pl.BlockSpec(memory_space=pltpu.VMEM)


def split_sum(ones, values):
    high = values.astype(BF16)
    rest = values - high.astype(F32)
    middle = rest.astype(BF16)
    low = (rest - middle.astype(F32)).astype(BF16)
    return nn(ones, high) + nn(ones, middle) + nn(ones, low)


def lower_ones(size):
    rows = lax.broadcasted_iota(jnp.int32, (size, size), 0)
    cols = lax.broadcasted_iota(jnp.int32, (size, size), 1)
    return (rows >= cols).astype(F32).astype(BF16)


def upper_ones(size):
    rows = lax.broadcasted_iota(jnp.int32, (size, size), 0)
    cols = lax.broadcasted_iota(jnp.int32, (size, size), 1)
    return (rows <= cols).astype(F32).astype(BF16)


def log_decay(pre):
    return (jnp.minimum(pre, 0.0) - jnp.log1p(jnp.exp(-jnp.abs(pre)))) / GATE_NORM


def row_of(small_ref, row):
    return small_ref[ROW_MIXER:SMALL_ROWS, :].astype(F32)[row - ROW_MIXER : row - ROW_MIXER + 1, :]


def expand_of(small_ref):
    half = small_ref.shape[1] // 2
    quarter = half // 2
    part = small_ref[ROW_EXPAND:ROW_MIXER, :]
    return jnp.concatenate([part[:, :quarter], part[:, half : half + quarter]], axis=1)


def bias_of(small_ref):
    half = small_ref.shape[1] // 2
    quarter = half // 2
    row = row_of(small_ref, ROW_MIXED)
    return jnp.concatenate([row[:, :quarter], row[:, half : half + quarter]], axis=1)


def head_gain_of(small_ref):
    half = small_ref.shape[1] // 2
    at = half // 2
    count = DV // 2
    row = row_of(small_ref, ROW_MIXED)
    return jnp.concatenate([row[:, at : at + count], row[:, half + at : half + at + count]], axis=1)


def place_rows(who_ref, full_ref, own, pieces):
    x = who_ref[0]
    q = who_ref[1]
    half = own.shape[0]
    rows = pieces[0].shape[0]
    full_ref[pl.ds(pl.multiple_of(x * half, half), half), :] = own
    for k in range(4):
        at = (1 - x) * half + (q ^ k) * rows
        full_ref[pl.ds(pl.multiple_of(at, rows), rows), :] = pieces[k]


def place_grads(who_ref, keep_ref, send_ref, scratch_ref, row, cols, rows=32):
    x = who_ref[0]
    me = who_ref[2]
    half = scratch_ref.shape[0] // 2
    for core, out_ref in ((0, keep_ref), (1, send_ref)):
        for xx in range(2):
            for yy in range(2):
                for zz in range(4):
                    block = me ^ (core * 8 + yy * 4 + zz)
                    at = pl.multiple_of((x ^ xx) * half + block * rows, rows)
                    out_ref[xx, yy, zz, row : row + rows, cols] = scratch_ref[pl.ds(at, rows), :]


def project_kernel(
    who, x, small, q_own, k_own, v_own, r0, r1, r2, r3, normed, qkv, pre, narrow_out, full
):
    j = pl.program_id(0)

    @pl.when(j == 0)
    def _():
        tokens = x[...].astype(F32)
        mean_sq = jnp.mean(tokens * tokens, axis=-1, keepdims=True)
        normed[...] = (
            tokens * lax.rsqrt(mean_sq + EPSILON) * row_of(small, ROW_MIXER)
        ).astype(BF16)
        narrow = nt(normed[...], small[0:ROW_EXPAND, :]).astype(BF16)
        narrow_out[...] = narrow
        pre[...] = nn(narrow, expand_of(small)) + bias_of(small)

    pieces = [r[...] for r in (r0, r1, r2, r3)]

    @pl.when(j < 2)
    def _():
        place_rows(who, full, q_own[...], pieces)

    @pl.when((j >= 2) & (j < 4))
    def _():
        place_rows(who, full, k_own[...], pieces)

    @pl.when(j >= 4)
    def _():
        place_rows(who, full, v_own[...], pieces)

    qkv[...] = nn(normed[...], full[...]).astype(BF16)


def project(who, x, small, q_own, k_own, v_own, pieces):
    t, d = x.shape
    half = d // 2
    kd = HEADS * DK
    vd = HEADS * DV
    width = 2 * kd + vd
    const = lambda j: (0, 0)
    qn = kd // 256
    vn = vd // 256
    return call(
        project_kernel,
        (sds((t, d), BF16), sds((t, width), BF16), sds((t, kd), F32), sds((t, 16), BF16)),
        grid=(width // 256,),
        in_specs=[
            SMEM,
            pl.BlockSpec((t, d), const),
            pl.BlockSpec(small.shape, const),
            pl.BlockSpec((half, 256), lambda j: (0, jnp.minimum(j, qn - 1))),
            pl.BlockSpec((half, 256), lambda j: (0, jnp.clip(j - qn, 0, qn - 1))),
            pl.BlockSpec((half, 256), lambda j: (0, jnp.clip(j - 2 * qn, 0, vn - 1))),
        ]
        + [pl.BlockSpec((half // 4, 256), lambda j: (0, j))] * 4,
        out_specs=(
            pl.BlockSpec((t, d), const),
            pl.BlockSpec((t, 256), lambda j: (0, j)),
            pl.BlockSpec((t, kd), const),
            pl.BlockSpec((t, 16), const),
        ),
        scratch_shapes=[pltpu.VMEM((d, 256), BF16)],
    )(who, x, small, q_own, k_own, v_own, *pieces)


def swish_kernel(who, normed, own, r0, r1, r2, r3, out, full):
    place_rows(who, full, own[...], [r[...] for r in (r0, r1, r2, r3)])
    out[...] = nn(normed[...], full[...])


def swish_project(who, normed, own, pieces):
    t, d = normed.shape
    half = d // 2
    vd = HEADS * DV
    return call(
        swish_kernel,
        sds((t, vd), F32),
        grid=(vd // 256,),
        in_specs=[
            SMEM,
            pl.BlockSpec((t, d), lambda j: (0, 0)),
            pl.BlockSpec((half, 256), lambda j: (0, j)),
        ]
        + [pl.BlockSpec((half // 4, 256), lambda j: (0, j))] * 4,
        out_specs=pl.BlockSpec((t, 256), lambda j: (0, j)),
        scratch_shapes=[pltpu.VMEM((d, 256), BF16)],
    )(who, normed, own, *pieces)


def mark_at(mrow, place):
    return mrow[0:1, place : place + 1]


def state_kernel(qkv, pre, mcol, mrow, payload, passing):
    t = pre.shape[0]
    kd = HEADS * DK
    ones = lower_ones(WIDE)
    states = [jnp.zeros((DV, DK), F32) for _ in range(HEADS)]
    total = jnp.zeros((1, kd), F32)
    for i in range(t // WIDE):
        rows = slice(i * WIDE, (i + 1) * WIDE)
        cumul = split_sum(ones, log_decay(pre[rows, :]))
        end = cumul[WIDE - 1 : WIDE, :]
        total = total + end
        last = mark_at(mrow, (i + 1) * WIDE - 1)
        keys = qkv[rows, kd : 2 * kd].astype(F32)
        tail = jnp.where(mcol[rows, :] == last, keys * jnp.exp(end - cumul), 0.0).astype(BF16)
        if i:
            keep = jnp.where(mark_at(mrow, i * WIDE - 1) == last, jnp.exp(end), 0.0)
        for h in range(HEADS):
            c = slice(h * DK, (h + 1) * DK)
            values = qkv[rows, 2 * kd + h * DV : 2 * kd + (h + 1) * DV]
            update = tn(values, tail[:, c])
            states[h] = states[h] * keep[:, c] + update if i else update
    for h in range(HEADS):
        payload[h * DV : (h + 1) * DV, :] = states[h].astype(BF16)
    last = mark_at(mrow, t - 1)
    payload[HEADS * DV :, :] = jnp.broadcast_to(last, (16, DK)).astype(BF16)
    passes = jnp.where(mark_at(mrow, 0) == last, jnp.exp(total), 0.0)
    passing[...] = jnp.broadcast_to(passes, passing.shape)


def local_state(qkv, pre, mcol, mrow):
    return call(
        state_kernel,
        (sds((HEADS * DV + 16, DK), BF16), sds((8, HEADS * DK), F32)),
    )(qkv, pre, mcol, mrow)


def mixer_kernel(
    who, x, small, qkv, pre, swish, mcol, mrow, payload, own, r0, r1, r2, r3,
    mixed_out, states_out, gated_out, hidden_out, second_out, full,
):
    t, d = x.shape
    kd = HEADS * DK
    ones = lower_ones(WIDE)
    causal_rows = lax.broadcasted_iota(jnp.int32, (WIDE, WIDE), 0)
    causal_cols = lax.broadcasted_iota(jnp.int32, (WIDE, WIDE), 1)
    states = [payload[h * DV : (h + 1) * DV, :].astype(F32) for h in range(HEADS)]
    before = payload[HEADS * DV :, :].astype(F32)[0:1, 0:1]
    place_rows(who, full, own[...], [r[...] for r in (r0, r1, r2, r3)])
    for i in range(t // WIDE):
        rows = slice(i * WIDE, (i + 1) * WIDE)
        marks = mcol[rows, :]
        last = mark_at(mrow, (i + 1) * WIDE - 1)
        cumul = split_sum(ones, log_decay(pre[rows, :]))
        middle = cumul[SPAN - 1 : SPAN, :]
        end = cumul[WIDE - 1 : WIDE, :]
        queries = qkv[rows, 0:kd].astype(F32)
        keys = qkv[rows, kd : 2 * kd].astype(F32)
        lifted = (queries * jnp.exp(cumul - middle)).astype(BF16)
        lowered = (keys * jnp.exp(middle - cumul)).astype(BF16)
        carried = jnp.where(marks == before, queries * jnp.exp(cumul), 0.0).astype(BF16)
        tail = jnp.where(marks == last, keys * jnp.exp(end - cumul), 0.0).astype(BF16)
        keep = jnp.where(before == last, jnp.exp(end), 0.0)
        causal = (causal_rows >= causal_cols) & (marks == mrow[0:1, rows])
        for h in range(HEADS):
            c = slice(h * DK, (h + 1) * DK)
            values = qkv[rows, 2 * kd + h * DV : 2 * kd + (h + 1) * DV]
            low_state = states[h].astype(BF16)
            states_out[i, h] = low_state
            scores = jnp.where(causal, nt(lifted[:, c], lowered[:, c]), 0.0).astype(BF16)
            mixed_out[rows, h * DV : (h + 1) * DV] = nn(scores, values) + nt(
                carried[:, c], low_state
            )
            states[h] = states[h] * keep[:, c] + tn(values, tail[:, c])
        before = last
    gain = head_gain_of(small)
    for h in range(HEADS):
        c = slice(h * DV, (h + 1) * DV)
        mixed = mixed_out[:, c]
        scale = lax.rsqrt(jnp.mean(mixed * mixed, axis=-1, keepdims=True) + HEAD_FLOOR)
        pre_gate = swish[:, c]
        gated_out[:, c] = (mixed * scale * gain * (pre_gate * sigmoid(pre_gate))).astype(BF16)
    hidden = x[...].astype(F32) + nn(gated_out[...], full[...])
    hidden_out[...] = hidden
    mean_sq = jnp.mean(hidden * hidden, axis=-1, keepdims=True)
    second_out[...] = (
        hidden * lax.rsqrt(mean_sq + EPSILON) * row_of(small, ROW_FEED)
    ).astype(BF16)


def mixer(who, x, small, qkv, pre, swish, mcol, mrow, payload, own, pieces):
    t, d = x.shape
    vd = HEADS * DV
    quarter = own.shape[0] // 4
    right = pl.BlockSpec((quarter, d), lambda i: (0, 1))
    whole = lambda a: pl.BlockSpec(a.shape, lambda i: (0,) * a.ndim)
    outs = (
        sds((t, vd), F32),
        sds((t // WIDE, HEADS, DV, DK), BF16),
        sds((t, vd), BF16),
        sds((t, d), F32),
        sds((t, d), BF16),
    )
    ins = (x, small, qkv, pre, swish, mcol, mrow, payload, own)
    return call(
        mixer_kernel,
        outs,
        grid=(1,),
        in_specs=[SMEM] + [whole(a) for a in ins] + [right] * 4,
        out_specs=tuple(whole(a) for a in outs),
        scratch_shapes=[pltpu.VMEM((vd, d), BF16)],
    )(who, *ins, *pieces)


def feed_kernel(
    who, second, cot, g0, g1, u0, u1, down, r0, r1, r2, r3, *rest, first, blocks
):
    if first:
        total_out, total_ds, keep, send, wg, wu, wd, sec_t, cot_t, sg_, su_, sd_ = rest
    else:
        in_out, in_ds, total_out, total_ds, keep, send, wg, wu, wd, sec_t, cot_t, sg_, su_, sd_ = rest
    j = pl.program_id(0)

    @pl.when(j == 0)
    def _():
        if first:
            total_out[...] = jnp.zeros_like(total_out)
            total_ds[...] = jnp.zeros_like(total_ds)
        else:
            total_out[...] = in_out[...]
            total_ds[...] = in_ds[...]
        sec_t[...] = second[...].T
        cot_t[...] = cot[...].T

    x = who[0]
    q = who[1]
    half = g0.shape[0]
    rows = pl.ds(pl.multiple_of(x * half, half), half)
    wg[rows, 0:128] = g0[...]
    wg[rows, 128:256] = g1[...]
    wu[rows, 0:128] = u0[...]
    wu[rows, 128:256] = u1[...]
    wd[pl.ds(pl.multiple_of(x * 128, 128), 128), :] = down[...]
    for k, r in enumerate((r0, r1, r2, r3)):
        at = q ^ k
        rows = pl.ds(pl.multiple_of((1 - x) * half + at * 128, 128), 128)
        wg[rows, :] = r[:, 0:256]
        wu[rows, :] = r[:, 256:512]
        wd[pl.ds(pl.multiple_of((1 - x) * 128, 128), 128), pl.ds(pl.multiple_of(at * 256, 256), 256)] = r[:, 512:768]
    gate = nn(second[...], wg[...])
    upward = nn(second[...], wu[...])
    d_inner = nt(cot[...], wd[...])
    sig = sigmoid(gate)
    silu = gate * sig
    inner = (silu * upward).astype(BF16)
    d_gate = (d_inner * upward * sig * (1.0 + gate * (1.0 - sig))).astype(BF16)
    d_up = (d_inner * silu).astype(BF16)
    total_out[...] += nn(inner, wd[...])
    total_ds[...] += nt(d_gate, wg[...]) + nt(d_up, wu[...])
    sg_[...] = nn(sec_t[...], d_gate).astype(BF16)
    su_[...] = nn(sec_t[...], d_up).astype(BF16)
    grad_down = tn(inner, cot[...]).astype(BF16)
    for part in range(2):
        for cb in range(4):
            at = part * half + cb * 128
            sd_[at : at + 128, :] = grad_down[part * 128 : (part + 1) * 128, cb * 256 : (cb + 1) * 256]
    cols = slice(0, 256)
    place_grads(who, keep, send, sg_, 0, cols)
    place_grads(who, keep, send, su_, 32, cols)
    place_grads(who, keep, send, sd_, 64, cols)


def feed(who, second, cot, gate_own, up_own, down_own, pieces, totals, start, blocks):
    t, d = second.shape
    half = d // 2
    ff = gate_own.shape[1]
    halves = ff // 256
    const = lambda j: (0, 0)
    first = totals is None
    left = pl.BlockSpec((half, 128), lambda j: (0, start + j))
    right = pl.BlockSpec((half, 128), lambda j: (0, halves + start + j))
    full = pl.BlockSpec((t, d), const)
    grads = pl.BlockSpec((2, 2, 4, 96, 256), lambda j: (0, 0, 0, 0, j))
    grads_shape = sds((2, 2, 4, 96, blocks * 256), BF16)
    return call(
        functools.partial(feed_kernel, first=first, blocks=blocks),
        (sds((t, d), F32), sds((t, d), F32), grads_shape, grads_shape),
        grid=(blocks,),
        in_specs=[
            SMEM, full, full, left, right, left, right,
            pl.BlockSpec((128, d), lambda j: (start + j, 0)),
        ]
        + [pl.BlockSpec((half // 4, 768), lambda j: (0, j))] * 4
        + ([] if first else [full, full]),
        out_specs=(full, full, grads, grads),
        scratch_shapes=[
            pltpu.VMEM((d, 256), BF16),
            pltpu.VMEM((d, 256), BF16),
            pltpu.VMEM((256, d), BF16),
            pltpu.VMEM((d, t), BF16),
            pltpu.VMEM((d, t), BF16),
            pltpu.VMEM((d, 256), BF16),
            pltpu.VMEM((d, 256), BF16),
            pltpu.VMEM((d, 256), BF16),
        ],
    )(
        who, second, cot, gate_own, gate_own, up_own, up_own, down_own, *pieces,
        *(() if first else totals),
    )


def pack_kernel(who, g0, g1, u0, u1, down, out):
    out[:, 0:128] = g0[...]
    out[:, 128:256] = g1[...]
    out[:, 256:384] = u0[...]
    out[:, 384:512] = u1[...]
    out[:, 512:768] = down[...]


def pack_feed(who, gate_own, up_own, down_own, start, blocks):
    half, ff = gate_own.shape
    halves = ff // 256
    quarter = half // 4
    left = pl.BlockSpec((quarter, 128), lambda j, w: (w[1], start + j))
    right = pl.BlockSpec((quarter, 128), lambda j, w: (w[1], halves + start + j))
    return pl.pallas_call(
        pack_kernel,
        out_shape=sds((quarter, blocks * 768), BF16),
        grid_spec=pltpu.PrefetchScalarGridSpec(
            num_scalar_prefetch=1,
            grid=(blocks,),
            in_specs=[
                left, right, left, right,
                pl.BlockSpec((128, down_own.shape[1] // 4), lambda j, w: (start + j, w[1])),
            ],
            out_specs=pl.BlockSpec((quarter, 768), lambda j, w: (0, j)),
        ),
    )(who, gate_own, gate_own, up_own, up_own, down_own)


def mixer_back_kernel(
    who, small, d_second, hidden, cot, swish, mixed, qkv, pre, mcol, payload,
    own, r0, r1, r2, r3,
    d_hidden_out, low_out, d_swish_out, d_mixed_out, rows_out, back_out, full, d_gated,
):
    t, d = hidden.shape
    kd = HEADS * DK
    place_rows(who, full, own[...], [r[...] for r in (r0, r1, r2, r3)])
    values = hidden[...]
    upstream = d_second[...]
    scale = lax.rsqrt(jnp.mean(values * values, axis=-1, keepdims=True) + EPSILON)
    rows_out[...] = jnp.zeros_like(rows_out)
    rows_out[0:1, :] = jnp.sum(upstream * values * scale, axis=0, keepdims=True)
    scaled = upstream * row_of(small, ROW_FEED)
    mean = jnp.mean(scaled * values, axis=-1, keepdims=True)
    d_hidden = cot[...].astype(F32) + scale * scaled - values * (scale * scale * scale * mean)
    d_hidden_out[...] = d_hidden
    low_out[...] = d_hidden.astype(BF16)
    d_gated[...] = nt(low_out[...], full[...])
    gain = head_gain_of(small)
    grad_heads = jnp.zeros((1, DV), F32)
    for h in range(HEADS):
        c = slice(h * DV, (h + 1) * DV)
        values = mixed[:, c]
        scale = lax.rsqrt(jnp.mean(values * values, axis=-1, keepdims=True) + HEAD_FLOOR)
        pre_gate = swish[:, c]
        sig = sigmoid(pre_gate)
        up = d_gated[:, c]
        unit = values * scale
        d_swish_out[:, c] = (up * unit * gain * sig * (1.0 + pre_gate * (1.0 - sig))).astype(BF16)
        err = up * pre_gate * sig
        grad_heads = grad_heads + jnp.sum(err * unit, axis=0, keepdims=True)
        scaled = err * gain
        mean = jnp.mean(scaled * unit, axis=-1, keepdims=True)
        d_mixed_out[:, c] = (scale * (scaled - unit * mean)).astype(BF16)
    rows_out[1:2, 0:DV] = grad_heads
    ones = lower_ones(WIDE)
    before = payload[HEADS * DV :, :].astype(F32)[0:1, 0:1]
    base = jnp.zeros((1, kd), F32)
    sums = [jnp.zeros((DV, DK), F32) for _ in range(HEADS)]
    for i in range(t // WIDE):
        rows = slice(i * WIDE, (i + 1) * WIDE)
        cumul = split_sum(ones, log_decay(pre[rows, :])) + base
        base = cumul[WIDE - 1 : WIDE, :]
        queries = qkv[rows, 0:kd].astype(F32)
        carried = jnp.where(mcol[rows, :] == before, queries * jnp.exp(cumul), 0.0).astype(BF16)
        for h in range(HEADS):
            sums[h] = sums[h] + tn(
                d_mixed_out[rows, h * DV : (h + 1) * DV], carried[:, h * DK : (h + 1) * DK]
            )
    for h in range(HEADS):
        back_out[h * DV : (h + 1) * DV, :] = sums[h].astype(BF16)


def mixer_back(who, small, d_second, hidden, cot, swish, mixed, qkv, pre, mcol, payload, own, pieces):
    t, d = hidden.shape
    vd = HEADS * DV
    quarter = own.shape[0] // 4
    right = pl.BlockSpec((quarter, d), lambda i: (0, 1))
    whole = lambda a: pl.BlockSpec(a.shape, lambda i: (0,) * len(a.shape))
    outs = (
        sds((t, d), F32),
        sds((t, d), BF16),
        sds((t, vd), BF16),
        sds((t, vd), BF16),
        sds((8, d), F32),
        sds((HEADS * DV, DK), BF16),
    )
    ins = (small, d_second, hidden, cot, swish, mixed, qkv, pre, mcol, payload, own)
    return call(
        mixer_back_kernel,
        outs,
        grid=(1,),
        in_specs=[SMEM] + [whole(a) for a in ins] + [right] * 4,
        out_specs=tuple(whole(a) for a in outs),
        scratch_shapes=[pltpu.VMEM((vd, d), BF16), pltpu.VMEM((t, vd), F32)],
    )(who, *ins, *pieces)


def gate_grads_kernel(who, normed, d_swish, gated, low, keep, send, scratch, left_t):
    j = pl.program_id(0)
    count = d_swish.shape[1]
    half = pl.num_programs(0) // 2

    @pl.when(j == 0)
    def _():
        left_t[...] = normed[...].T

    @pl.when(j == half)
    def _():
        left_t[...] = gated[...].T

    @pl.when(j < half)
    def _():
        scratch[...] = nn(left_t[...], d_swish[...]).astype(BF16)

    @pl.when(j >= half)
    def _():
        scratch[...] = nn(left_t[...], low[...]).astype(BF16)

    place_grads(who, keep, send, scratch, 0, slice(0, 256))


def gate_grads(who, normed, d_swish, gated, low):
    t, d = normed.shape
    n = d_swish.shape[1] // 256
    const = lambda j: (0, 0)
    shape = sds((2, 2, 4, 32, 2 * n * 256), BF16)
    spec = pl.BlockSpec((2, 2, 4, 32, 256), lambda j: (0, 0, 0, 0, j))
    return call(
        gate_grads_kernel,
        (shape, shape),
        grid=(2 * n,),
        in_specs=[
            SMEM,
            pl.BlockSpec((t, d), const),
            pl.BlockSpec((t, 256), lambda j: (0, jnp.minimum(j, n - 1))),
            pl.BlockSpec((t, d), const),
            pl.BlockSpec((t, 256), lambda j: (0, jnp.maximum(j - n, 0))),
        ],
        out_specs=(spec, spec),
        scratch_shapes=[pltpu.VMEM((d, 256), BF16), pltpu.VMEM((d, t), BF16)],
    )(who, normed, d_swish, gated, low)


def recurrence_back_kernel(
    small, qkv, pre, d_mixed, mcol, mrow, payload, states, entering,
    d_qkv, d_pre_out, d_narrow_out, bias_out,
):
    t = pre.shape[0]
    kd = HEADS * DK
    ones = lower_ones(WIDE)
    reverse = upper_ones(WIDE)
    causal_rows = lax.broadcasted_iota(jnp.int32, (WIDE, WIDE), 0)
    causal_cols = lax.broadcasted_iota(jnp.int32, (WIDE, WIDE), 1)
    grads = [entering[h * DV : (h + 1) * DV, :].astype(F32) for h in range(HEADS)]
    bias_sum = jnp.zeros((1, kd), F32)
    for i in reversed(range(t // WIDE)):
        rows = slice(i * WIDE, (i + 1) * WIDE)
        marks = mcol[rows, :]
        last = mark_at(mrow, (i + 1) * WIDE - 1)
        if i:
            before = mark_at(mrow, i * WIDE - 1)
        else:
            before = payload[HEADS * DV :, :].astype(F32)[0:1, 0:1]
        pre_here = pre[rows, :]
        cumul = split_sum(ones, log_decay(pre_here))
        middle = cumul[SPAN - 1 : SPAN, :]
        end = cumul[WIDE - 1 : WIDE, :]
        queries = qkv[rows, 0:kd].astype(F32)
        keys = qkv[rows, kd : 2 * kd].astype(F32)
        lift = jnp.exp(cumul - middle)
        sink = jnp.exp(middle - cumul)
        rise = jnp.where(marks == before, jnp.exp(cumul), 0.0)
        fall = jnp.where(marks == last, jnp.exp(end - cumul), 0.0)
        lifted = (queries * lift).astype(BF16)
        lowered = (keys * sink).astype(BF16)
        carried = (queries * rise).astype(BF16)
        tail = (keys * fall).astype(BF16)
        keep = jnp.where(before == last, jnp.exp(end), 0.0)
        causal = (causal_rows >= causal_cols) & (marks == mrow[0:1, rows])
        slopes = []
        ends = []
        for h in range(HEADS):
            c = slice(h * DK, (h + 1) * DK)
            values = qkv[rows, 2 * kd + h * DV : 2 * kd + (h + 1) * DV]
            up = d_mixed[rows, h * DV : (h + 1) * DV]
            state = states[i, h]
            grad = grads[h]
            low_grad = grad.astype(BF16)
            scores = jnp.where(causal, nt(lifted[:, c], lowered[:, c]), 0.0).astype(BF16)
            d_scores = jnp.where(causal, nt(up, values), 0.0).astype(BF16)
            d_lifted = nn(d_scores, lowered[:, c])
            d_lowered = tn(d_scores, lifted[:, c])
            d_carried = nn(up, state)
            d_tail = nn(values, low_grad)
            d_values = tn(scores, up) + nt(tail[:, c], low_grad)
            d_qkv[rows, c] = (d_lifted * lift[:, c] + d_carried * rise[:, c]).astype(BF16)
            d_qkv[rows, kd + h * DK : kd + (h + 1) * DK] = (
                d_lowered * sink[:, c] + d_tail * fall[:, c]
            ).astype(BF16)
            d_qkv[rows, 2 * kd + h * DV : 2 * kd + (h + 1) * DV] = d_values.astype(BF16)
            tail_term = tail[:, c].astype(F32) * d_tail
            slopes.append(
                lifted[:, c].astype(F32) * d_lifted
                - lowered[:, c].astype(F32) * d_lowered
                + carried[:, c].astype(F32) * d_carried
                - tail_term
            )
            kept = keep[:, c] * grad
            ends.append(
                jnp.sum(tail_term, axis=0, keepdims=True)
                + jnp.sum(kept * state.astype(F32), axis=0, keepdims=True)
            )
            grads[h] = kept + tn(up, carried[:, c])
        d_decay = split_sum(reverse, jnp.concatenate(slopes, axis=1)) + jnp.concatenate(ends, axis=1)
        d_pre = d_decay * sigmoid(-pre_here) / GATE_NORM
        bias_sum = bias_sum + jnp.sum(d_pre, axis=0, keepdims=True)
        d_pre_out[rows, :] = d_pre.astype(BF16)
    bias_out[...] = jnp.broadcast_to(bias_sum, bias_out.shape)
    d_narrow_out[...] = nt(d_pre_out[...], expand_of(small)).astype(BF16)


def recurrence_back(small, qkv, pre, d_mixed, mcol, mrow, payload, states, entering):
    t, width = qkv.shape
    return call(
        recurrence_back_kernel,
        (
            sds((t, width), BF16),
            sds(pre.shape, BF16),
            sds((t, 16), BF16),
            sds((8, HEADS * DK), F32),
        ),
    )(small, qkv, pre, d_mixed, mcol, mrow, payload, states, entering)


def input_back_kernel(
    who, x, small, d_hidden, d_qkv, d_swish, d_narrow, q_own, k_own, v_own, s_own,
    a0, a1, a2, a3, b0, b1, b2, b3, grad_input, mixer_out, total, full,
):
    j = pl.program_id(0)
    steps = pl.num_programs(0)

    @pl.when(j == 0)
    def _():
        total[...] = nn(d_narrow[...], small[0:ROW_EXPAND, :])

    first = [r[...] for r in (a0, a1, a2, a3)]

    @pl.when(j < 2)
    def _():
        place_rows(who, full, q_own[...], first)

    @pl.when((j >= 2) & (j < 4))
    def _():
        place_rows(who, full, k_own[...], first)

    @pl.when((j >= 4) & (j < 8))
    def _():
        place_rows(who, full, v_own[...], first)

    @pl.when(j >= 8)
    def _():
        place_rows(who, full, s_own[...], [r[...] for r in (b0, b1, b2, b3)])

    @pl.when(j < 8)
    def _():
        total[...] += nt(d_qkv[...], full[...])

    @pl.when(j >= 8)
    def _():
        total[...] += nt(d_swish[...], full[...])

    @pl.when(j == steps - 1)
    def _():
        values = x[...].astype(F32)
        upstream = total[...]
        scale = lax.rsqrt(jnp.mean(values * values, axis=-1, keepdims=True) + EPSILON)
        unit = values * scale
        mixer_out[...] = jnp.broadcast_to(
            jnp.sum(upstream * unit, axis=0, keepdims=True), mixer_out.shape
        )
        scaled = upstream * row_of(small, ROW_MIXER)
        mean = jnp.mean(scaled * unit, axis=-1, keepdims=True)
        grad_input[...] = (d_hidden[...] + scale * (scaled - unit * mean)).astype(BF16)


def input_back(who, x, small, d_hidden, d_qkv, d_swish, d_narrow, owns, pieces, gate_pieces):
    t, d = x.shape
    half = d // 2
    kd = HEADS * DK
    vd = HEADS * DV
    qn = kd // 256
    vn = vd // 256
    wn = 2 * qn + vn
    const = lambda j: (0, 0)
    col = lambda low, count: (lambda j: (0, jnp.clip(j - low, 0, count - 1)))
    return call(
        input_back_kernel,
        (sds((t, d), BF16), sds((8, d), F32)),
        grid=(wn + vn,),
        in_specs=[
            SMEM,
            pl.BlockSpec((t, d), const),
            pl.BlockSpec(small.shape, const),
            pl.BlockSpec((t, d), const),
            pl.BlockSpec((t, 256), col(0, wn)),
            pl.BlockSpec((t, 256), col(wn, vn)),
            pl.BlockSpec((t, 16), const),
            pl.BlockSpec((half, 256), col(0, qn)),
            pl.BlockSpec((half, 256), col(qn, qn)),
            pl.BlockSpec((half, 256), col(2 * qn, vn)),
            pl.BlockSpec((half, 256), col(wn, vn)),
        ]
        + [pl.BlockSpec((half // 4, 256), col(0, wn))] * 4
        + [pl.BlockSpec((half // 4, 256), col(wn, vn))] * 4,
        out_specs=(pl.BlockSpec((t, d), const), pl.BlockSpec((8, d), const)),
        scratch_shapes=[pltpu.VMEM((t, d), F32), pltpu.VMEM((d, 256), BF16)],
    )(who, x, small, d_hidden, d_qkv, d_swish, d_narrow, *owns, *pieces, *gate_pieces)


def pair_grads_kernel(who, normed, d_qkv, keep, send, scratch, left_t):
    j = pl.program_id(0)

    @pl.when(j == 0)
    def _():
        left_t[...] = normed[...].T

    scratch[...] = nn(left_t[...], d_qkv[...]).astype(BF16)
    place_grads(who, keep, send, scratch, 0, slice(0, 256))


def pair_grads(who, normed, d_qkv):
    t, d = normed.shape
    n = 2 * HEADS * DK // 256
    shape = sds((2, 2, 4, 32, n * 256), BF16)
    spec = pl.BlockSpec((2, 2, 4, 32, 256), lambda j: (0, 0, 0, 0, j))
    return call(
        pair_grads_kernel,
        (shape, shape),
        grid=(n,),
        in_specs=[
            SMEM,
            pl.BlockSpec((t, d), lambda j: (0, 0)),
            pl.BlockSpec((t, 256), lambda j: (0, j)),
        ],
        out_specs=(spec, spec),
        scratch_shapes=[pltpu.VMEM((d, 256), BF16), pltpu.VMEM((d, t), BF16)],
    )(who, normed, d_qkv)


def value_grads_kernel(
    who, normed, d_values, d_narrow, narrow, d_pre, rows_in, bias_in, mixer_in,
    keep, send, scratch, strip, left_t, rows,
):
    t, d = normed.shape
    half = d // 2
    kd = HEADS * DK
    n = d_values.shape[1] // 256
    left_t[...] = normed[...].T
    for j in range(n):
        c = slice(j * 256, (j + 1) * 256)
        scratch[...] = nn(left_t[...], d_values[:, c]).astype(BF16)
        place_grads(who, keep, send, scratch, 0, c)
    rows[...] = jnp.zeros_like(rows)
    rows[LANE_MIXER : LANE_MIXER + 1, :] = mixer_in[0:1, :]
    rows[LANE_FEED : LANE_FEED + 1, :] = rows_in[0:1, :]
    part = kd // 2
    rows[LANE_BIAS : LANE_BIAS + 1, 0:part] = bias_in[0:1, 0:part]
    rows[LANE_BIAS : LANE_BIAS + 1, half : half + part] = bias_in[0:1, part:kd]
    part = DV // 2
    rows[LANE_HEADS : LANE_HEADS + 1, 0:part] = rows_in[1:2, 0:part]
    rows[LANE_HEADS : LANE_HEADS + 1, half : half + part] = rows_in[1:2, part:DV]
    columns = rows[...].T
    squeeze = nn(left_t[...], d_narrow[...])
    expand = tn(d_pre[...], narrow[...])
    part = kd // 2
    strip[...] = columns.astype(BF16)
    strip[:, 0:16] = squeeze.astype(BF16)
    strip[0:part, LANE_EXPAND : LANE_EXPAND + 16] = expand[0:part].astype(BF16)
    strip[half : half + part, LANE_EXPAND : LANE_EXPAND + 16] = expand[part:kd].astype(BF16)
    place_grads(who, keep, send, strip, 0, slice(n * 256, n * 256 + 128))


def value_grads(who, normed, d_qkv, d_narrow, narrow, d_pre, rows_in, bias_in, mixer_in):
    t, d = normed.shape
    vd = HEADS * DV
    shape = sds((2, 2, 4, 32, vd + 128), BF16)
    whole = lambda a: pl.BlockSpec(a.shape, lambda i: (0,) * len(a.shape))
    ins = (normed, d_qkv, d_narrow, narrow, d_pre, rows_in, bias_in, mixer_in)
    specs = [whole(a) for a in ins]
    specs[1] = pl.BlockSpec((t, vd), lambda i: (0, (2 * HEADS * DK) // vd))
    return call(
        value_grads_kernel,
        (shape, shape),
        grid=(1,),
        in_specs=[SMEM] + specs,
        out_specs=(whole(shape), whole(shape)),
        scratch_shapes=[
            pltpu.VMEM((d, 256), BF16),
            pltpu.VMEM((d, 128), BF16),
            pltpu.VMEM((d, t), BF16),
            pltpu.VMEM((128, d), F32),
        ],
    )(who, *ins)


def settle(who, parts, out_refs_of):
    me = who[2]
    for k, part in enumerate(parts):
        for zz in range(4):
            out_refs_of(me ^ (k * 4 + zz), part, zz)


def feed_settle_kernel(who, a, b, c, d, *rest, first):
    gate, up, down = rest if first else rest[3:]
    h = pl.program_id(1)
    me = who[2]
    for k, part in enumerate((a, b, c, d)):
        for zz in range(4):
            block = me ^ (k * 4 + zz)
            rows = pl.ds(pl.multiple_of(block * 32, 32), 32)
            gate[rows, :] = part[zz, 0:32, :].astype(F32)
            up[rows, :] = part[zz, 32:64, :].astype(F32)
            at = pl.ds(pl.multiple_of((block % 4) * 32, 32), 32)
            cols = pl.ds(pl.multiple_of((block // 4) * 256 + h * 128, 128), 128)
            down[at, cols] = part[zz, 64:96, :].astype(F32)


def feed_settle(who, parts, before, start, blocks, half, ff, d):
    halves = ff // 256
    first = before is None
    shapes = (sds((half, ff), F32), sds((half, ff), F32), sds((ff // 2, d), F32))
    wide = pl.BlockSpec((half, 128), lambda j, h: (0, h * halves + start + j))
    tall = pl.BlockSpec((128, d), lambda j, h: (start + j, 0))
    any_spec = pl.BlockSpec(memory_space=pl.ANY)
    return call(
        functools.partial(feed_settle_kernel, first=first),
        shapes,
        grid=(blocks, 2),
        in_specs=[SMEM]
        + [pl.BlockSpec((4, 96, 128), lambda j, h: (0, 0, 2 * j + h))] * 4
        + ([] if first else [any_spec] * 3),
        out_specs=(wide, wide, tall),
        input_output_aliases={} if first else {5: 0, 6: 1, 7: 2},
    )(who, *parts, *(() if first else before))


def pair_settle_kernel(who, a, b, c, d, left, right):
    me = who[2]
    count = left.shape[1]
    for k, part in enumerate((a, b, c, d)):
        for zz in range(4):
            rows = pl.ds(pl.multiple_of((me ^ (k * 4 + zz)) * 32, 32), 32)
            left[rows, :] = part[zz, :, 0:count].astype(F32)
            right[rows, :] = part[zz, :, count:].astype(F32)


def pair_settle(who, parts, half):
    count = parts[0].shape[2] // 2
    shape = sds((half, count), F32)
    return call(pair_settle_kernel, (shape, shape), in_specs=[SMEM] + [VMEM] * 4)(who, *parts)


def added(*terms):
    total = terms[0].astype(F32)
    for term in terms[1:]:
        total = total + term.astype(F32)
    return total.astype(BF16)


def swap(v, bit):
    count = lax.axis_size("replica")
    return lax.ppermute(v, "replica", [(i, i ^ bit) for i in range(count)])


def cross(v):
    return lax.ppermute(v, "fsdp", [(0, 1), (1, 0)])


def spread(piece):
    first = cross(piece)
    second = swap(first, 2)
    return (first, swap(first, 1), second, swap(second, 1))


def reduced(keep, send):
    got = swap(send, 1)
    over = cross(added(keep[1], got[1]))
    side = swap(added(keep[0, 1], got[0, 1], over[1]), 2)
    parts = [added(keep[0, 0, j], got[0, 0, j], over[0, j], side[j]) for j in range(4)]
    deep = [swap(parts[j], 4 * j) for j in range(1, 4)]
    own = added(parts[0], *deep)
    line = jnp.stack([own] + [swap(own, 4 * j) for j in range(1, 4)])
    beside = swap(line, 2)
    return (line, beside, swap(line, 1), swap(beside, 1))


def natural(keep, send):
    both = jnp.stack([keep, send])
    both = jnp.moveaxis(both, 0, 1)
    return both.reshape((2, 16) + keep.shape[3:])


def total_over(v, dim):
    v = lax.psum_scatter(v.astype(BF16), "fsdp", scatter_dimension=dim, tiled=True)
    return lax.psum(v, "replica").astype(F32)


def chain_join(earlier, later):
    factor_early, state_early, first_early, last_early = earlier
    factor_late, state_late, first_late, last_late = later
    joined = (first_late == last_early) | (last_early < 0) | (first_late < 0)
    linked = jnp.where(joined, factor_late, 0.0)
    return (
        linked * factor_early,
        linked[:, None] * state_early + state_late,
        jnp.where(first_early < 0, first_late, first_early),
        jnp.where(last_late < 0, last_early, last_late),
    )


def chained(payload, passing, first_mark):
    place = lax.axis_index("fsdp")
    own = (
        passing[0].reshape(HEADS, DK).astype(BF16),
        payload,
        first_mark.astype(BF16),
    )
    factors, payloads, firsts = [lax.all_gather(a, "fsdp") for a in own]
    rows = HEADS * DV

    def one(turn, carry):
        pick = lambda a: lax.dynamic_index_in_dim(a, turn, 0, False).astype(F32)
        factor, block, first = pick(factors), pick(payloads), pick(firsts)
        later = (factor, block[:rows].reshape(HEADS, DV, DK), first, block[rows, :1])
        earlier_factor, state, earlier_first, earlier_last = carry
        joined = (later[2] == earlier_last) | (earlier_last < 0)
        linked = jnp.where(joined, later[0], 0.0)
        return (
            linked * earlier_factor,
            linked[:, None, :] * state + later[1],
            jnp.where(earlier_first < 0, later[2], earlier_first),
            later[3],
        )

    none = -jnp.ones((1,), F32)
    start = (jnp.ones((HEADS, DK), F32), jnp.zeros((HEADS, DV, DK), F32), none, none)
    done = lax.fori_loop(0, place, one, start)
    marks = jnp.broadcast_to(done[3][:, None], (16, DK))
    return jnp.concatenate([done[1].reshape(rows, DK), marks]).astype(BF16)


def chained_back(back, passing, linked):
    count = lax.axis_size("fsdp")
    ahead = count - 1 - lax.axis_index("fsdp")
    factor = jnp.where(linked, passing[0], 0.0).reshape(HEADS, DK).astype(BF16)
    factors, backs = [lax.all_gather(a, "fsdp") for a in (factor, back)]

    def one(turn, grad):
        source = count - 1 - turn
        pick = lambda a: lax.dynamic_index_in_dim(a, source, 0, False).astype(F32)
        return pick(backs).reshape(HEADS, DV, DK) + pick(factors)[:, None, :] * grad

    grad = lax.fori_loop(0, ahead, one, jnp.zeros((HEADS, DV, DK), F32))
    return grad.reshape(HEADS * DV, DK).astype(BF16)


def on_device(
    inputs, segments, cotangent, mixer_gain, query_map, key_map, value_map, swish_map, squeeze,
    expand, forget_bias, head_gain, readout, feed_gain, gate_map, up_map, down_map,
):
    shards = lax.axis_size("fsdp")
    copies = lax.axis_size("replica")
    paired = shards == 2 and copies == 16
    t, d = inputs.shape
    kd, vd = HEADS * DK, HEADS * DV
    half = d // 2
    quarter = half // 4
    marks = segments[0].astype(F32)
    mcol, mrow = marks[:, None], marks[None, :]

    if paired:
        place = lax.axis_index("replica")
        core, side, deep = place % 2, (place // 2) % 2, place // 4
        x = lax.axis_index("fsdp")
        q = side * 2 + core
        who = jnp.stack([x, q, core * 8 + side * 4 + deep]).astype(jnp.int32)
    else:
        who = jnp.zeros((3,), jnp.int32)
        x = q = 0
        gather = lambda a, dim=0: lax.all_gather(a, "fsdp", axis=dim, tiled=True)
        query_map, key_map, value_map, swish_map, readout, gate_map, up_map, down_map = [
            gather(a)
            for a in (query_map, key_map, value_map, swish_map, readout, gate_map, up_map, down_map)
        ]
        mixer_gain, feed_gain, forget_bias, head_gain, squeeze = [
            gather(a) for a in (mixer_gain, feed_gain, forget_bias, head_gain, squeeze)
        ]
        expand = gather(expand, 1)

    def small_half(k):
        cut = lambda a, dim=0: lax.slice_in_dim(a, k * (a.shape[dim] // 2), (k + 1) * (a.shape[dim] // 2), axis=dim)
        return packed(cut(squeeze), cut(expand, 1), cut(mixer_gain), cut(feed_gain), cut(forget_bias), cut(head_gain))

    def packed(squeeze, expand, mixer_gain, feed_gain, forget_bias, head_gain):
        wide = lambda a: jnp.pad(a, ((0, 0), (0, half - a.shape[1])))
        mixed = jnp.concatenate([forget_bias, head_gain])[None]
        rows = [squeeze.T, wide(expand), mixer_gain[None], feed_gain[None], wide(mixed)]
        block = jnp.concatenate(rows)
        return jnp.pad(block, ((0, SMALL_ROWS - block.shape[0]), (0, 0)))

    ff = gate_map.shape[1]
    halves = ff // 256
    counts = chunk_blocks(halves)
    starts = [sum(counts[:i]) for i in range(len(counts))]

    def quarter_rows(a, k):
        return lax.dynamic_slice_in_dim(a, k * quarter, quarter, 0)

    if paired:
        small_own = packed(squeeze, expand, mixer_gain, feed_gain, forget_bias, head_gain)
        small_other = cross(small_own)
        small = jnp.concatenate(
            [jnp.where(x == 0, small_own, small_other), jnp.where(x == 0, small_other, small_own)],
            axis=1,
        )
        share = lambda maps: spread(jnp.concatenate([quarter_rows(a, q) for a in maps], axis=1))
        qkv_pieces = share((query_map, key_map, value_map))
        gate_pieces = share((swish_map, readout))
        feed_pieces = [
            spread(pack_feed(who, gate_map, up_map, down_map, s, n))
            for s, n in zip(starts, counts)
        ]
    else:
        small = jnp.concatenate([small_half(0), small_half(1)], axis=1)
        lower = lambda a: a[: a.shape[0] // 2]
        upper = lambda a: a[a.shape[0] // 2 :]
        share = lambda maps: tuple(
            jnp.concatenate([quarter_rows(upper(a), k) for a in maps], axis=1) for k in range(4)
        )
        qkv_pieces = share((query_map, key_map, value_map))
        gate_pieces = share((swish_map, readout))
        others = (upper(gate_map), upper(up_map), upper(down_map))
        feed_pieces = [
            tuple(
                pack_feed(jnp.full((3,), k, jnp.int32), *others, s, n) for k in range(4)
            )
            for s, n in zip(starts, counts)
        ]
        query_map, key_map, value_map, swish_map, readout, gate_map, up_map, down_map = [
            lower(a)
            for a in (query_map, key_map, value_map, swish_map, readout, gate_map, up_map, down_map)
        ]

    normed, qkv, pre, narrow = project(
        who, inputs, small, query_map, key_map, value_map, qkv_pieces
    )
    local, passing = local_state(qkv, pre, mcol, mrow)
    if paired:
        payload = lax.ppermute(local, "fsdp", [(0, 1)])
    else:
        payload = chained(local, passing, marks[:1])
    swish = swish_project(who, normed, swish_map, gate_pieces)
    mixed, states, gated, hidden, second = mixer(
        who, inputs, small, qkv, pre, swish, mcol, mrow, payload, readout, gate_pieces
    )

    totals = None
    feed_grads = []
    for s, n, pieces in zip(starts, counts, feed_pieces):
        *totals, keep, send = feed(
            who, second, cotangent, gate_map, up_map, down_map, pieces, totals, s, n
        )
        feed_grads.append((keep, send))
    output = (hidden + totals[0]).astype(BF16)

    d_hidden, low, d_swish, d_mixed, rows, back = mixer_back(
        who, small, totals[1], hidden, cotangent, swish, mixed, qkv, pre, mcol, payload,
        readout, gate_pieces,
    )
    if paired:
        entering = lax.ppermute(back, "fsdp", [(1, 0)])
    else:
        linked = marks[0] == payload[HEADS * DV, 0].astype(F32)
        entering = chained_back(back, passing, linked)
    gate_grad = gate_grads(who, normed, d_swish, gated, low)
    d_qkv, d_pre, d_narrow, bias_row = recurrence_back(
        small, qkv, pre, d_mixed, mcol, mrow, payload, states, entering
    )
    pair_grad = pair_grads(who, normed, d_qkv)
    grad_input, mixer_row = input_back(
        who, inputs, small, d_hidden, d_qkv, d_swish, d_narrow,
        (query_map, key_map, value_map, swish_map), qkv_pieces, gate_pieces,
    )
    value_grad = value_grads(
        who, normed, d_qkv, d_narrow, narrow, d_pre, rows, bias_row, mixer_row
    )

    if paired:
        feeds = None
        for (keep, send), s, n in zip(feed_grads, starts, counts):
            feeds = feed_settle(who, reduced(keep, send), feeds, s, n, half, ff, d)
        grad_gate, grad_up, grad_down = feeds
        grad_swish, grad_readout = pair_settle(who, reduced(*gate_grad), half)
        grad_query, grad_key = pair_settle(who, reduced(*pair_grad), half)
        parts = reduced(*value_grad)
        grad_value, strip = value_settle(who, parts, half)
        return (
            output, grad_input, strip[:, LANE_MIXER], grad_query, grad_key, grad_value, grad_swish,
            strip[:, :16], strip[: kd // 2, LANE_EXPAND : LANE_EXPAND + 16].T,
            strip[: kd // 2, LANE_BIAS], strip[: DV // 2, LANE_HEADS], grad_readout,
            strip[:, LANE_FEED], grad_gate, grad_up, grad_down,
        )

    gates, ups, downs = [], [], []
    for (keep, send), n in zip(feed_grads, counts):
        block = natural(keep, send)
        sides = lambda k: block[:, :, 32 * k : 32 * (k + 1), :].reshape(d, n, 2, 128)
        gates.append(sides(0))
        ups.append(sides(1))
        part = block[:, :, 64:96, :].reshape(2, 4, 128, n, 256)
        downs.append(part.transpose(0, 3, 2, 1, 4).reshape(2, n * 128, d))
    whole = lambda parts: jnp.concatenate(parts, axis=1).transpose(0, 2, 1, 3).reshape(d, ff)
    grad_gate, grad_up = whole(gates), whole(ups)
    grad_down = jnp.concatenate(downs, axis=1).reshape(ff, d)
    flat = lambda pair: natural(*pair).reshape(d, -1)
    gate_flat, pair_flat, value_flat = flat(gate_grad), flat(pair_grad), flat(value_grad)
    strip = value_flat[:, vd:]
    joined = lambda lane, count: jnp.concatenate(
        [strip[:count, lane], strip[half : half + count, lane]]
    )
    part = kd // 2
    grad_expand = jnp.concatenate([strip[:part, 16:32], strip[half : half + part, 16:32]]).T
    results = (
        joined(LANE_MIXER, half), pair_flat[:, :kd], pair_flat[:, kd:], value_flat[:, :vd],
        gate_flat[:, :vd], strip[:, :16], grad_expand, joined(LANE_BIAS, part),
        joined(LANE_HEADS, DV // 2), gate_flat[:, vd:], joined(LANE_FEED, half),
        grad_gate, grad_up, grad_down,
    )
    return (output, grad_input) + tuple(
        total_over(a, 1 if i == 6 else 0) for i, a in enumerate(results)
    )


def value_settle_kernel(who, a, b, c, d, left, right):
    me = who[2]
    count = left.shape[1]
    for k, part in enumerate((a, b, c, d)):
        for zz in range(4):
            rows = pl.ds(pl.multiple_of((me ^ (k * 4 + zz)) * 32, 32), 32)
            left[rows, :] = part[zz, :, 0:count].astype(F32)
            right[rows, :] = part[zz, :, count:].astype(F32)


def value_settle(who, parts, half):
    vd = HEADS * DV
    shapes = (sds((half, vd), F32), sds((half, 128), F32))
    return call(value_settle_kernel, shapes, in_specs=[SMEM] + [VMEM] * 4)(who, *parts)


def chunk_blocks(halves):
    parts = 3
    base, extra = divmod(halves, parts)
    return [base + (1 if i >= parts - extra else 0) for i in range(parts)]


def solution(mesh):
    placed = (
        P(("replica", "fsdp"), None),
        P("replica", "fsdp"),
        P(("replica", "fsdp"), None),
        P("fsdp"),
        P("fsdp", None),
        P("fsdp", None),
        P("fsdp", None),
        P("fsdp", None),
        P("fsdp", None),
        P(None, "fsdp"),
        P("fsdp"),
        P("fsdp"),
        P("fsdp", None),
        P("fsdp"),
        P("fsdp", None),
        P("fsdp", None),
        P("fsdp", None),
    )
    return jax.shard_map(
        on_device,
        mesh=mesh,
        in_specs=placed,
        out_specs=(
            P(("replica", "fsdp"), None),
            P(("replica", "fsdp"), None),
            P("fsdp"),
            P("fsdp", None),
            P("fsdp", None),
            P("fsdp", None),
            P("fsdp", None),
            P("fsdp", None),
            P(None, "fsdp"),
            P("fsdp"),
            P("fsdp"),
            P("fsdp", None),
            P("fsdp"),
            P("fsdp", None),
            P("fsdp", None),
            P("fsdp", None),
        ),
        check_vma=False,
    )
```

time: 1270 us -> 647 us (0.51)
  waiting for transfers between devices: 665 us -> 309 us
  matrix products: 186 us -> 0 us
  Pallas kernels: 0 us -> 181 us
  blocking collectives: 148 us -> 0 us
  starting transfers between devices: 1.39 us -> 111 us
  local copies, waits for them, and re-layouts: 115 us -> 18 us
  other arithmetic: 106 us -> 18.8 us
  loops' own time: 22.9 us -> 0 us
  between operations: 21.3 us -> 1.89 us
    reduce_scatter x10 -> x0, waiting for transfers between devices: 314 us -> none  [the longest x1 74.2 us: on_device(): lax.psum_scatter(grad_gate.astype(jnp.bfloat16), 'fsdp', scatter_dimensio...]
    ppermute x0 -> x95, waiting for transfers between devices: none -> 309 us  [the longest x81 159 us: swap(): return lax.ppermute(v, 'replica', [(i, i ^ bit) for i in range(count)])]
    dot_general x137 -> x0, matrix products: 186 us -> none  [the longest x30 113 us: product(): return jnp.einsum(form, left, right, preferred_element_type=jnp.float32)]
    pallas_call x0 -> x22, Pallas kernels: none -> 181 us  [the longest x3 51.2 us: feed(): call(functools.partial(feed_kernel, first=first, blocks=blocks), (sds((t,...]
    psum x1 -> x0, waiting for transfers between devices: 181 us -> none  [on_device(): lax.psum(parts[1].astype(jnp.bfloat16), 'replica').astype(jnp.float32)]
    all_gather x8 -> x0, waiting for transfers between devices: 164 us -> none  [the longest x1 67.2 us: on_device(): lax.all_gather(down_map, 'fsdp', axis=0, tiled=True)]
    ppermute x0 -> x95, starting transfers between devices: none -> 111 us  [the longest x81 94.4 us: swap(): return lax.ppermute(v, 'replica', [(i, i ^ bit) for i in range(count)])]
    all_gather x10 -> x0, blocking collectives: 74.5 us -> none  [the longest x2 28.1 us: entering(): lax.all_gather(a.astype(kind), axis)]
  transfers between devices with their start and end apart: 19 -> 95, of which waited for: 11 -> 32; matrix products, arithmetic and copies ran while one was open for 16% -> 5% of each run, Pallas kernels for 0% -> 20%
where the time goes in v1:
time: 647 us; the launch traced here: 640 us
  waiting for transfers between devices  309 us (48%)
  Pallas kernels  181 us (28%)
  starting transfers between devices  111 us (17%)
  other arithmetic  18.8 us (3%)
  local copies, waits for them, and re-layouts  18 us (3%)
    ppermute x81, waiting for transfers between devices, swap(): return lax.ppermute(v, 'replica', [(i, i ^ bit) for i in range(count)])  159 us
    ppermute x12, waiting for transfers between devices, cross(): return lax.ppermute(v, 'fsdp', [(0, 1), (1, 0)])  138 us
    ppermute x81, starting transfers between devices, swap(): return lax.ppermute(v, 'replica', [(i, i ^ bit) for i in range(count)])  94.4 us
    pallas_call x3, Pallas kernels, feed(): call(functools.partial(feed_kernel, first=first, blocks=blocks), (sds((t,...  51.2 us
    pallas_call x3, Pallas kernels, feed_settle(): call(functools.partial(feed_settle_kernel, first=first), shapes, grid=(bl...  21.3 us
    pallas_call x1, Pallas kernels, input_back(): call(input_back_kernel, (sds((t, d), BF16), sds((8, d), F32)), grid=(wn +...  15.1 us
    convert_element_type x24, other arithmetic, added(): return total.astype(BF16)  15.1 us
  transfers between devices with their start and end apart: 95, of which 32 were waited for; matrix products, arithmetic and copies ran while one was open for 5% of the time, Pallas kernels for 20%

profile of v1, /device:TPU:0, one launch (start us, length us, event | category | flops | bytes accessed | tf_op | source)
XLA Modules:
  0.0 639.8 jit_solution(12543800689030630210)
XLA Ops:
  26.2 33.2 %collective-permute-done = bf16[48,512]{1,0:T(8,128)(2,1)S(1)} collective-permute-done((bf16[48,512]{1,0:T(8,128)(2,1)S(1)}, bf16[48,512]{1,0:T(8,128)(2,1)S(1)}, u32[]{:S(2)}, u32[]{:S(2)}) %collective-permute-start) | collective-permute-done | bytes 49184 | tf_op jit(solution)/shard_map/ppermute | solution.py:932
  63.4 15.2 %collective-permute-done.14.r0 = bf16[128,3072]{1,0:T(8,128)(2,1)} collective-permute-done((bf16[128,3072]{1,0:T(8,128)(2,1)}, bf16[128,3072]{1,0:T(8,128)(2,1)}, u32[]{:S(2)}, u32[]{:S(2)}) %collective-permute-start.14) | collective-permute-done | bytes 786464 | tf_op jit(solution)/shard_map/ppermute | solution.py:932
  85.8 9.8 %shard_map.288 = (bf16[512,1024]{1,0:T(8,128)(2,1)}, bf16[512,2048]{1,0:T(8,128)(2,1)}, f32[512,512]{1,0:T(8,128)}, bf16[512,16]{1,0:T(8,128)(2,1)}) custom-call(s32[3]{0:T(128)} %pad_add_fusion.who, bf16[512,1024]{1,0:T(8,128)(2,1)} %x.11, bf16[48,1024]{1,0:T(8,128)(2,1)} %pad_maximum_fusion.8.small, bf16[512,512]{1,0:T(8,128)(2,1)} %q_own.3, ...), custom_call_target="tpu_custom_call" | custom-call | tf_op jit(solution)/shard_map/pallas_call | solution.py:185
  100.3 26.0 %collective-permute-done.20.r2 = bf16[128,2304]{1,0:T(8,128)(2,1)} collective-permute-done((bf16[128,2304]{1,0:T(8,128)(2,1)}, bf16[128,2304]{1,0:T(8,128)(2,1)}, u32[]{:S(2)}, u32[]{:S(2)}) %collective-permute-start.20) | collective-permute-done | bytes 589856 | tf_op jit(solution)/shard_map/ppermute | solution.py:928
  138.7 10.6 %shard_map.291 = (f32[512,1024]{1,0:T(8,128)}, bf16[4,4,256,128]{3,2,1,0:T(8,128)(2,1)}, bf16[512,1024]{1,0:T(8,128)(2,1)}, f32[512,1024]{1,0:T(8,128)}, bf16[512,1024]{1,0:T(8,128)(2,1)}) custom-call(s32[3]{0:T(128)} %pad_add_fusion.who, bf16[512,1024]{1,0:T(8,128)(2,1)} %x.11, bf16[48,1024]{1,0:T(8,128)(2,1)} %pad_maximum_fusion.8.small, ...), custom_call_target="tpu_custom_call" | custom-call | tf_op jit(solution)/shard_map/pallas_call | solution.py:339
  150.1 14.2 %shard_map.295 = (f32[512,1024]{1,0:T(8,128)}, f32[512,1024]{1,0:T(8,128)}, bf16[2,2,4,96,768]{4,3,2,1,0:T(8,128)(2,1)}, bf16[2,2,4,96,768]{4,3,2,1,0:T(8,128)(2,1)}) custom-call(s32[3]{0:T(128)} %pad_add_fusion.who, bf16[512,1024]{1,0:T(8,128)(2,1)} %get-tuple-element.76.second, bf16[512,1024]{1,0:T(8,128)(2,1)} %cot.7, bf16[512,2816]{1,0:T(8,128)(2,1)} %g1.11, ...), custom_call_target="tpu_custom_call" | custom-call | tf_op jit(solution)/shard_map/pallas_call | solution.py:419
  165.5 18.3 %shard_map.296 = (f32[512,1024]{1,0:T(8,128)}, f32[512,1024]{1,0:T(8,128)}, bf16[2,2,4,96,1024]{4,3,2,1,0:T(8,128)(2,1)}, bf16[2,2,4,96,1024]{4,3,2,1,0:T(8,128)(2,1)}) custom-call(s32[3]{0:T(128)} %pad_add_fusion.who, bf16[512,1024]{1,0:T(8,128)(2,1)} %get-tuple-element.76.second, bf16[512,1024]{1,0:T(8,128)(2,1)} %cot.7, bf16[512,2816]{1,0:T(8,128)(2,1)} %g1.11, ...), custom_call_target="tpu_custom_call" | custom-call | tf_op jit(solution)/shard_map/pallas_call | solution.py:419
  185.0 18.6 %shard_map.297 = (f32[512,1024]{1,0:T(8,128)}, f32[512,1024]{1,0:T(8,128)}, bf16[2,2,4,96,1024]{4,3,2,1,0:T(8,128)(2,1)}, bf16[2,2,4,96,1024]{4,3,2,1,0:T(8,128)(2,1)}) custom-call(s32[3]{0:T(128)} %pad_add_fusion.who, bf16[512,1024]{1,0:T(8,128)(2,1)} %get-tuple-element.76.second, bf16[512,1024]{1,0:T(8,128)(2,1)} %cot.7, bf16[512,2816]{1,0:T(8,128)(2,1)} %g1.11, ...), custom_call_target="tpu_custom_call" | custom-call | tf_op jit(solution)/shard_map/pallas_call | solution.py:419
  203.6 11.4 %shard_map.298 = (f32[512,1024]{1,0:T(8,128)}, bf16[512,1024]{1,0:T(8,128)(2,1)}, bf16[512,1024]{1,0:T(8,128)(2,1)}, bf16[512,1024]{1,0:T(8,128)(2,1)}, f32[8,1024]{1,0:T(8,128)}, /*index=5*/bf16[1024,128]{1,0:T(8,128)(2,1)}) custom-call(s32[3]{0:T(128)} %pad_add_fusion.who, bf16[48,1024]{1,0:T(8,128)(2,1)} %pad_maximum_fusion.8.small, ...), custom_call_target="tpu_custom_call" | custom-call | tf_op jit(solution)/shard_map/pallas_call | solution.py:544
  216.5 9.2 %collective-permute-done.22.entering = bf16[1024,128]{1,0:T(8,128)(2,1)S(1)} collective-permute-done((bf16[1024,128]{1,0:T(8,128)(2,1)}, bf16[1024,128]{1,0:T(8,128)(2,1)S(1)}, u32[]{:S(2)}, u32[]{:S(2)}) %collective-permute-start.22) | collective-permute-done | bytes 262176 | tf_op jit(solution)/shard_map/ppermute | solution.py:1137
  226.4 11.1 %shard_map.299 = (bf16[512,2048]{1,0:T(8,128)(2,1)}, bf16[512,512]{1,0:T(8,128)(2,1)}, bf16[512,16]{1,0:T(8,128)(2,1)}, f32[8,512]{1,0:T(8,128)}) custom-call(bf16[48,1024]{1,0:T(8,128)(2,1)} %pad_maximum_fusion.8.small, bf16[512,2048]{1,0:T(8,128)(2,1)} %get-tuple-element.71.qkv, f32[512,512]{1,0:T(8,128)} %get-tuple-element.72.pre, ...), custom_call_target="tpu_custom_call" | custom-call | tf_op jit(solution)/shard_map/pallas_call | solution.py:680
  243.0 15.1 %shard_map.300 = (bf16[512,1024]{1,0:T(8,128)(2,1)}, f32[8,1024]{1,0:T(8,128)}) custom-call(s32[3]{0:T(128)} %pad_add_fusion.who, bf16[512,1024]{1,0:T(8,128)(2,1)} %x.11, bf16[48,1024]{1,0:T(8,128)(2,1)} %pad_maximum_fusion.8.small, f32[512,1024]{1,0:T(8,128)} %get-tuple-element.84.d_hidden, bf16[512,2048]{1,0:T(8,128)(2,1)} %get-tuple-element.88.d_qkv.d_values, ...), custom_call_target="tpu_custom_call" | custom-call | tf_op jit(solution)/shard_map/pallas_call | solution.py:752
  269.0 9.5 %shard_map.305 = (bf16[2,2,4,32,2048]{4,3,2,1,0:T(8,128)(2,1)}, bf16[2,2,4,32,2048]{4,3,2,1,0:T(8,128)(2,1)}) custom-call(s32[3]{0:T(128)} %pad_add_fusion.who, bf16[512,1024]{1,0:T(8,128)(2,1)} %get-tuple-element.73.normed, bf16[512,1024]{1,0:T(8,128)(2,1)} %get-tuple-element.89.d_swish, bf16[512,1024]{1,0:T(8,128)(2,1)} %get-tuple-element.105.gated, ...), custom_call_target="tpu_custom_call" | custom-call | tf_op jit(solution)/shard_map/pallas_call | solution.py:584
  281.2 11.1 %collective-permute-done.24 = bf16[2,4,32,1152]{3,2,1,0:T(8,128)(2,1)} collective-permute-done((bf16[2,4,32,1152]{3,2,1,0:T(8,128)(2,1)}, bf16[2,4,32,1152]{3,2,1,0:T(8,128)(2,1)}, u32[]{:S(2)}, u32[]{:S(2)}) %collective-permute-start.24) | collective-permute-done | bytes 589856 | tf_op jit(solution)/shard_map/ppermute | solution.py:932
  295.7 5.7 collective-permute-done.37
  328.9 11.3 %collective-permute-done.84 = bf16[2,4,96,768]{3,2,1,0:T(8,128)(2,1)S(1)} collective-permute-done((bf16[2,4,96,768]{3,2,1,0:T(8,128)(2,1)S(1)}, bf16[2,4,96,768]{3,2,1,0:T(8,128)(2,1)S(1)}, u32[]{:S(2)}, u32[]{:S(2)}) %collective-permute-start.84) | collective-permute-done | bytes 1179680 | tf_op jit(solution)/shard_map/ppermute | solution.py:932
  348.7 14.0 %collective-permute-done.48 = bf16[2,4,32,2048]{3,2,1,0:T(8,128)(2,1)S(1)} collective-permute-done((bf16[2,4,32,2048]{3,2,1,0:T(8,128)(2,1)S(1)}, bf16[2,4,32,2048]{3,2,1,0:T(8,128)(2,1)S(1)}, u32[]{:S(2)}, u32[]{:S(2)}) %collective-permute-start.48) | collective-permute-done | bytes 1048608 | tf_op jit(solution)/shard_map/ppermute | solution.py:932
  370.0 5.5 collective-permute-done.49
  376.3 20.1 %collective-permute-done.60 = bf16[2,4,96,1024]{3,2,1,0:T(8,128)(2,1)S(1)} collective-permute-done((bf16[2,4,96,1024]{3,2,1,0:T(8,128)(2,1)S(1)}, bf16[2,4,96,1024]{3,2,1,0:T(8,128)(2,1)S(1)}, u32[]{:S(2)}, u32[]{:S(2)}) %collective-permute-start.60) | collective-permute-done | bytes 1572896 | tf_op jit(solution)/shard_map/ppermute | solution.py:932
  396.8 30.8 %collective-permute-done.72 = bf16[2,4,96,1024]{3,2,1,0:T(8,128)(2,1)S(1)} collective-permute-done((bf16[2,4,96,1024]{3,2,1,0:T(8,128)(2,1)S(1)}, bf16[2,4,96,1024]{3,2,1,0:T(8,128)(2,1)S(1)}, u32[]{:S(2)}, u32[]{:S(2)}) %collective-permute-start.72) | collective-permute-done | bytes 1572896 | tf_op jit(solution)/shard_map/ppermute | solution.py:932
  442.2 5.9 collective-permute-done.61
  451.0 13.6 %collective-permute-done.73 = bf16[4,96,1024]{2,1,0:T(8,128)(2,1)S(1)} collective-permute-done((bf16[4,96,1024]{2,1,0:T(8,128)(2,1)S(1)}, bf16[4,96,1024]{2,1,0:T(8,128)(2,1)S(1)}, u32[]{:S(2)}, u32[]{:S(2)}) %collective-permute-start.73) | collective-permute-done | bytes 786464 | tf_op jit(solution)/shard_map/ppermute | solution.py:928
  469.5 13.1 %collective-permute-done.63 = bf16[96,1024]{1,0:T(8,128)(2,1)S(1)} collective-permute-done((bf16[96,1024]{1,0:T(8,128)(2,1)S(1)}, bf16[96,1024]{1,0:T(8,128)(2,1)S(1)}, u32[]{:S(2)}, u32[]{:S(2)}) %collective-permute-start.63) | collective-permute-done | bytes 196640 | tf_op jit(solution)/shard_map/ppermute | solution.py:928
  488.0 8.1 %collective-permute-start.53 = (bf16[32,2048]{1,0:T(8,128)(2,1)S(1)}, bf16[32,2048]{1,0:T(8,128)(2,1)S(1)}, u32[]{:S(2)}, u32[]{:S(2)}) collective-permute-start(bf16[32,2048]{1,0:T(8,128)(2,1)S(1)} %add_convert_fusion.10), channel_id=1, source_target_pairs={{0,8},{2,10},{4,12},{6,14},{8,0},{10,2},{12,4},{14,6},{16,24},{18,... | collective-permute-start | bytes 393224 | tf_op jit(solution)/shard_map/ppermute | solution.py:928
  505.8 11.0 %collective-permute-start.65 = (bf16[96,1024]{1,0:T(8,128)(2,1)S(1)}, bf16[96,1024]{1,0:T(8,128)(2,1)S(1)}, u32[]{:S(2)}, u32[]{:S(2)}) collective-permute-start(bf16[96,1024]{1,0:T(8,128)(2,1)S(1)} %add_convert_fusion.8), channel_id=1, source_target_pairs={{0,8},{2,10},{4,12},{6,14},{8,0},{10,2},{12,4},{14,6},{16,24},{18,... | collective-permute-start | bytes 589832 | tf_op jit(solution)/shard_map/ppermute | solution.py:928
  523.9 7.8 %collective-permute-done.66 = bf16[96,1024]{1,0:T(8,128)(2,1)S(1)} collective-permute-done((bf16[96,1024]{1,0:T(8,128)(2,1)S(1)}, bf16[96,1024]{1,0:T(8,128)(2,1)S(1)}, u32[]{:S(2)}, u32[]{:S(2)}) %collective-permute-start.66) | collective-permute-done | bytes 196640 | tf_op jit(solution)/shard_map/ppermute | solution.py:928
  531.7 7.5 %collective-permute-start.89 = (bf16[96,768]{1,0:T(8,128)(2,1)S(1)}, bf16[96,768]{1,0:T(8,128)(2,1)S(1)}, u32[]{:S(2)}, u32[]{:S(2)}) collective-permute-start(bf16[96,768]{1,0:T(8,128)(2,1)S(1)} %add_convert_fusion.9), channel_id=1, source_target_pairs={{0,8},{2,10},{4,12},{6,14},{8,0},{10,2},{12,4},{14,6},{16,24},{18,... | collective-permute-start | bytes 442376 | tf_op jit(solution)/shard_map/ppermute | solution.py:928
  547.5 8.2 %collective-permute-done.56.b = bf16[4,32,2048]{2,1,0:T(8,128)(2,1)S(1)} collective-permute-done((bf16[4,32,2048]{2,1,0:T(8,128)(2,1)S(1)}, bf16[4,32,2048]{2,1,0:T(8,128)(2,1)S(1)}, u32[]{:S(2)}, u32[]{:S(2)}) %collective-permute-start.56) | collective-permute-done | bytes 524320 | tf_op jit(solution)/shard_map/ppermute | solution.py:928
  555.6 42.1 %collective-permute-done.92.b = bf16[4,96,768]{2,1,0:T(8,128)(2,1)} collective-permute-done((bf16[4,96,768]{2,1,0:T(8,128)(2,1)S(1)}, bf16[4,96,768]{2,1,0:T(8,128)(2,1)}, u32[]{:S(2)}, u32[]{:S(2)}) %collective-permute-start.92) | collective-permute-done | bytes 589856 | tf_op jit(solution)/shard_map/ppermute | solution.py:928
  618.2 6.0 shard_map.307
  624.2 7.7 %shard_map.308 = (f32[512,2816]{1,0:T(8,128)}, f32[512,2816]{1,0:T(8,128)}, f32[1408,1024]{1,0:T(8,128)}) custom-call(s32[3]{0:T(128)} %pad_add_fusion.who, bf16[4,96,1024]{2,1,0:T(8,128)(2,1)} %copy-done.6, bf16[4,96,1024]{2,1,0:T(8,128)(2,1)} %copy-done.26, ...), custom_call_target="tpu_custom_call", output_to_operand_aliasing={{0}: (5, {}), {1}: (6, {}), {2}: (7, {})} | custom-call | tf_op jit(solution)/shard_map/pallas_call | solution.py:891
  631.9 7.7 %shard_map.309 = (f32[512,2816]{1,0:T(8,128)}, f32[512,2816]{1,0:T(8,128)}, f32[1408,1024]{1,0:T(8,128)}) custom-call(s32[3]{0:T(128)} %pad_add_fusion.who, bf16[4,96,1024]{2,1,0:T(8,128)(2,1)} %copy-done.5, bf16[4,96,1024]{2,1,0:T(8,128)(2,1)} %copy-done.25, ...), custom_call_target="tpu_custom_call", output_to_operand_aliasing={{0}: (5, {}), {1}: (6, {}), {2}: (7, {})} | custom-call | tf_op jit(solution)/shard_map/pallas_call | solution.py:891
  (335 shorter events, 198.9 us)
Async XLA Ops:
  10.3 52.4 %collective-permute-start.10 = (bf16[128,3072]{1,0:T(8,128)(2,1)}, bf16[128,3072]{1,0:T(8,128)(2,1)S(1)}, u32[]{:S(2)}, u32[]{:S(2)}) collective-permute-start(bf16[128,3072]{1,0:T(8,128)(2,1)} %shard_map.292), channel_id=1, source_target_pairs={{0,1},{1,0},{2,3},{3,2},{4,5},{5,4},{6,7},{7,6},{8,9},{9,8},{10,11... | collective-permute-start | bytes 2359304 | tf_op jit(solution)/shard_map/ppermute | solution.py:932
  11.5 49.6 %collective-permute-start.5 = (bf16[128,2048]{1,0:T(8,128)(2,1)S(1)}, bf16[128,2048]{1,0:T(8,128)(2,1)S(1)}, u32[]{:S(2)}, u32[]{:S(2)}) collective-permute-start(bf16[128,2048]{1,0:T(8,128)(2,1)S(1)} %pad_maximum_fusion.4), channel_id=1, source_target_pairs={{0,1},{1,0},{2,3},{3,2},{4,5},{5,4},{6,7},{7,6},{8,9},{9,8},{10,11... | collective-permute-start | bytes 1572872 | tf_op jit(solution)/shard_map/ppermute | solution.py:932
  17.0 45.7 %collective-permute-start.18 = (bf16[128,2304]{1,0:T(8,128)(2,1)}, bf16[128,2304]{1,0:T(8,128)(2,1)}, u32[]{:S(2)}, u32[]{:S(2)}) collective-permute-start(bf16[128,2304]{1,0:T(8,128)(2,1)} %shard_map.294), channel_id=1, source_target_pairs={{0,1},{1,0},{2,3},{3,2},{4,5},{5,4},{6,7},{7,6},{8,9},{9,8},{10,11... | collective-permute-start | bytes 1769480 | tf_op jit(solution)/shard_map/ppermute | solution.py:932
  18.5 44.8 %collective-permute-start.3 = (bf16[128,2048]{1,0:T(8,128)(2,1)S(1)}, bf16[128,2048]{1,0:T(8,128)(2,1)S(1)}, u32[]{:S(2)}, u32[]{:S(2)}) collective-permute-start(bf16[128,2048]{1,0:T(8,128)(2,1)S(1)} %collective-permute-done.1.r0.a0), channel_id=1, source_target_pairs={{0,4},{2,6},{4,0},{6,2},{8,12},{10,14},{12,8},{14,10},{16,20},{18,... | collective-permute-start | bytes 1572872 | tf_op jit(solution)/shard_map/ppermute | solution.py:928
  20.7 38.7 %collective-permute-start = (bf16[48,512]{1,0:T(8,128)(2,1)S(1)}, bf16[48,512]{1,0:T(8,128)(2,1)S(1)}, u32[]{:S(2)}, u32[]{:S(2)}) collective-permute-start(bf16[48,512]{1,0:T(8,128)(2,1)S(1)} %pad.14), channel_id=1, source_target_pairs={{0,1},{1,0},{2,3},{3,2},{4,5},{5,4},{6,7},{7,6},{8,9},{9,8},{10,11... | collective-permute-start | bytes 147464 | tf_op jit(solution)/shard_map/ppermute | solution.py:932
  78.6 51.4 %collective-permute-start.16 = (bf16[128,3072]{1,0:T(8,128)(2,1)}, bf16[128,3072]{1,0:T(8,128)(2,1)}, u32[]{:S(2)}, u32[]{:S(2)}) collective-permute-start(bf16[128,3072]{1,0:T(8,128)(2,1)} %collective-permute-done.14.r0), channel_id=1, source_target_pairs={{0,4},{2,6},{4,0},{6,2},{8,12},{10,14},{12,8},{14,10},{16,20},{18,... | collective-permute-start | bytes 2359304 | tf_op jit(solution)/shard_map/ppermute | solution.py:928
  80.0 50.5 %collective-permute-start.12 = (bf16[128,3072]{1,0:T(8,128)(2,1)S(1)}, bf16[128,3072]{1,0:T(8,128)(2,1)}, u32[]{:S(2)}, u32[]{:S(2)}) collective-permute-start(bf16[128,3072]{1,0:T(8,128)(2,1)S(1)} %collective-permute-done.10.r0), channel_id=1, source_target_pairs={{0,4},{2,6},{4,0},{6,2},{8,12},{10,14},{12,8},{14,10},{16,20},{18,... | collective-permute-start | bytes 2359304 | tf_op jit(solution)/shard_map/ppermute | solution.py:928
  80.6 45.7 %collective-permute-start.20 = (bf16[128,2304]{1,0:T(8,128)(2,1)}, bf16[128,2304]{1,0:T(8,128)(2,1)}, u32[]{:S(2)}, u32[]{:S(2)}) collective-permute-start(bf16[128,2304]{1,0:T(8,128)(2,1)} %collective-permute-done.18.r0), channel_id=1, source_target_pairs={{0,4},{2,6},{4,0},{6,2},{8,12},{10,14},{12,8},{14,10},{16,20},{18,... | collective-permute-start | bytes 1769480 | tf_op jit(solution)/shard_map/ppermute | solution.py:928
  82.1 47.8 %collective-permute-start.19 = (bf16[128,2304]{1,0:T(8,128)(2,1)}, bf16[128,2304]{1,0:T(8,128)(2,1)}, u32[]{:S(2)}, u32[]{:S(2)}) collective-permute-start(bf16[128,2304]{1,0:T(8,128)(2,1)} %collective-permute-done.18.r0), channel_id=1, source_target_pairs={{0,2},{2,0},{4,6},{6,4},{8,10},{10,8},{12,14},{14,12},{16,18},{18,... | collective-permute-start | bytes 1769480 | tf_op jit(solution)/shard_map/ppermute | solution.py:928
  83.7 46.8 %collective-permute-start.8 = (bf16[128,2048]{1,0:T(8,128)(2,1)S(1)}, bf16[128,2048]{1,0:T(8,128)(2,1)S(1)}, u32[]{:S(2)}, u32[]{:S(2)}) collective-permute-start(bf16[128,2048]{1,0:T(8,128)(2,1)S(1)} %collective-permute-done.7.r2.b2), channel_id=1, source_target_pairs={{0,2},{2,0},{4,6},{6,4},{8,10},{10,8},{12,14},{14,12},{16,18},{18,... | collective-permute-start | bytes 1572872 | tf_op jit(solution)/shard_map/ppermute | solution.py:928
  129.8 34.5 %collective-permute-start.15 = (bf16[128,3072]{1,0:T(8,128)(2,1)}, bf16[128,3072]{1,0:T(8,128)(2,1)S(1)}, u32[]{:S(2)}, u32[]{:S(2)}) collective-permute-start(bf16[128,3072]{1,0:T(8,128)(2,1)} %collective-permute-done.14.r0), channel_id=1, source_target_pairs={{0,2},{2,0},{4,6},{6,4},{8,10},{10,8},{12,14},{14,12},{16,18},{18,... | collective-permute-start | bytes 2359304 | tf_op jit(solution)/shard_map/ppermute | solution.py:928
  129.9 34.5 %collective-permute-start.17 = (bf16[128,3072]{1,0:T(8,128)(2,1)}, bf16[128,3072]{1,0:T(8,128)(2,1)S(1)}, u32[]{:S(2)}, u32[]{:S(2)}) collective-permute-start(bf16[128,3072]{1,0:T(8,128)(2,1)} %collective-permute-done.16.r2), channel_id=1, source_target_pairs={{0,2},{2,0},{4,6},{6,4},{8,10},{10,8},{12,14},{14,12},{16,18},{18,... | collective-permute-start | bytes 2359304 | tf_op jit(solution)/shard_map/ppermute | solution.py:928
  130.4 53.4 %collective-permute-start.11 = (bf16[128,3072]{1,0:T(8,128)(2,1)S(1)}, bf16[128,3072]{1,0:T(8,128)(2,1)S(1)}, u32[]{:S(2)}, u32[]{:S(2)}) collective-permute-start(bf16[128,3072]{1,0:T(8,128)(2,1)S(1)} %collective-permute-done.10.r0), channel_id=1, source_target_pairs={{0,2},{2,0},{4,6},{6,4},{8,10},{10,8},{12,14},{14,12},{16,18},{18,... | collective-permute-start | bytes 2359304 | tf_op jit(solution)/shard_map/ppermute | solution.py:928
  130.5 53.4 %collective-permute-start.13 = (bf16[128,3072]{1,0:T(8,128)(2,1)}, bf16[128,3072]{1,0:T(8,128)(2,1)S(1)}, u32[]{:S(2)}, u32[]{:S(2)}) collective-permute-start(bf16[128,3072]{1,0:T(8,128)(2,1)} %collective-permute-done.12.r2), channel_id=1, source_target_pairs={{0,2},{2,0},{4,6},{6,4},{8,10},{10,8},{12,14},{14,12},{16,18},{18,... | collective-permute-start | bytes 2359304 | tf_op jit(solution)/shard_map/ppermute | solution.py:928
  278.6 61.8 %collective-permute-start.59 = (bf16[2,2,4,96,1024]{4,3,2,1,0:T(8,128)(2,1)}, bf16[2,2,4,96,1024]{4,3,2,1,0:T(8,128)(2,1)S(1)}, u32[]{:S(2)}, u32[]{:S(2)}) collective-permute-start(bf16[2,2,4,96,1024]{4,3,2,1,0:T(8,128)(2,1)} %get-tuple-element.112), channel_id=1, source_target_pairs={{0,2},{2,0},{4,6},{6,4},{8,10},{10,8},{12,14},{14,12},{16,18},{18,... | collective-permute-start | bytes 9437192 | tf_op jit(solution)/shard_map/ppermute | solution.py:928
  280.0 62.0 %collective-permute-start.71 = (bf16[2,2,4,96,1024]{4,3,2,1,0:T(8,128)(2,1)}, bf16[2,2,4,96,1024]{4,3,2,1,0:T(8,128)(2,1)S(1)}, u32[]{:S(2)}, u32[]{:S(2)}) collective-permute-start(bf16[2,2,4,96,1024]{4,3,2,1,0:T(8,128)(2,1)} %get-tuple-element.114), channel_id=1, source_target_pairs={{0,2},{2,0},{4,6},{6,4},{8,10},{10,8},{12,14},{14,12},{16,18},{18,... | collective-permute-start | bytes 9437192 | tf_op jit(solution)/shard_map/ppermute | solution.py:928
  324.1 38.6 %collective-permute-start.48 = (bf16[2,4,32,2048]{3,2,1,0:T(8,128)(2,1)S(1)}, bf16[2,4,32,2048]{3,2,1,0:T(8,128)(2,1)S(1)}, u32[]{:S(2)}, u32[]{:S(2)}) collective-permute-start(bf16[2,4,32,2048]{3,2,1,0:T(8,128)(2,1)S(1)} %fusion.6), channel_id=1, source_target_pairs={{0,1},{1,0},{2,3},{3,2},{4,5},{5,4},{6,7},{7,6},{8,9},{9,8},{10,11... | collective-permute-start | bytes 3145736 | tf_op jit(solution)/shard_map/ppermute | solution.py:932
  348.2 48.1 %collective-permute-start.60 = (bf16[2,4,96,1024]{3,2,1,0:T(8,128)(2,1)S(1)}, bf16[2,4,96,1024]{3,2,1,0:T(8,128)(2,1)S(1)}, u32[]{:S(2)}, u32[]{:S(2)}) collective-permute-start(bf16[2,4,96,1024]{3,2,1,0:T(8,128)(2,1)S(1)} %fusion), channel_id=1, source_target_pairs={{0,1},{1,0},{2,3},{3,2},{4,5},{5,4},{6,7},{7,6},{8,9},{9,8},{10,11... | collective-permute-start | bytes 4718600 | tf_op jit(solution)/shard_map/ppermute | solution.py:932
  362.6 64.9 %collective-permute-start.72 = (bf16[2,4,96,1024]{3,2,1,0:T(8,128)(2,1)S(1)}, bf16[2,4,96,1024]{3,2,1,0:T(8,128)(2,1)S(1)}, u32[]{:S(2)}, u32[]{:S(2)}) collective-permute-start(bf16[2,4,96,1024]{3,2,1,0:T(8,128)(2,1)S(1)} %fusion.1), channel_id=1, source_target_pairs={{0,1},{1,0},{2,3},{3,2},{4,5},{5,4},{6,7},{7,6},{8,9},{9,8},{10,11... | collective-permute-start | bytes 4718600 | tf_op jit(solution)/shard_map/ppermute | solution.py:932
  368.5 61.1 %collective-permute-start.44 = (bf16[4,32,1024]{2,1,0:T(8,128)(2,1)S(1)}, bf16[4,32,1024]{2,1,0:T(8,128)(2,1)S(1)}, u32[]{:S(2)}, u32[]{:S(2)}) collective-permute-start(bf16[4,32,1024]{2,1,0:T(8,128)(2,1)S(1)} %pad_maximum_fusion.7.a), channel_id=1, source_target_pairs={{0,4},{2,6},{4,0},{6,2},{8,12},{10,14},{12,8},{14,10},{16,20},{18,... | collective-permute-start | bytes 786440 | tf_op jit(solution)/shard_map/ppermute | solution.py:928
  369.7 60.0 %collective-permute-start.86 = (bf16[96,768]{1,0:T(8,128)(2,1)S(1)}, bf16[96,768]{1,0:T(8,128)(2,1)S(1)}, u32[]{:S(2)}, u32[]{:S(2)}) collective-permute-start(bf16[96,768]{1,0:T(8,128)(2,1)S(1)} %get-tuple-element.166), channel_id=1, source_target_pairs={{0,8},{2,10},{4,12},{6,14},{8,0},{10,2},{12,4},{14,6},{16,24},{18,... | collective-permute-start | bytes 442376 | tf_op jit(solution)/shard_map/ppermute | solution.py:928
  375.5 55.1 %collective-permute-start.88 = (bf16[96,768]{1,0:T(8,128)(2,1)S(1)}, bf16[96,768]{1,0:T(8,128)(2,1)S(1)}, u32[]{:S(2)}, u32[]{:S(2)}) collective-permute-start(bf16[96,768]{1,0:T(8,128)(2,1)S(1)} %get-tuple-element.167), channel_id=1, source_target_pairs={{0,24},{2,26},{4,28},{6,30},{8,16},{10,18},{12,20},{14,22},{16,8},... | collective-permute-start | bytes 442376 | tf_op jit(solution)/shard_map/ppermute | solution.py:928
  396.3 36.9 %collective-permute-start.87 = (bf16[96,768]{1,0:T(8,128)(2,1)S(1)}, bf16[96,768]{1,0:T(8,128)(2,1)S(1)}, u32[]{:S(2)}, u32[]{:S(2)}) collective-permute-start(bf16[96,768]{1,0:T(8,128)(2,1)S(1)} %get-tuple-element.168), channel_id=1, source_target_pairs={{0,16},{2,18},{4,20},{6,22},{8,24},{10,26},{12,28},{14,30},{16,0},... | collective-permute-start | bytes 442376 | tf_op jit(solution)/shard_map/ppermute | solution.py:928
  437.1 45.8 %collective-permute-start.33 = (bf16[4,32,1152]{2,1,0:T(8,128)(2,1)S(1)}, bf16[4,32,1152]{2,1,0:T(8,128)(2,1)S(1)}, u32[]{:S(2)}, u32[]{:S(2)}) collective-permute-start(bf16[4,32,1152]{2,1,0:T(8,128)(2,1)S(1)} %pad_maximum_fusion.6.a), channel_id=1, source_target_pairs={{0,2},{2,0},{4,6},{6,4},{8,10},{10,8},{12,14},{14,12},{16,18},{18,... | collective-permute-start | bytes 884744 | tf_op jit(solution)/shard_map/ppermute | solution.py:928
  448.0 36.8 %collective-permute-start.32 = (bf16[4,32,1152]{2,1,0:T(8,128)(2,1)S(1)}, bf16[4,32,1152]{2,1,0:T(8,128)(2,1)S(1)}, u32[]{:S(2)}, u32[]{:S(2)}) collective-permute-start(bf16[4,32,1152]{2,1,0:T(8,128)(2,1)S(1)} %pad_maximum_fusion.6.a), channel_id=1, source_target_pairs={{0,4},{2,6},{4,0},{6,2},{8,12},{10,14},{12,8},{14,10},{16,20},{18,... | collective-permute-start | bytes 884744 | tf_op jit(solution)/shard_map/ppermute | solution.py:928
  544.0 54.5 %collective-permute-start.68 = (bf16[4,96,1024]{2,1,0:T(8,128)(2,1)S(1)}, bf16[4,96,1024]{2,1,0:T(8,128)(2,1)S(1)}, u32[]{:S(2)}, u32[]{:S(2)}) collective-permute-start(bf16[4,96,1024]{2,1,0:T(8,128)(2,1)S(1)} %pad_maximum_fusion.a), channel_id=1, source_target_pairs={{0,4},{2,6},{4,0},{6,2},{8,12},{10,14},{12,8},{14,10},{16,20},{18,... | collective-permute-start | bytes 2359304 | tf_op jit(solution)/shard_map/ppermute | solution.py:928
  545.2 53.7 %collective-permute-start.80 = (bf16[4,96,1024]{2,1,0:T(8,128)(2,1)S(1)}, bf16[4,96,1024]{2,1,0:T(8,128)(2,1)S(1)}, u32[]{:S(2)}, u32[]{:S(2)}) collective-permute-start(bf16[4,96,1024]{2,1,0:T(8,128)(2,1)S(1)} %pad_maximum_fusion.1.a), channel_id=1, source_target_pairs={{0,4},{2,6},{4,0},{6,2},{8,12},{10,14},{12,8},{14,10},{16,20},{18,... | collective-permute-start | bytes 2359304 | tf_op jit(solution)/shard_map/ppermute | solution.py:928
  546.8 50.9 %collective-permute-start.92 = (bf16[4,96,768]{2,1,0:T(8,128)(2,1)S(1)}, bf16[4,96,768]{2,1,0:T(8,128)(2,1)}, u32[]{:S(2)}, u32[]{:S(2)}) collective-permute-start(bf16[4,96,768]{2,1,0:T(8,128)(2,1)S(1)} %pad_maximum_fusion.2.a), channel_id=1, source_target_pairs={{0,4},{2,6},{4,0},{6,2},{8,12},{10,14},{12,8},{14,10},{16,20},{18,... | collective-permute-start | bytes 1769480 | tf_op jit(solution)/shard_map/ppermute | solution.py:928
  547.5 50.3 %collective-permute-start.93 = (bf16[4,96,768]{2,1,0:T(8,128)(2,1)S(1)}, bf16[4,96,768]{2,1,0:T(8,128)(2,1)S(1)}, u32[]{:S(2)}, u32[]{:S(2)}) collective-permute-start(bf16[4,96,768]{2,1,0:T(8,128)(2,1)S(1)} %pad_maximum_fusion.2.a), channel_id=1, source_target_pairs={{0,2},{2,0},{4,6},{6,4},{8,10},{10,8},{12,14},{14,12},{16,18},{18,... | collective-permute-start | bytes 1769480 | tf_op jit(solution)/shard_map/ppermute | solution.py:928
  555.6 42.6 %collective-permute-start.58 = (bf16[4,32,2048]{2,1,0:T(8,128)(2,1)S(1)}, bf16[4,32,2048]{2,1,0:T(8,128)(2,1)S(1)}, u32[]{:S(2)}, u32[]{:S(2)}) collective-permute-start(bf16[4,32,2048]{2,1,0:T(8,128)(2,1)S(1)} %collective-permute-done.56.b), channel_id=1, source_target_pairs={{0,2},{2,0},{4,6},{6,4},{8,10},{10,8},{12,14},{14,12},{16,18},{18,... | collective-permute-start | bytes 1572872 | tf_op jit(solution)/shard_map/ppermute | solution.py:928
  597.7 34.1 %collective-permute-start.69 = (bf16[4,96,1024]{2,1,0:T(8,128)(2,1)S(1)}, bf16[4,96,1024]{2,1,0:T(8,128)(2,1)}, u32[]{:S(2)}, u32[]{:S(2)}) collective-permute-start(bf16[4,96,1024]{2,1,0:T(8,128)(2,1)S(1)} %pad_maximum_fusion.a), channel_id=1, source_target_pairs={{0,2},{2,0},{4,6},{6,4},{8,10},{10,8},{12,14},{14,12},{16,18},{18,... | collective-permute-start | bytes 2359304 | tf_op jit(solution)/shard_map/ppermute | solution.py:928
  598.5 33.4 %collective-permute-start.70 = (bf16[4,96,1024]{2,1,0:T(8,128)(2,1)S(1)}, bf16[4,96,1024]{2,1,0:T(8,128)(2,1)}, u32[]{:S(2)}, u32[]{:S(2)}) collective-permute-start(bf16[4,96,1024]{2,1,0:T(8,128)(2,1)S(1)} %collective-permute-done.68.b), channel_id=1, source_target_pairs={{0,2},{2,0},{4,6},{6,4},{8,10},{10,8},{12,14},{14,12},{16,18},{18,... | collective-permute-start | bytes 2359304 | tf_op jit(solution)/shard_map/ppermute | solution.py:928
  (113 other events, 2329.7 us)

commit v2 on v1

--- a/solution.py
+++ b/solution.py
@@ -27,10 +27,9 @@
 ROW_MIXED = 34
 SMALL_ROWS = 48
 LANE_EXPAND = 16
-LANE_MIXER = 32
-LANE_FEED = 33
-LANE_BIAS = 34
-LANE_HEADS = 35
+LANE_FEED = 32
+LANE_BIAS = 33
+LANE_HEADS = 34
 
 
 def nn(a, b):
@@ -49,10 +48,17 @@
     return 1.0 / (1.0 + jnp.exp(-v))
 
 
-def call(kernel, out_shape, **kw):
+def cost(us):
+    return pl.CostEstimate(
+        flops=int(us * 1e7), bytes_accessed=int(us * 3.6e4), transcendentals=0
+    )
+
+
+def call(kernel, out_shape, us=5, **kw):
     return pl.pallas_call(
         kernel,
         out_shape=out_shape,
+        cost_estimate=cost(us),
         compiler_params=pltpu.CompilerParams(vmem_limit_bytes=VMEM_BYTES),
         **kw,
     )
@@ -141,7 +147,7 @@
 
 
 def project_kernel(
-    who, x, small, q_own, k_own, v_own, r0, r1, r2, r3, normed, qkv, pre, narrow_out, full
+    who, x, small, k_own, v_own, r0, r1, r2, r3, normed, kv, pre, narrow_out, full
 ):
     j = pl.program_id(0)
 
@@ -160,25 +166,21 @@
 
     @pl.when(j < 2)
     def _():
-        place_rows(who, full, q_own[...], pieces)
-
-    @pl.when((j >= 2) & (j < 4))
-    def _():
         place_rows(who, full, k_own[...], pieces)
 
-    @pl.when(j >= 4)
+    @pl.when(j >= 2)
     def _():
         place_rows(who, full, v_own[...], pieces)
 
-    qkv[...] = nn(normed[...], full[...]).astype(BF16)
-
-
-def project(who, x, small, q_own, k_own, v_own, pieces):
+    kv[...] = nn(normed[...], full[...]).astype(BF16)
+
+
+def project(who, x, small, k_own, v_own, pieces):
     t, d = x.shape
     half = d // 2
     kd = HEADS * DK
     vd = HEADS * DV
-    width = 2 * kd + vd
+    width = kd + vd
     const = lambda j: (0, 0)
     qn = kd // 256
     vn = vd // 256
@@ -191,8 +193,7 @@
             pl.BlockSpec((t, d), const),
             pl.BlockSpec(small.shape, const),
             pl.BlockSpec((half, 256), lambda j: (0, jnp.minimum(j, qn - 1))),
-            pl.BlockSpec((half, 256), lambda j: (0, jnp.clip(j - qn, 0, qn - 1))),
-            pl.BlockSpec((half, 256), lambda j: (0, jnp.clip(j - 2 * qn, 0, vn - 1))),
+            pl.BlockSpec((half, 256), lambda j: (0, jnp.clip(j - qn, 0, vn - 1))),
         ]
         + [pl.BlockSpec((half // 4, 256), lambda j: (0, j))] * 4,
         out_specs=(
@@ -202,38 +203,54 @@
             pl.BlockSpec((t, 16), const),
         ),
         scratch_shapes=[pltpu.VMEM((d, 256), BF16)],
-    )(who, x, small, q_own, k_own, v_own, *pieces)
-
-
-def swish_kernel(who, normed, own, r0, r1, r2, r3, out, full):
-    place_rows(who, full, own[...], [r[...] for r in (r0, r1, r2, r3)])
-    out[...] = nn(normed[...], full[...])
-
-
-def swish_project(who, normed, own, pieces):
+    )(who, x, small, k_own, v_own, *pieces)
+
+
+def swish_kernel(who, normed, q_own, s_own, r0, r1, r2, r3, queries, swish, full):
+    j = pl.program_id(0)
+    pieces = [r[...] for r in (r0, r1, r2, r3)]
+
+    @pl.when(j < 2)
+    def _():
+        place_rows(who, full, q_own[...], pieces)
+        queries[...] = nn(normed[...], full[...]).astype(BF16)
+
+    @pl.when(j >= 2)
+    def _():
+        place_rows(who, full, s_own[...], pieces)
+        swish[...] = nn(normed[...], full[...])
+
+
+def swish_project(who, normed, q_own, s_own, pieces):
     t, d = normed.shape
     half = d // 2
+    kd = HEADS * DK
     vd = HEADS * DV
+    qn = kd // 256
+    vn = vd // 256
+    low = lambda j: (0, jnp.minimum(j, qn - 1))
+    high = lambda j: (0, jnp.clip(j - qn, 0, vn - 1))
     return call(
         swish_kernel,
-        sds((t, vd), F32),
-        grid=(vd // 256,),
+        (sds((t, kd), BF16), sds((t, vd), F32)),
+        grid=(qn + vn,),
         in_specs=[
             SMEM,
             pl.BlockSpec((t, d), lambda j: (0, 0)),
-            pl.BlockSpec((half, 256), lambda j: (0, j)),
+            pl.BlockSpec((half, 256), low),
+            pl.BlockSpec((half, 256), high),
         ]
         + [pl.BlockSpec((half // 4, 256), lambda j: (0, j))] * 4,
-        out_specs=pl.BlockSpec((t, 256), lambda j: (0, j)),
+        out_specs=(pl.BlockSpec((t, 256), low), pl.BlockSpec((t, 256), high)),
         scratch_shapes=[pltpu.VMEM((d, 256), BF16)],
-    )(who, normed, own, *pieces)
+    )(who, normed, q_own, s_own, *pieces)
 
 
 def mark_at(mrow, place):
     return mrow[0:1, place : place + 1]
 
 
-def state_kernel(qkv, pre, mcol, mrow, payload, passing):
+def state_kernel(kv, pre, mcol, mrow, payload, passing):
     t = pre.shape[0]
     kd = HEADS * DK
     ones = lower_ones(WIDE)
@@ -245,13 +262,13 @@
         end = cumul[WIDE - 1 : WIDE, :]
         total = total + end
         last = mark_at(mrow, (i + 1) * WIDE - 1)
-        keys = qkv[rows, kd : 2 * kd].astype(F32)
+        keys = kv[rows, 0:kd].astype(F32)
         tail = jnp.where(mcol[rows, :] == last, keys * jnp.exp(end - cumul), 0.0).astype(BF16)
         if i:
             keep = jnp.where(mark_at(mrow, i * WIDE - 1) == last, jnp.exp(end), 0.0)
         for h in range(HEADS):
             c = slice(h * DK, (h + 1) * DK)
-            values = qkv[rows, 2 * kd + h * DV : 2 * kd + (h + 1) * DV]
+            values = kv[rows, kd + h * DV : kd + (h + 1) * DV]
             update = tn(values, tail[:, c])
             states[h] = states[h] * keep[:, c] + update if i else update
     for h in range(HEADS):
@@ -262,15 +279,14 @@
     passing[...] = jnp.broadcast_to(passes, passing.shape)
 
 
-def local_state(qkv, pre, mcol, mrow):
+def local_state(kv, pre, mcol, mrow):
     return call(
         state_kernel,
-        (sds((HEADS * DV + 16, DK), BF16), sds((8, HEADS * DK), F32)),
-    )(qkv, pre, mcol, mrow)
+        (sds((HEADS * DV + 16, DK), BF16), sds((8, HEADS * DK), F32)), us=5)(kv, pre, mcol, mrow)
 
 
 def mixer_kernel(
-    who, x, small, qkv, pre, swish, mcol, mrow, payload, own, r0, r1, r2, r3,
+    who, x, small, q, kv, pre, swish, mcol, mrow, payload, own, r0, r1, r2, r3,
     mixed_out, states_out, gated_out, hidden_out, second_out, full,
 ):
     t, d = x.shape
@@ -288,8 +304,8 @@
         cumul = split_sum(ones, log_decay(pre[rows, :]))
         middle = cumul[SPAN - 1 : SPAN, :]
         end = cumul[WIDE - 1 : WIDE, :]
-        queries = qkv[rows, 0:kd].astype(F32)
-        keys = qkv[rows, kd : 2 * kd].astype(F32)
+        queries = q[rows, :].astype(F32)
+        keys = kv[rows, 0:kd].astype(F32)
         lifted = (queries * jnp.exp(cumul - middle)).astype(BF16)
         lowered = (keys * jnp.exp(middle - cumul)).astype(BF16)
         carried = jnp.where(marks == before, queries * jnp.exp(cumul), 0.0).astype(BF16)
@@ -298,7 +314,7 @@
         causal = (causal_rows >= causal_cols) & (marks == mrow[0:1, rows])
         for h in range(HEADS):
             c = slice(h * DK, (h + 1) * DK)
-            values = qkv[rows, 2 * kd + h * DV : 2 * kd + (h + 1) * DV]
+            values = kv[rows, kd + h * DV : kd + (h + 1) * DV]
             low_state = states[h].astype(BF16)
             states_out[i, h] = low_state
             scores = jnp.where(causal, nt(lifted[:, c], lowered[:, c]), 0.0).astype(BF16)
@@ -322,11 +338,11 @@
     ).astype(BF16)
 
 
-def mixer(who, x, small, qkv, pre, swish, mcol, mrow, payload, own, pieces):
+def mixer(who, x, small, q, kv, pre, swish, mcol, mrow, payload, own, pieces):
     t, d = x.shape
     vd = HEADS * DV
     quarter = own.shape[0] // 4
-    right = pl.BlockSpec((quarter, d), lambda i: (0, 1))
+    right = pl.BlockSpec((quarter, d), lambda i: (0, 0))
     whole = lambda a: pl.BlockSpec(a.shape, lambda i: (0,) * a.ndim)
     outs = (
         sds((t, vd), F32),
@@ -335,15 +351,14 @@
         sds((t, d), F32),
         sds((t, d), BF16),
     )
-    ins = (x, small, qkv, pre, swish, mcol, mrow, payload, own)
+    ins = (x, small, q, kv, pre, swish, mcol, mrow, payload, own)
     return call(
         mixer_kernel,
         outs,
         grid=(1,),
         in_specs=[SMEM] + [whole(a) for a in ins] + [right] * 4,
         out_specs=tuple(whole(a) for a in outs),
-        scratch_shapes=[pltpu.VMEM((vd, d), BF16)],
-    )(who, *ins, *pieces)
+        scratch_shapes=[pltpu.VMEM((vd, d), BF16)], us=11)(who, *ins, *pieces)
 
 
 def feed_kernel(
@@ -419,6 +434,7 @@
     return call(
         functools.partial(feed_kernel, first=first, blocks=blocks),
         (sds((t, d), F32), sds((t, d), F32), grads_shape, grads_shape),
+        us=1 + 4.5 * blocks,
         grid=(blocks,),
         in_specs=[
             SMEM, full, full, left, right, left, right,
@@ -460,6 +476,7 @@
     return pl.pallas_call(
         pack_kernel,
         out_shape=sds((quarter, blocks * 768), BF16),
+        cost_estimate=cost(blocks),
         grid_spec=pltpu.PrefetchScalarGridSpec(
             num_scalar_prefetch=1,
             grid=(blocks,),
@@ -473,7 +490,7 @@
 
 
 def mixer_back_kernel(
-    who, small, d_second, hidden, cot, swish, mixed, qkv, pre, mcol, payload,
+    who, small, d_second, hidden, cot, swish, mixed, q, pre, mcol, payload,
     own, r0, r1, r2, r3,
     d_hidden_out, low_out, d_swish_out, d_mixed_out, rows_out, back_out, full, d_gated,
 ):
@@ -516,7 +533,7 @@
         rows = slice(i * WIDE, (i + 1) * WIDE)
         cumul = split_sum(ones, log_decay(pre[rows, :])) + base
         base = cumul[WIDE - 1 : WIDE, :]
-        queries = qkv[rows, 0:kd].astype(F32)
+        queries = q[rows, :].astype(F32)
         carried = jnp.where(mcol[rows, :] == before, queries * jnp.exp(cumul), 0.0).astype(BF16)
         for h in range(HEADS):
             sums[h] = sums[h] + tn(
@@ -526,11 +543,11 @@
         back_out[h * DV : (h + 1) * DV, :] = sums[h].astype(BF16)
 
 
-def mixer_back(who, small, d_second, hidden, cot, swish, mixed, qkv, pre, mcol, payload, own, pieces):
+def mixer_back(who, small, d_second, hidden, cot, swish, mixed, q, pre, mcol, payload, own, pieces):
     t, d = hidden.shape
     vd = HEADS * DV
     quarter = own.shape[0] // 4
-    right = pl.BlockSpec((quarter, d), lambda i: (0, 1))
+    right = pl.BlockSpec((quarter, d), lambda i: (0, 0))
     whole = lambda a: pl.BlockSpec(a.shape, lambda i: (0,) * len(a.shape))
     outs = (
         sds((t, d), F32),
@@ -540,15 +557,14 @@
         sds((8, d), F32),
         sds((HEADS * DV, DK), BF16),
     )
-    ins = (small, d_second, hidden, cot, swish, mixed, qkv, pre, mcol, payload, own)
+    ins = (small, d_second, hidden, cot, swish, mixed, q, pre, mcol, payload, own)
     return call(
         mixer_back_kernel,
         outs,
         grid=(1,),
         in_specs=[SMEM] + [whole(a) for a in ins] + [right] * 4,
         out_specs=tuple(whole(a) for a in outs),
-        scratch_shapes=[pltpu.VMEM((vd, d), BF16), pltpu.VMEM((t, vd), F32)],
-    )(who, *ins, *pieces)
+        scratch_shapes=[pltpu.VMEM((vd, d), BF16), pltpu.VMEM((t, vd), F32)], us=11)(who, *ins, *pieces)
 
 
 def gate_grads_kernel(who, normed, d_swish, gated, low, keep, send, scratch, left_t):
@@ -593,12 +609,11 @@
             pl.BlockSpec((t, 256), lambda j: (0, jnp.maximum(j - n, 0))),
         ],
         out_specs=(spec, spec),
-        scratch_shapes=[pltpu.VMEM((d, 256), BF16), pltpu.VMEM((d, t), BF16)],
-    )(who, normed, d_swish, gated, low)
+        scratch_shapes=[pltpu.VMEM((d, 256), BF16), pltpu.VMEM((d, t), BF16)], us=9)(who, normed, d_swish, gated, low)
 
 
 def recurrence_back_kernel(
-    small, qkv, pre, d_mixed, mcol, mrow, payload, states, entering,
+    small, q, kv, pre, d_mixed, mcol, mrow, payload, states, entering,
     d_qkv, d_pre_out, d_narrow_out, bias_out,
 ):
     t = pre.shape[0]
@@ -621,8 +636,8 @@
         cumul = split_sum(ones, log_decay(pre_here))
         middle = cumul[SPAN - 1 : SPAN, :]
         end = cumul[WIDE - 1 : WIDE, :]
-        queries = qkv[rows, 0:kd].astype(F32)
-        keys = qkv[rows, kd : 2 * kd].astype(F32)
+        queries = q[rows, :].astype(F32)
+        keys = kv[rows, 0:kd].astype(F32)
         lift = jnp.exp(cumul - middle)
         sink = jnp.exp(middle - cumul)
         rise = jnp.where(marks == before, jnp.exp(cumul), 0.0)
@@ -637,7 +652,7 @@
         ends = []
         for h in range(HEADS):
             c = slice(h * DK, (h + 1) * DK)
-            values = qkv[rows, 2 * kd + h * DV : 2 * kd + (h + 1) * DV]
+            values = kv[rows, kd + h * DV : kd + (h + 1) * DV]
             up = d_mixed[rows, h * DV : (h + 1) * DV]
             state = states[i, h]
             grad = grads[h]
@@ -675,8 +690,9 @@
     d_narrow_out[...] = nt(d_pre_out[...], expand_of(small)).astype(BF16)
 
 
-def recurrence_back(small, qkv, pre, d_mixed, mcol, mrow, payload, states, entering):
-    t, width = qkv.shape
+def recurrence_back(small, q, kv, pre, d_mixed, mcol, mrow, payload, states, entering):
+    t = q.shape[0]
+    width = q.shape[1] + kv.shape[1]
     return call(
         recurrence_back_kernel,
         (
@@ -684,8 +700,7 @@
             sds(pre.shape, BF16),
             sds((t, 16), BF16),
             sds((8, HEADS * DK), F32),
-        ),
-    )(small, qkv, pre, d_mixed, mcol, mrow, payload, states, entering)
+        ), us=11)(small, q, kv, pre, d_mixed, mcol, mrow, payload, states, entering)
 
 
 def input_back_kernel(
@@ -700,10 +715,11 @@
         total[...] = nn(d_narrow[...], small[0:ROW_EXPAND, :])
 
     first = [r[...] for r in (a0, a1, a2, a3)]
+    other = [r[...] for r in (b0, b1, b2, b3)]
 
     @pl.when(j < 2)
     def _():
-        place_rows(who, full, q_own[...], first)
+        place_rows(who, full, q_own[...], other)
 
     @pl.when((j >= 2) & (j < 4))
     def _():
@@ -715,7 +731,7 @@
 
     @pl.when(j >= 8)
     def _():
-        place_rows(who, full, s_own[...], [r[...] for r in (b0, b1, b2, b3)])
+        place_rows(who, full, s_own[...], other)
 
     @pl.when(j < 8)
     def _():
@@ -748,6 +764,7 @@
     vn = vd // 256
     wn = 2 * qn + vn
     const = lambda j: (0, 0)
+    beyond = lambda j: (0, jnp.where(j < wn, jnp.minimum(j, qn - 1), j - wn + qn))
     col = lambda low, count: (lambda j: (0, jnp.clip(j - low, 0, count - 1)))
     return call(
         input_back_kernel,
@@ -766,58 +783,26 @@
             pl.BlockSpec((half, 256), col(2 * qn, vn)),
             pl.BlockSpec((half, 256), col(wn, vn)),
         ]
-        + [pl.BlockSpec((half // 4, 256), col(0, wn))] * 4
-        + [pl.BlockSpec((half // 4, 256), col(wn, vn))] * 4,
+        + [pl.BlockSpec((half // 4, 256), col(qn, qn + vn))] * 4
+        + [pl.BlockSpec((half // 4, 256), beyond)] * 4,
         out_specs=(pl.BlockSpec((t, d), const), pl.BlockSpec((8, d), const)),
-        scratch_shapes=[pltpu.VMEM((t, d), F32), pltpu.VMEM((d, 256), BF16)],
-    )(who, x, small, d_hidden, d_qkv, d_swish, d_narrow, *owns, *pieces, *gate_pieces)
-
-
-def pair_grads_kernel(who, normed, d_qkv, keep, send, scratch, left_t):
-    j = pl.program_id(0)
-
-    @pl.when(j == 0)
-    def _():
-        left_t[...] = normed[...].T
-
-    scratch[...] = nn(left_t[...], d_qkv[...]).astype(BF16)
-    place_grads(who, keep, send, scratch, 0, slice(0, 256))
-
-
-def pair_grads(who, normed, d_qkv):
-    t, d = normed.shape
-    n = 2 * HEADS * DK // 256
-    shape = sds((2, 2, 4, 32, n * 256), BF16)
-    spec = pl.BlockSpec((2, 2, 4, 32, 256), lambda j: (0, 0, 0, 0, j))
-    return call(
-        pair_grads_kernel,
-        (shape, shape),
-        grid=(n,),
-        in_specs=[
-            SMEM,
-            pl.BlockSpec((t, d), lambda j: (0, 0)),
-            pl.BlockSpec((t, 256), lambda j: (0, j)),
-        ],
-        out_specs=(spec, spec),
-        scratch_shapes=[pltpu.VMEM((d, 256), BF16), pltpu.VMEM((d, t), BF16)],
-    )(who, normed, d_qkv)
-
-
-def value_grads_kernel(
-    who, normed, d_values, d_narrow, narrow, d_pre, rows_in, bias_in, mixer_in,
+        scratch_shapes=[pltpu.VMEM((t, d), F32), pltpu.VMEM((d, 256), BF16)], us=15)(who, x, small, d_hidden, d_qkv, d_swish, d_narrow, *owns, *pieces, *gate_pieces)
+
+
+def late_grads_kernel(
+    who, normed, d_qkv, d_narrow, narrow, d_pre, rows_in, bias_in,
     keep, send, scratch, strip, left_t, rows,
 ):
     t, d = normed.shape
     half = d // 2
     kd = HEADS * DK
-    n = d_values.shape[1] // 256
+    n = d_qkv.shape[1] // 256
     left_t[...] = normed[...].T
     for j in range(n):
         c = slice(j * 256, (j + 1) * 256)
-        scratch[...] = nn(left_t[...], d_values[:, c]).astype(BF16)
+        scratch[...] = nn(left_t[...], d_qkv[:, c]).astype(BF16)
         place_grads(who, keep, send, scratch, 0, c)
     rows[...] = jnp.zeros_like(rows)
-    rows[LANE_MIXER : LANE_MIXER + 1, :] = mixer_in[0:1, :]
     rows[LANE_FEED : LANE_FEED + 1, :] = rows_in[0:1, :]
     part = kd // 2
     rows[LANE_BIAS : LANE_BIAS + 1, 0:part] = bias_in[0:1, 0:part]
@@ -836,19 +821,17 @@
     place_grads(who, keep, send, strip, 0, slice(n * 256, n * 256 + 128))
 
 
-def value_grads(who, normed, d_qkv, d_narrow, narrow, d_pre, rows_in, bias_in, mixer_in):
+def late_grads(who, normed, d_qkv, d_narrow, narrow, d_pre, rows_in, bias_in):
     t, d = normed.shape
-    vd = HEADS * DV
-    shape = sds((2, 2, 4, 32, vd + 128), BF16)
+    shape = sds((2, 2, 4, 32, d_qkv.shape[1] + 128), BF16)
     whole = lambda a: pl.BlockSpec(a.shape, lambda i: (0,) * len(a.shape))
-    ins = (normed, d_qkv, d_narrow, narrow, d_pre, rows_in, bias_in, mixer_in)
-    specs = [whole(a) for a in ins]
-    specs[1] = pl.BlockSpec((t, vd), lambda i: (0, (2 * HEADS * DK) // vd))
+    ins = (normed, d_qkv, d_narrow, narrow, d_pre, rows_in, bias_in)
     return call(
-        value_grads_kernel,
+        late_grads_kernel,
         (shape, shape),
+        us=10,
         grid=(1,),
-        in_specs=[SMEM] + specs,
+        in_specs=[SMEM] + [whole(a) for a in ins],
         out_specs=(whole(shape), whole(shape)),
         scratch_shapes=[
             pltpu.VMEM((d, 256), BF16),
@@ -859,11 +842,21 @@
     )(who, *ins)
 
 
-def settle(who, parts, out_refs_of):
+def settle_kernel(who, a, b, c, d, *outs):
     me = who[2]
-    for k, part in enumerate(parts):
+    for k, part in enumerate((a, b, c, d)):
         for zz in range(4):
-            out_refs_of(me ^ (k * 4 + zz), part, zz)
+            rows = pl.ds(pl.multiple_of((me ^ (k * 4 + zz)) * 32, 32), 32)
+            at = 0
+            for out in outs:
+                count = out.shape[1]
+                out[rows, :] = part[zz, :, at : at + count].astype(F32)
+                at += count
+
+
+def settle(who, parts, half, widths):
+    shapes = tuple(sds((half, width), F32) for width in widths)
+    return call(settle_kernel, shapes, us=4, in_specs=[SMEM] + [VMEM] * 4)(who, *parts)
 
 
 def feed_settle_kernel(who, a, b, c, d, *rest, first):
@@ -891,6 +884,7 @@
     return call(
         functools.partial(feed_settle_kernel, first=first),
         shapes,
+        us=2 * blocks,
         grid=(blocks, 2),
         in_specs=[SMEM]
         + [pl.BlockSpec((4, 96, 128), lambda j, h: (0, 0, 2 * j + h))] * 4
@@ -900,22 +894,6 @@
     )(who, *parts, *(() if first else before))
 
 
-def pair_settle_kernel(who, a, b, c, d, left, right):
-    me = who[2]
-    count = left.shape[1]
-    for k, part in enumerate((a, b, c, d)):
-        for zz in range(4):
-            rows = pl.ds(pl.multiple_of((me ^ (k * 4 + zz)) * 32, 32), 32)
-            left[rows, :] = part[zz, :, 0:count].astype(F32)
-            right[rows, :] = part[zz, :, count:].astype(F32)
-
-
-def pair_settle(who, parts, half):
-    count = parts[0].shape[2] // 2
-    shape = sds((half, count), F32)
-    return call(pair_settle_kernel, (shape, shape), in_specs=[SMEM] + [VMEM] * 4)(who, *parts)
-
-
 def added(*terms):
     total = terms[0].astype(F32)
     for term in terms[1:]:
@@ -932,22 +910,67 @@
     return lax.ppermute(v, "fsdp", [(0, 1), (1, 0)])
 
 
-def spread(piece):
-    first = cross(piece)
-    second = swap(first, 2)
-    return (first, swap(first, 1), second, swap(second, 1))
-
-
-def reduced(keep, send):
+def tied(v, *after):
+    return lax.optimization_barrier((v,) + after)[0]
+
+
+def fenced(go, *jobs):
+    work = lambda: tuple(job() for job in jobs)
+    shapes = jax.eval_shape(work)
+    blank = lambda: jax.tree.map(lambda a: jnp.zeros(a.shape, a.dtype), shapes)
+    return lax.cond(go, work, blank)
+
+
+class Chain:
+    def __init__(self, keep, got):
+        self.keep = keep
+        self.got = got
+
+    def to_y(self, now):
+        return added(self.keep[0, 1], self.got[0, 1], tied(self.over, now)[1])
+
+    def here(self, k, side):
+        return self.keep[0, 0, k], self.got[0, 0, k], self.over[0, k], side[k]
+
+    def to_near(self, now):
+        side = tied(self.side, now)
+        odd = slice(1, 4, 2)
+        return added(*self.here(odd, side))
+
+    def to_far(self, now):
+        return added(*self.here(2, self.side), tied(self.near, now)[1])
+
+    def to_line(self, now):
+        side = tied(self.side, now)
+        return [added(*self.here(k, side)) for k in range(1, 4)]
+
+    def own_of_line(self, now):
+        deep = tied(self.deep[0], now)
+        self.own = added(*self.here(0, self.side), deep, *self.deep[1:])
+        return self.own
+
+    def own_of_far(self, now):
+        self.own = added(*self.here(0, self.side), self.near[0], tied(self.far, now))
+        return self.own
+
+    def back_near(self, now):
+        self.pair = jnp.stack([self.own, tied(self.far, now)])
+        return self.pair
+
+    def back_y(self, now):
+        near = tied(self.near, now)
+        self.line = jnp.stack([self.pair[0], near[0], self.pair[1], near[1]])
+        return self.line
+
+    def back_y_of_line(self, now):
+        deep = tied(self.deep[0], now)
+        self.line = jnp.stack([self.own, deep, *self.deep[1:]])
+        return self.line
+
+
+def over_core(keep, send):
     got = swap(send, 1)
-    over = cross(added(keep[1], got[1]))
-    side = swap(added(keep[0, 1], got[0, 1], over[1]), 2)
-    parts = [added(keep[0, 0, j], got[0, 0, j], over[0, j], side[j]) for j in range(4)]
-    deep = [swap(parts[j], 4 * j) for j in range(1, 4)]
-    own = added(parts[0], *deep)
-    line = jnp.stack([own] + [swap(own, 4 * j) for j in range(1, 4)])
-    beside = swap(line, 2)
-    return (line, beside, swap(line, 1), swap(beside, 1))
+    return got, added(keep[1], got[1])
 
 
 def natural(keep, send):
@@ -1073,51 +1096,39 @@
         return lax.dynamic_slice_in_dim(a, k * quarter, quarter, 0)
 
     if paired:
-        small_own = packed(squeeze, expand, mixer_gain, feed_gain, forget_bias, head_gain)
-        small_other = cross(small_own)
-        small = jnp.concatenate(
-            [jnp.where(x == 0, small_own, small_other), jnp.where(x == 0, small_other, small_own)],
-            axis=1,
+        return paired_device(
+            who, x, q, mcol, mrow, inputs, cotangent, query_map, key_map, value_map, swish_map,
+            readout, gate_map, up_map, down_map,
+            packed(squeeze, expand, mixer_gain, feed_gain, forget_bias, head_gain),
+            starts, counts,
         )
-        share = lambda maps: spread(jnp.concatenate([quarter_rows(a, q) for a in maps], axis=1))
-        qkv_pieces = share((query_map, key_map, value_map))
-        gate_pieces = share((swish_map, readout))
-        feed_pieces = [
-            spread(pack_feed(who, gate_map, up_map, down_map, s, n))
-            for s, n in zip(starts, counts)
-        ]
-    else:
-        small = jnp.concatenate([small_half(0), small_half(1)], axis=1)
-        lower = lambda a: a[: a.shape[0] // 2]
-        upper = lambda a: a[a.shape[0] // 2 :]
-        share = lambda maps: tuple(
-            jnp.concatenate([quarter_rows(upper(a), k) for a in maps], axis=1) for k in range(4)
+    small = jnp.concatenate([small_half(0), small_half(1)], axis=1)
+    lower = lambda a: a[: a.shape[0] // 2]
+    upper = lambda a: a[a.shape[0] // 2 :]
+    share = lambda maps: tuple(
+        jnp.concatenate([quarter_rows(upper(a), k) for a in maps], axis=1) for k in range(4)
+    )
+    kv_pieces = share((key_map, value_map))
+    gate_pieces = share((query_map, swish_map))
+    read_pieces = share((readout,))
+    others = (upper(gate_map), upper(up_map), upper(down_map))
+    feed_pieces = [
+        tuple(
+            pack_feed(jnp.full((3,), k, jnp.int32), *others, s, n) for k in range(4)
         )
-        qkv_pieces = share((query_map, key_map, value_map))
-        gate_pieces = share((swish_map, readout))
-        others = (upper(gate_map), upper(up_map), upper(down_map))
-        feed_pieces = [
-            tuple(
-                pack_feed(jnp.full((3,), k, jnp.int32), *others, s, n) for k in range(4)
-            )
-            for s, n in zip(starts, counts)
-        ]
-        query_map, key_map, value_map, swish_map, readout, gate_map, up_map, down_map = [
-            lower(a)
-            for a in (query_map, key_map, value_map, swish_map, readout, gate_map, up_map, down_map)
-        ]
-
-    normed, qkv, pre, narrow = project(
-        who, inputs, small, query_map, key_map, value_map, qkv_pieces
-    )
-    local, passing = local_state(qkv, pre, mcol, mrow)
-    if paired:
-        payload = lax.ppermute(local, "fsdp", [(0, 1)])
-    else:
-        payload = chained(local, passing, marks[:1])
-    swish = swish_project(who, normed, swish_map, gate_pieces)
+        for s, n in zip(starts, counts)
+    ]
+    query_map, key_map, value_map, swish_map, readout, gate_map, up_map, down_map = [
+        lower(a)
+        for a in (query_map, key_map, value_map, swish_map, readout, gate_map, up_map, down_map)
+    ]
+
+    normed, kv, pre, narrow = project(who, inputs, small, key_map, value_map, kv_pieces)
+    local, passing = local_state(kv, pre, mcol, mrow)
+    payload = chained(local, passing, marks[:1])
+    queries, swish = swish_project(who, normed, query_map, swish_map, gate_pieces)
     mixed, states, gated, hidden, second = mixer(
-        who, inputs, small, qkv, pre, swish, mcol, mrow, payload, readout, gate_pieces
+        who, inputs, small, queries, kv, pre, swish, mcol, mrow, payload, readout, read_pieces
     )
 
     totals = None
@@ -1130,42 +1141,20 @@
     output = (hidden + totals[0]).astype(BF16)
 
     d_hidden, low, d_swish, d_mixed, rows, back = mixer_back(
-        who, small, totals[1], hidden, cotangent, swish, mixed, qkv, pre, mcol, payload,
-        readout, gate_pieces,
-    )
-    if paired:
-        entering = lax.ppermute(back, "fsdp", [(1, 0)])
-    else:
-        linked = marks[0] == payload[HEADS * DV, 0].astype(F32)
-        entering = chained_back(back, passing, linked)
+        who, small, totals[1], hidden, cotangent, swish, mixed, queries, pre, mcol, payload,
+        readout, read_pieces,
+    )
+    linked = marks[0] == payload[HEADS * DV, 0].astype(F32)
+    entering = chained_back(back, passing, linked)
     gate_grad = gate_grads(who, normed, d_swish, gated, low)
     d_qkv, d_pre, d_narrow, bias_row = recurrence_back(
-        small, qkv, pre, d_mixed, mcol, mrow, payload, states, entering
-    )
-    pair_grad = pair_grads(who, normed, d_qkv)
+        small, queries, kv, pre, d_mixed, mcol, mrow, payload, states, entering
+    )
     grad_input, mixer_row = input_back(
         who, inputs, small, d_hidden, d_qkv, d_swish, d_narrow,
-        (query_map, key_map, value_map, swish_map), qkv_pieces, gate_pieces,
-    )
-    value_grad = value_grads(
-        who, normed, d_qkv, d_narrow, narrow, d_pre, rows, bias_row, mixer_row
-    )
-
-    if paired:
-        feeds = None
-        for (keep, send), s, n in zip(feed_grads, starts, counts):
-            feeds = feed_settle(who, reduced(keep, send), feeds, s, n, half, ff, d)
-        grad_gate, grad_up, grad_down = feeds
-        grad_swish, grad_readout = pair_settle(who, reduced(*gate_grad), half)
-        grad_query, grad_key = pair_settle(who, reduced(*pair_grad), half)
-        parts = reduced(*value_grad)
-        grad_value, strip = value_settle(who, parts, half)
-        return (
-            output, grad_input, strip[:, LANE_MIXER], grad_query, grad_key, grad_value, grad_swish,
-            strip[:, :16], strip[: kd // 2, LANE_EXPAND : LANE_EXPAND + 16].T,
-            strip[: kd // 2, LANE_BIAS], strip[: DV // 2, LANE_HEADS], grad_readout,
-            strip[:, LANE_FEED], grad_gate, grad_up, grad_down,
-        )
+        (query_map, key_map, value_map, swish_map), kv_pieces, gate_pieces,
+    )
+    late_grad = late_grads(who, normed, d_qkv, d_narrow, narrow, d_pre, rows, bias_row)
 
     gates, ups, downs = [], [], []
     for (keep, send), n in zip(feed_grads, counts):
@@ -1179,15 +1168,16 @@
     grad_gate, grad_up = whole(gates), whole(ups)
     grad_down = jnp.concatenate(downs, axis=1).reshape(ff, d)
     flat = lambda pair: natural(*pair).reshape(d, -1)
-    gate_flat, pair_flat, value_flat = flat(gate_grad), flat(pair_grad), flat(value_grad)
-    strip = value_flat[:, vd:]
+    gate_flat, late_flat = flat(gate_grad), flat(late_grad)
+    strip = late_flat[:, 2 * kd + vd :]
     joined = lambda lane, count: jnp.concatenate(
         [strip[:count, lane], strip[half : half + count, lane]]
     )
     part = kd // 2
     grad_expand = jnp.concatenate([strip[:part, 16:32], strip[half : half + part, 16:32]]).T
     results = (
-        joined(LANE_MIXER, half), pair_flat[:, :kd], pair_flat[:, kd:], value_flat[:, :vd],
+        mixer_row[0], late_flat[:, :kd], late_flat[:, kd : 2 * kd],
+        late_flat[:, 2 * kd : 2 * kd + vd],
         gate_flat[:, :vd], strip[:, :16], grad_expand, joined(LANE_BIAS, part),
         joined(LANE_HEADS, DV // 2), gate_flat[:, vd:], joined(LANE_FEED, half),
         grad_gate, grad_up, grad_down,
@@ -1197,20 +1187,205 @@
     )
 
 
-def value_settle_kernel(who, a, b, c, d, left, right):
-    me = who[2]
-    count = left.shape[1]
-    for k, part in enumerate((a, b, c, d)):
-        for zz in range(4):
-            rows = pl.ds(pl.multiple_of((me ^ (k * 4 + zz)) * 32, 32), 32)
-            left[rows, :] = part[zz, :, 0:count].astype(F32)
-            right[rows, :] = part[zz, :, count:].astype(F32)
-
-
-def value_settle(who, parts, half):
+def paired_device(
+    who, x, q, mcol, mrow, inputs, cotangent, query_map, key_map, value_map, swish_map,
+    readout, gate_map, up_map, down_map, small_own, starts, counts,
+):
+    t, d = inputs.shape
+    half = d // 2
+    quarter = half // 4
+    kd = HEADS * DK
+    ff = gate_map.shape[1]
+
+    def share(maps):
+        cut = lambda a: lax.dynamic_slice_in_dim(a, q * quarter, quarter, 0)
+        return jnp.concatenate([cut(a) for a in maps], axis=1)
+
+    def spread(first, *after):
+        second = swap(first, 2)
+        return (first, swap(first, 1), second, swap(second, 1))
+
+    go = x < 2
     vd = HEADS * DV
-    shapes = (sds((half, vd), F32), sds((half, 128), F32))
-    return call(value_settle_kernel, shapes, in_specs=[SMEM] + [VMEM] * 4)(who, *parts)
+
+    def together(*values):
+        return lax.optimization_barrier(values)
+
+    def core_step(grads, *after):
+        keep, send = grads
+        ((got, out),) = fenced(tied(go, *after), lambda: over_core(keep, send))
+        return Chain(keep, got), out
+
+    small_other = cross(small_own)
+    kv_share = share((key_map, value_map))
+    kv_first = cross(kv_share)
+    gate_share = share((tied(query_map, kv_share), swish_map))
+    read_share = share((tied(readout, kv_share),))
+    feed_shares = [
+        pack_feed(tied(who, gate_share, read_share), gate_map, up_map, down_map, s, n)
+        for s, n in zip(starts, counts)
+    ]
+    kv_first, small_other, gate_share, read_share, *feed_shares = together(
+        kv_first, small_other, gate_share, read_share, *feed_shares
+    )
+    kv_second, kv_third = swap(kv_first, 2), swap(kv_first, 1)
+    gate_first = cross(gate_share)
+    small = jnp.concatenate(
+        [jnp.where(x == 0, small_own, small_other), jnp.where(x == 0, small_other, small_own)],
+        axis=1,
+    )
+    gate_first, kv_second = together(gate_first, kv_second)
+    kv_pieces = (kv_first, kv_third, kv_second, swap(kv_second, 1))
+    gate_second, gate_third = swap(gate_first, 2), swap(gate_first, 1)
+    read_first = cross(tied(read_share, gate_first))
+    f0_first = cross(tied(feed_shares[0], gate_first))
+    normed, kv, pre, narrow = project(
+        tied(who, gate_first), inputs, small, key_map, value_map, kv_pieces
+    )
+    gate_second, read_first, normed = together(gate_second, read_first, normed)
+    gate_fourth = swap(gate_second, 1)
+    gate_pieces = (gate_first, gate_third, gate_second, gate_fourth)
+    read_second, read_third = swap(read_first, 2), swap(read_first, 1)
+    local, _ = local_state(kv, pre, mcol, tied(mrow, normed))
+    payload, (queries, swish) = fenced(
+        tied(go, local, gate_fourth, read_third),
+        lambda: lax.ppermute(local, "fsdp", [(0, 1)]),
+        lambda: swish_project(who, normed, query_map, swish_map, gate_pieces),
+    )
+    f0_first, read_second, swish = together(f0_first, read_second, swish)
+    f0_second, f0_third = swap(f0_first, 2), swap(f0_first, 1)
+    read_pieces = (read_first, read_third, read_second, swap(read_second, 1))
+    f1_first = cross(tied(feed_shares[1], f0_first))
+    mixed, states, gated, hidden, second = mixer(
+        tied(who, swish), inputs, small, queries, kv, pre, swish, mcol, mrow, payload,
+        readout, read_pieces,
+    )
+    f0_second, f1_first, hidden = together(f0_second, f1_first, hidden)
+    f0_pieces = (f0_first, f0_third, f0_second, swap(f0_second, 1))
+    f1_second, f1_third = swap(f1_first, 2), swap(f1_first, 1)
+    f2_first = cross(tied(feed_shares[2], f1_first))
+
+    def feed_part(i, pieces, totals, *after):
+        *totals, keep, send = feed(
+            tied(who, *after), second, cotangent, gate_map, up_map, down_map, pieces, totals,
+            starts[i], counts[i],
+        )
+        return totals, (keep, send)
+
+    totals, grads = feed_part(0, f0_pieces, None, hidden, f1_first)
+    f0, out = core_step(grads, totals[0], f1_third)
+    f2_first, f1_second, out = together(f2_first, f1_second, out)
+    f0.over = cross(out)
+    f1_pieces = (f1_first, f1_third, f1_second, swap(f1_second, 1))
+    f2_second, f2_third = swap(f2_first, 2), swap(f2_first, 1)
+    totals, grads = feed_part(1, f1_pieces, totals, out)
+    f1, out = core_step(grads, totals[0], f2_second, f2_third)
+    a = f0.to_y(out)
+    a, out = together(a, out)
+    f1.over = cross(out)
+    f0.side = swap(a, 2)
+    f2_pieces = (f2_first, f2_third, f2_second, swap(tied(f2_second, a), 1))
+    totals, grads = feed_part(2, f2_pieces, totals, a)
+    a = f0.to_near(totals[0])
+    f0.near = swap(a, 4)
+    keep, send = grads
+    back_parts, (got, f2_out) = fenced(
+        tied(go, a),
+        lambda: mixer_back(
+            who, small, totals[1], hidden, cotangent, swish, mixed, queries, pre, mcol, payload,
+            readout, read_pieces,
+        ),
+        lambda: over_core(keep, send),
+    )
+    d_hidden, low, d_swish, d_mixed, rows, back = back_parts
+    f2 = Chain(keep, got)
+    a, b = f0.to_far(back), f1.to_y(back)
+    a, b, back, out = together(a, b, back, f2_out)
+    f2.over = cross(out)
+    entering = lax.ppermute(back, "fsdp", [(1, 0)])
+    f0.far = swap(a, 8)
+    f1.side = swap(b, 2)
+    keep, send = gate_grads(tied(who, a), normed, d_swish, gated, low)
+    a = f0.own_of_far(keep)
+    a, entering = together(a, entering)
+    f0.far = swap(a, 8)
+    (d_qkv, d_pre, d_narrow, bias_row), (got, g_out) = fenced(
+        tied(go, a),
+        lambda: recurrence_back(
+            small, queries, kv, pre, d_mixed, mcol, mrow, payload, states, entering
+        ),
+        lambda: over_core(keep, send),
+    )
+    g = Chain(keep, got)
+    a, b = f0.back_near(d_qkv), f1.to_near(d_qkv)
+    a, b, out = together(a, b, g_out)
+    f0.near, f1.near = swap(a, 4), swap(b, 4)
+    g.over = cross(out)
+    keep, send = late_grads(tied(who, a), normed, d_qkv, d_narrow, narrow, d_pre, rows, bias_row)
+    a, b, c = f0.back_y(keep), f1.to_far(keep), f2.to_y(keep)
+    a, b, c = together(a, b, c)
+    f0.beside, f1.far, f2.side = swap(a, 2), swap(b, 8), swap(c, 2)
+    (grad_input, mixer_row), (got, v_out) = fenced(
+        tied(go, a),
+        lambda: input_back(
+            who, inputs, small, d_hidden, d_qkv, d_swish, d_narrow,
+            (query_map, key_map, value_map, swish_map), kv_pieces, gate_pieces,
+        ),
+        lambda: over_core(keep, send),
+    )
+    v = Chain(keep, got)
+    a, b, c = f1.own_of_far(mixer_row), f2.to_near(mixer_row), g.to_y(mixer_row)
+    f0_beside, a, b, c, out, mixer_row = together(f0.beside, a, b, c, v_out, mixer_row)
+    v.over = cross(out)
+    f1.far, f2.near, g.side = swap(a, 8), swap(b, 4), swap(c, 2)
+    f0_parts = (f0.line, f0_beside, swap(f0.line, 1), swap(f0_beside, 1))
+    mixer_half = jnp.where(x == 0, mixer_row[:, :half], mixer_row[:, half:])
+    mixer_half = mixer_half + cross(jnp.where(x == 0, mixer_row[:, half:], mixer_row[:, :half]))
+    output = (tied(hidden, b) + totals[0]).astype(BF16)
+    feeds = feed_settle(tied(who, output), f0_parts, None, starts[0], counts[0], half, ff, d)
+    a, b, c = f1.back_near(feeds[0]), f2.to_far(feeds[0]), g.to_near(feeds[0])
+    a, b, c, mixer_half = together(a, b, c, mixer_half)
+    f1.near, f2.far, g.near = swap(a, 4), swap(b, 8), swap(c, 4)
+    mixer_half = mixer_half + swap(mixer_half, 1)
+    a, b, c, e = f1.back_y(a), f2.own_of_far(a), g.to_far(a), v.to_y(a)
+    a, b, c, e, mixer_half = together(a, b, c, e, mixer_half)
+    f1.beside, f2.far, g.far, v.side = swap(a, 2), swap(b, 8), swap(c, 8), swap(e, 2)
+    mixer_half = mixer_half + swap(mixer_half, 2)
+    a, b, c = f2.back_near(a), g.own_of_far(a), v.to_near(a)
+    f1_beside, a, b, c, mixer_half = together(f1.beside, a, b, c, mixer_half)
+    f2.near, g.far, v.near = swap(a, 4), swap(b, 8), swap(c, 4)
+    f1_parts = (f1.line, f1_beside, swap(f1.line, 1), swap(f1_beside, 1))
+    a, b, c = f2.back_y(a), g.back_near(a), v.to_far(a)
+    a, b, c, mixer_half = together(a, b, c, mixer_half)
+    f2.beside, g.near, v.far = swap(a, 2), swap(b, 4), swap(c, 8)
+    feeds = feed_settle(tied(who, a), f1_parts, feeds, starts[1], counts[1], half, ff, d)
+    b, c = g.back_y(feeds[0]), v.own_of_far(feeds[0])
+    f2_beside, b, c, mixer_half = together(f2.beside, b, c, mixer_half)
+    f2_parts = (f2.line, f2_beside, swap(f2.line, 1), swap(f2_beside, 1))
+    g.beside, v.far = swap(b, 2), swap(c, 8)
+    mixer_half = mixer_half + swap(mixer_half, 4)
+    c = v.back_near(c)
+    g_beside, c, mixer_half = together(g.beside, c, mixer_half)
+    v.near = swap(c, 4)
+    g_parts = (g.line, g_beside, swap(g.line, 1), swap(g_beside, 1))
+    feeds = feed_settle(tied(who, c), f2_parts, feeds, starts[2], counts[2], half, ff, d)
+    c = v.back_y(feeds[0])
+    c, mixer_half = together(c, mixer_half)
+    v.beside = swap(c, 2)
+    mixer_half = mixer_half + swap(mixer_half, 8)
+    grad_swish, grad_readout = settle(tied(who, c), g_parts, half, (vd, vd))
+    v_beside = tied(v.beside, grad_swish)
+    v_parts = (v.line, v_beside, swap(v.line, 1), swap(v_beside, 1))
+    grad_query, grad_key, grad_value, strip = settle(
+        tied(who, grad_swish), v_parts, half, (kd, kd, vd, 128)
+    )
+    grad_gate, grad_up, grad_down = feeds
+    return (
+        output, grad_input, mixer_half[0], grad_query, grad_key, grad_value, grad_swish,
+        strip[:, :16], strip[: kd // 2, LANE_EXPAND : LANE_EXPAND + 16].T,
+        strip[: kd // 2, LANE_BIAS], strip[: DV // 2, LANE_HEADS], grad_readout,
+        strip[:, LANE_FEED], grad_gate, grad_up, grad_down,
+    )
 
 
 def chunk_blocks(halves):

time: 647 us -> 468 us (0.72)
  waiting for transfers between devices: 309 us -> 136 us
  starting transfers between devices: 111 us -> 68.8 us
  other arithmetic: 18.8 us -> 54.9 us
  local copies, waits for them, and re-layouts: 18 us -> 29.1 us
  Pallas kernels: 181 us -> 170 us
    ppermute x12 -> x13, waiting for transfers between devices: 138 us -> 17.9 us  [cross(): return lax.ppermute(v, 'fsdp', [(0, 1), (1, 0)])]
    ppermute x81 -> x67, starting transfers between devices: 94.4 us -> 50.1 us  [swap(): return lax.ppermute(v, 'replica', [(i, i ^ bit) for i in range(count)])]
    ppermute x81 -> x67, waiting for transfers between devices: 159 us -> 118 us  [swap(): return lax.ppermute(v, 'replica', [(i, i ^ bit) for i in range(count)])]
    convert_element_type x24 -> x25, other arithmetic: 15.1 us -> 48.3 us  [added(): return total.astype(BF16)]
    ppermute x2, waiting for transfers between devices: 11.8 us -> 0.01 us  [the longest x1 0.01 us: paired_device(): lax.ppermute(local, 'fsdp', [(0, 1)])]
    pallas_call x9 -> x7, Pallas kernels: 46.4 us -> 42 us  [the longest x3 21.3 us: feed_settle(): call(functools.partial(feed_settle_kernel, first=first), shapes, us=2 * b...]
    ppermute x12 -> x13, starting transfers between devices: 11.8 us -> 14.1 us  [cross(): return lax.ppermute(v, 'fsdp', [(0, 1), (1, 0)])]
  transfers between devices with their start and end apart: 95 -> 82, of which waited for: 32 -> 35; matrix products, arithmetic and copies ran while one was open for 5% -> 11% of each run, Pallas kernels for 20% -> 36%
where the time goes in v2:
time: 468 us; the launch traced here: 461 us
  Pallas kernels  170 us (36%)
  waiting for transfers between devices  136 us (29%)
  starting transfers between devices  68.8 us (15%)
  other arithmetic  54.9 us (12%)
  local copies, waits for them, and re-layouts  29.1 us (6%)
    ppermute x67, waiting for transfers between devices, swap(): return lax.ppermute(v, 'replica', [(i, i ^ bit) for i in range(count)])  118 us
    pallas_call x3, Pallas kernels, feed(): call(functools.partial(feed_kernel, first=first, blocks=blocks), (sds((t,...  50.7 us
    ppermute x67, starting transfers between devices, swap(): return lax.ppermute(v, 'replica', [(i, i ^ bit) for i in range(count)])  50.1 us
    convert_element_type x25, other arithmetic, added(): return total.astype(BF16)  48.3 us
    pallas_call x3, Pallas kernels, feed_settle(): call(functools.partial(feed_settle_kernel, first=first), shapes, us=2 * b...  21.3 us
    ppermute x13, waiting for transfers between devices, cross(): return lax.ppermute(v, 'fsdp', [(0, 1), (1, 0)])  17.9 us
    pallas_call x1, Pallas kernels, input_back(): call(input_back_kernel, (sds((t, d), BF16), sds((8, d), F32)), grid=(wn +...  15.1 us
    ppermute x13, starting transfers between devices, cross(): return lax.ppermute(v, 'fsdp', [(0, 1), (1, 0)])  14.1 us
  transfers between devices with their start and end apart: 82, of which 35 were waited for; matrix products, arithmetic and copies ran while one was open for 11% of the time, Pallas kernels for 36%

profile of v2, /device:TPU:0, one launch (start us, length us, event | category | flops | bytes accessed | tf_op | source)
XLA Modules:
  0.0 460.8 jit_solution(5548226251051222718)
XLA Ops:
  26.6 7.2 %collective-permute-done.8 = bf16[128,1536]{1,0:T(8,128)(2,1)} collective-permute-done((bf16[128,1536]{1,0:T(8,128)(2,1)S(1)}, bf16[128,1536]{1,0:T(8,128)(2,1)}, u32[]{:S(2)}, u32[]{:S(2)}) %collective-permute-start.8) | collective-permute-done | bytes 393248 | tf_op jit(solution)/shard_map/ppermute | solution.py:910
  39.5 7.5 %shard_map.291 = (bf16[512,1024]{1,0:T(8,128)(2,1)}, bf16[512,1536]{1,0:T(8,128)(2,1)S(1)}, f32[512,512]{1,0:T(8,128)S(1)}, bf16[512,16]{1,0:T(8,128)(2,1)}) custom-call(s32[3]{0:T(128)S(1)} %pad_add_fusion.who, bf16[512,1024]{1,0:T(8,128)(2,1)} %x.9, bf16[48,1024]{1,0:T(8,128)(2,1)S(1)} %pad_maximum_fusion.12.small, bf16[512,512]{1,0:T(8,128)(2,1)S(1)} %copy-done.10, ...), custom_call_target="tpu_custom_call" | custom-call | flops 50000000 | bytes 180000 | tf_op jit(solution)/shard_map/pallas_call | solution.py:187
  54.3 10.0 %conditional.6 = (bf16[1040,128]{1,0:T(8,128)(2,1)}, bf16[512,512]{1,0:T(8,128)(2,1)}, f32[512,1024]{1,0:T(8,128)S(1)}) conditional(s32[]{:T(128)} %convert_element_type.603, () %tuple.145, (bf16[1040,128]{1,0:T(8,128)(2,1)}, s32[3]{0:T(128)S(1)}, bf16[512,1024]{1,0:T(8,128)(2,1)}, bf16[512,512]{1,0:T(8,128)(2,1)}, bf16[512,1024]{1,0:T(8,128)(2,1)}, ...), branch_computations={%region_0.1_spmd, %region_1.2_spmd} | conditional | flops 50000000 | bytes 2887712 | solution.py:921
  57.6 6.7 %branch_1_fun.4 = (bf16[512,512]{1,0:T(8,128)(2,1)}, f32[512,1024]{1,0:T(8,128)S(1)}) custom-call(s32[3]{0:T(128)S(1)} %get-tuple-element.129.who, bf16[512,1024]{1,0:T(8,128)(2,1)} %get-tuple-element.130.normed, bf16[512,512]{1,0:T(8,128)(2,1)} %get-tuple-element.131.q_own, bf16[512,1024]{1,0:T(8,128)(2,1)} %get-tuple-element.132.s_own, ...), custom_call_target="tpu_custom_call" | custom-call | flops 50000000 | bytes 180000 | tf_op jit(solution)/shard_map/cond/branch_1_fun/pallas_call | solution.py:233
  68.0 10.5 %shard_map.293 = (f32[512,1024]{1,0:T(8,128)}, bf16[4,4,256,128]{3,2,1,0:T(8,128)(2,1)}, bf16[512,1024]{1,0:T(8,128)(2,1)}, f32[512,1024]{1,0:T(8,128)}, bf16[512,1024]{1,0:T(8,128)(2,1)}) custom-call(s32[3]{0:T(128)S(1)} %pad_add_fusion.who, bf16[512,1024]{1,0:T(8,128)(2,1)} %x.9, bf16[48,1024]{1,0:T(8,128)(2,1)S(1)} %pad_maximum_fusion.12.small, ...), custom_call_target="tpu_custom_call" | custom-call | flops 110000000 | bytes 396000 | tf_op jit(solution)/shard_map/pallas_call | solution.py:355
  89.4 13.7 %shard_map.294 = (f32[512,1024]{1,0:T(8,128)}, f32[512,1024]{1,0:T(8,128)}, bf16[2,2,4,96,768]{4,3,2,1,0:T(8,128)(2,1)}, bf16[2,2,4,96,768]{4,3,2,1,0:T(8,128)(2,1)}) custom-call(s32[3]{0:T(128)S(1)} %pad_add_fusion.who, bf16[512,1024]{1,0:T(8,128)(2,1)} %get-tuple-element.450.second, bf16[512,1024]{1,0:T(8,128)(2,1)S(1)} %copy-done, bf16[512,2816]{1,0:T(8,128)(2,1)} %g1.11, ...), custom_call_target="tpu_custom_call" | custom-call | flops 145000000 | bytes 522000 | tf_op jit(solution)/shard_map/pallas_call | solution.py:434
  103.2 7.9 %conditional.7 = (bf16[2,2,4,96,768]{4,3,2,1,0:T(8,128)(2,1)}, bf16[2,4,96,768]{3,2,1,0:T(8,128)(2,1)}) conditional(s32[]{:T(128)} %convert_element_type.605, () %tuple.153, (bf16[2,2,4,96,768]{4,3,2,1,0:T(8,128)(2,1)}, bf16[2,2,4,96,768]{4,3,2,1,0:T(8,128)(2,1)}) %tuple.154), branch_computations={%region_2.3_spmd, %region_3.4_spmd} | conditional | flops 2359296 | bytes 12976184 | solution.py:921
  117.0 18.5 %shard_map.295 = (f32[512,1024]{1,0:T(8,128)}, f32[512,1024]{1,0:T(8,128)}, bf16[2,2,4,96,1024]{4,3,2,1,0:T(8,128)(2,1)}, bf16[2,2,4,96,1024]{4,3,2,1,0:T(8,128)(2,1)}) custom-call(s32[3]{0:T(128)S(1)} %pad_add_fusion.who, bf16[512,1024]{1,0:T(8,128)(2,1)} %get-tuple-element.450.second, bf16[512,1024]{1,0:T(8,128)(2,1)} %cot.5, bf16[512,2816]{1,0:T(8,128)(2,1)} %g1.11, ...), custom_call_target="tpu_custom_call" | custom-call | flops 190000000 | bytes 684000 | tf_op jit(solution)/shard_map/pallas_call | solution.py:434
  135.6 9.9 %conditional.8 = (bf16[2,2,4,96,1024]{4,3,2,1,0:T(8,128)(2,1)}, bf16[2,4,96,1024]{3,2,1,0:T(8,128)(2,1)}) conditional(s32[]{:T(128)} %convert_element_type.611, () %tuple.159, (bf16[2,2,4,96,1024]{4,3,2,1,0:T(8,128)(2,1)}, bf16[2,2,4,96,1024]{4,3,2,1,0:T(8,128)(2,1)}) %tuple.160), branch_computations={%region_4.5_spmd, %region_5.6_spmd} | conditional | flops 3145728 | bytes 17301560 | solution.py:921
  135.8 5.9 %collective-permute-done.2 = bf16[2,2,4,96,1024]{4,3,2,1,0:T(8,128)(2,1)} collective-permute-done((bf16[2,2,4,96,1024]{4,3,2,1,0:T(8,128)(2,1)}, bf16[2,2,4,96,1024]{4,3,2,1,0:T(8,128)(2,1)}, u32[]{:S(2)}, u32[]{:S(2)}) %collective-permute-start.2) | collective-permute-done | bytes 3145760 | tf_op jit(solution)/shard_map/cond/branch_1_fun/ppermute | solution.py:906
  150.7 18.4 %shard_map.296 = (f32[512,1024]{1,0:T(8,128)}, f32[512,1024]{1,0:T(8,128)}, bf16[2,2,4,96,1024]{4,3,2,1,0:T(8,128)(2,1)}, bf16[2,2,4,96,1024]{4,3,2,1,0:T(8,128)(2,1)}) custom-call(s32[3]{0:T(128)S(1)} %pad_add_fusion.who, bf16[512,1024]{1,0:T(8,128)(2,1)} %get-tuple-element.450.second, bf16[512,1024]{1,0:T(8,128)(2,1)S(1)} %copy-done.1, ...), custom_call_target="tpu_custom_call" | custom-call | flops 190000000 | bytes 684000 | tf_op jit(solution)/shard_map/pallas_call | solution.py:434
  173.5 14.7 %conditional.9 = (f32[512,1024]{1,0:T(8,128)}, bf16[512,1024]{1,0:T(8,128)(2,1)}, bf16[512,1024]{1,0:T(8,128)(2,1)}, bf16[512,1024]{1,0:T(8,128)(2,1)}, f32[8,10...) conditional(s32[]{:T(128)} %convert_element_type.631, ...), branch_computations={%region_6.7_spmd, %region_7.8_spmd} | conditional | flops 113145728 | bytes 30284644 | solution.py:921
  174.4 10.4 %branch_1_fun.5 = (f32[512,1024]{1,0:T(8,128)}, bf16[512,1024]{1,0:T(8,128)(2,1)}, bf16[512,1024]{1,0:T(8,128)(2,1)}, bf16[512,1024]{1,0:T(8,128)(2,1)}, f32[8,1024]{1,0:T(8,128)}, /*index=5*/bf16[1024,128]{1,0:T(8,128)(2,1)}) custom-call(s32[3]{0:T(128)S(1)} %get-tuple-element.143.who, bf16[48,1024]{1,0:T(8,128)(2,1)S(1)} %get-tuple-element.144.small, ...), custom_call_target="tpu_custom_call" | custom-call | flops 110000000 | bytes 396000 | tf_op jit(solution)/shard_map/cond/branch_1_fun/pallas_call | solution.py:561
  200.6 8.7 %shard_map.297 = (bf16[2,2,4,32,2048]{4,3,2,1,0:T(8,128)(2,1)}, bf16[2,2,4,32,2048]{4,3,2,1,0:T(8,128)(2,1)}) custom-call(s32[3]{0:T(128)S(1)} %pad_add_fusion.who, bf16[512,1024]{1,0:T(8,128)(2,1)S(1)} %copy-done.4, bf16[512,1024]{1,0:T(8,128)(2,1)} %get-tuple-element.490.d_swish, bf16[512,1024]{1,0:T(8,128)(2,1)} %get-tuple-element.491.gated, ...), custom_call_target="tpu_custom_call" | custom-call | flops 90000000 | bytes 324000 | tf_op jit(solution)/shard_map/pallas_call | solution.py:600
  211.1 13.9 %conditional.10 = (bf16[512,2048]{1,0:T(8,128)(2,1)S(1)}, bf16[512,512]{1,0:T(8,128)(2,1)}, bf16[512,16]{1,0:T(8,128)(2,1)S(1)}, f32[8,512]{1,0:T(8,128)S(1)}, b...) conditional(s32[]{:T(128)} %convert_element_type.642, () %tuple.176, ...), branch_computations={%region_8.9_spmd, %region_9.10_spmd} | conditional | flops 112097152 | bytes 21371760 | solution.py:921
  211.9 10.4 %branch_1_fun.6 = (bf16[512,2048]{1,0:T(8,128)(2,1)S(1)}, bf16[512,512]{1,0:T(8,128)(2,1)}, bf16[512,16]{1,0:T(8,128)(2,1)S(1)}, f32[8,512]{1,0:T(8,128)S(1)}) custom-call(bf16[48,1024]{1,0:T(8,128)(2,1)S(1)} %get-tuple-element.167.small, bf16[512,512]{1,0:T(8,128)(2,1)} %get-tuple-element.168.q, bf16[512,1536]{1,0:T(8,128)(2,1)} %get-tuple-element.169.kv, ...), custom_call_target="tpu_custom_call" | custom-call | flops 110000000 | bytes 396000 | tf_op jit(solution)/shard_map/cond/branch_1_fun/pallas_call | solution.py:696
  229.8 6.2 %shard_map.298 = (bf16[2,2,4,32,2176]{4,3,2,1,0:T(8,128)(2,1)}, bf16[2,2,4,32,2176]{4,3,2,1,0:T(8,128)(2,1)}) custom-call(s32[3]{0:T(128)S(1)} %pad_add_fusion.who, bf16[512,1024]{1,0:T(8,128)(2,1)S(1)} %copy-done.5, bf16[512,2048]{1,0:T(8,128)(2,1)S(1)} %get-tuple-element.502.d_qkv, bf16[512,16]{1,0:T(8,128)(2,1)S(1)} %get-tuple-element.509.d_narrow, ...), custom_call_target="tpu_custom_call" | custom-call | flops 100000000 | bytes 360000 | tf_op jit(solution)/shard_map/pallas_call | solution.py:829
  239.3 6.2 %collective-permute-done.40 = bf16[2,96,1024]{2,1,0:T(8,128)(2,1)S(1)} collective-permute-done((bf16[2,96,1024]{2,1,0:T(8,128)(2,1)S(1)}, bf16[2,96,1024]{2,1,0:T(8,128)(2,1)S(1)}, u32[]{:S(2)}, u32[]{:S(2)}) %collective-permute-start.40) | collective-permute-done | bytes 393248 | tf_op jit(solution)/shard_map/ppermute | solution.py:906
  253.9 18.2 %conditional.11 = (bf16[512,1024]{1,0:T(8,128)(2,1)}, f32[8,1024]{1,0:T(8,128)S(1)}, bf16[2,2,4,32,2176]{4,3,2,1,0:T(8,128)(2,1)}, bf16[2,4,32,2176]{3,2,1,0:T(8,128)(2,1)}) conditional(s32[]{:T(128)} %convert_element_type.671, () %tuple.187, (s32[3]{0:T(128)S(1)}, bf16[512,1024]{1,0:T(8,128)(2,1)S(1)}, bf16[48,1024]{1,0:T(8,128)(2,1)S(1)}, ...), branch_computations={%region_10.11_spmd, %region_11.12_spmd} | conditional | flops 152228224 | bytes 21708228 | solution.py:921
  254.4 15.1 %branch_1_fun.7 = (bf16[512,1024]{1,0:T(8,128)(2,1)}, f32[8,1024]{1,0:T(8,128)S(1)}) custom-call(s32[3]{0:T(128)S(1)} %get-tuple-element.183.who, bf16[512,1024]{1,0:T(8,128)(2,1)S(1)} %get-tuple-element.184.x, bf16[48,1024]{1,0:T(8,128)(2,1)S(1)} %get-tuple-element.185.small, f32[512,1024]{1,0:T(8,128)} %get-tuple-element.186.d_hidden, ...), custom_call_target="tpu_custom_call" | custom-call | flops 150000000 | bytes 540000 | tf_op jit(solution)/shard_map/cond/branch_1_fun/pallas_call | solution.py:769
  278.6 9.0 %collective-permute-done.42.b = bf16[4,96,768]{2,1,0:T(8,128)(2,1)S(1)} collective-permute-done((bf16[4,96,768]{2,1,0:T(8,128)(2,1)}, bf16[4,96,768]{2,1,0:T(8,128)(2,1)S(1)}, u32[]{:S(2)}, u32[]{:S(2)}) %collective-permute-start.42) | collective-permute-done | bytes 589856 | tf_op jit(solution)/shard_map/ppermute | solution.py:906
  293.0 5.9 %shard_map.299 = (f32[512,2816]{1,0:T(8,128)}, f32[512,2816]{1,0:T(8,128)}, f32[1408,1024]{1,0:T(8,128)}) custom-call(s32[3]{0:T(128)S(1)} %pad_add_fusion.who, bf16[4,96,768]{2,1,0:T(8,128)(2,1)} %pad_maximum_fusion.2.a, bf16[4,96,768]{2,1,0:T(8,128)(2,1)} %copy-done.34, bf16[4,96,768]{2,1,0:T(8,128)(2,1)} %collective-permute-done.48.c, ...), custom_call_target="tpu_custom_call" | custom-call | flops 60000000 | bytes 216000 | tf_op jit(solution)/shard_map/pallas_call | solution.py:884
  309.6 7.9 %collective-permute-done.54 = bf16[96,1024]{1,0:T(8,128)(2,1)S(1)} collective-permute-done((bf16[96,1024]{1,0:T(8,128)(2,1)S(1)}, bf16[96,1024]{1,0:T(8,128)(2,1)S(1)}, u32[]{:S(2)}, u32[]{:S(2)}) %collective-permute-start.54) | collective-permute-done | bytes 196640 | tf_op jit(solution)/shard_map/ppermute | solution.py:906
  321.9 6.8 %collective-permute-done.53 = bf16[2,96,1024]{2,1,0:T(8,128)(2,1)S(1)} collective-permute-done((bf16[2,96,1024]{2,1,0:T(8,128)(2,1)S(1)}, bf16[2,96,1024]{2,1,0:T(8,128)(2,1)S(1)}, u32[]{:S(2)}, u32[]{:S(2)}) %collective-permute-start.53) | collective-permute-done | bytes 393248 | tf_op jit(solution)/shard_map/ppermute | solution.py:906
  328.8 5.8 %collective-permute-done.46 = bf16[2,4,32,2176]{3,2,1,0:T(8,128)(2,1)S(1)} collective-permute-done((bf16[2,4,32,2176]{3,2,1,0:T(8,128)(2,1)}, bf16[2,4,32,2176]{3,2,1,0:T(8,128)(2,1)S(1)}, u32[]{:S(2)}, u32[]{:S(2)}) %collective-permute-start.46) | collective-permute-done | bytes 1114144 | tf_op jit(solution)/shard_map/ppermute | solution.py:910
  342.9 5.7 %collective-permute-done.60 = bf16[32,2048]{1,0:T(8,128)(2,1)S(1)} collective-permute-done((bf16[32,2048]{1,0:T(8,128)(2,1)S(1)}, bf16[32,2048]{1,0:T(8,128)(2,1)S(1)}, u32[]{:S(2)}, u32[]{:S(2)}) %collective-permute-start.60) | collective-permute-done | bytes 131104 | tf_op jit(solution)/shard_map/ppermute | solution.py:906
  357.1 13.4 %collective-permute-done.58.b = bf16[4,96,1024]{2,1,0:T(8,128)(2,1)S(1)} collective-permute-done((bf16[4,96,1024]{2,1,0:T(8,128)(2,1)S(1)}, bf16[4,96,1024]{2,1,0:T(8,128)(2,1)S(1)}, u32[]{:S(2)}, u32[]{:S(2)}) %collective-permute-start.58) | collective-permute-done | bytes 786464 | tf_op jit(solution)/shard_map/ppermute | solution.py:906
  377.4 5.3 %collective-permute-done.62 = bf16[2,32,2176]{2,1,0:T(8,128)(2,1)S(1)} collective-permute-done((bf16[2,32,2176]{2,1,0:T(8,128)(2,1)S(1)}, bf16[2,32,2176]{2,1,0:T(8,128)(2,1)S(1)}, u32[]{:S(2)}, u32[]{:S(2)}) %collective-permute-start.62) | collective-permute-done | bytes 278560 | tf_op jit(solution)/shard_map/ppermute | solution.py:906
  384.5 5.0 %collective-permute-done.63 = bf16[2,96,1024]{2,1,0:T(8,128)(2,1)S(1)} collective-permute-done((bf16[2,96,1024]{2,1,0:T(8,128)(2,1)S(1)}, bf16[2,96,1024]{2,1,0:T(8,128)(2,1)S(1)}, u32[]{:S(2)}, u32[]{:S(2)}) %collective-permute-start.63) | collective-permute-done | bytes 393248 | tf_op jit(solution)/shard_map/ppermute | solution.py:906
  393.1 7.7 %shard_map.300 = (f32[512,2816]{1,0:T(8,128)}, f32[512,2816]{1,0:T(8,128)}, f32[1408,1024]{1,0:T(8,128)}) custom-call(s32[3]{0:T(128)S(1)} %copy-done.50, bf16[4,96,1024]{2,1,0:T(8,128)(2,1)} %copy-done.7, bf16[4,96,1024]{2,1,0:T(8,128)(2,1)} %copy-done.23, ...), custom_call_target="tpu_custom_call", output_to_operand_aliasing={{0}: (5, {}), {1}: (6, {}), {2}: (7, {})} | custom-call | flops 80000000 | bytes 288000 | tf_op jit(solution)/shard_map/pallas_call | solution.py:884
  402.3 5.5 %collective-permute-done.68.b = bf16[4,96,1024]{2,1,0:T(8,128)(2,1)S(1)} collective-permute-done((bf16[4,96,1024]{2,1,0:T(8,128)(2,1)S(1)}, bf16[4,96,1024]{2,1,0:T(8,128)(2,1)S(1)}, u32[]{:S(2)}, u32[]{:S(2)}) %collective-permute-start.68) | collective-permute-done | bytes 786464 | tf_op jit(solution)/shard_map/ppermute | solution.py:906
  421.8 7.7 %shard_map.301 = (f32[512,2816]{1,0:T(8,128)}, f32[512,2816]{1,0:T(8,128)}, f32[1408,1024]{1,0:T(8,128)}) custom-call(s32[3]{0:T(128)S(1)} %copy-done.51, bf16[4,96,1024]{2,1,0:T(8,128)(2,1)} %copy-done.8, bf16[4,96,1024]{2,1,0:T(8,128)(2,1)} %copy-done.24, ...), custom_call_target="tpu_custom_call", output_to_operand_aliasing={{0}: (5, {}), {1}: (6, {}), {2}: (7, {})} | custom-call | flops 80000000 | bytes 288000 | tf_op jit(solution)/shard_map/pallas_call | solution.py:884
  (342 shorter events, 227.8 us)
Async XLA Ops:
  4.2 18.8 %collective-permute-start.7 = (bf16[48,512]{1,0:T(8,128)(2,1)S(1)}, bf16[48,512]{1,0:T(8,128)(2,1)S(1)}, u32[]{:S(2)}, u32[]{:S(2)}) collective-permute-start(bf16[48,512]{1,0:T(8,128)(2,1)S(1)} %pad.14), channel_id=1, source_target_pairs={{0,1},{1,0},{2,3},{3,2},{4,5},{5,4},{6,7},{7,6},{8,9},{9,8},{10,11... | collective-permute-start | bytes 147464 | tf_op jit(solution)/shard_map/ppermute | solution.py:910
  37.1 27.2 %collective-permute-start.10 = (bf16[128,2304]{1,0:T(8,128)(2,1)}, bf16[128,2304]{1,0:T(8,128)(2,1)}, u32[]{:S(2)}, u32[]{:S(2)}) collective-permute-start(bf16[128,2304]{1,0:T(8,128)(2,1)} %shard_map.288), channel_id=1, source_target_pairs={{0,1},{1,0},{2,3},{3,2},{4,5},{5,4},{6,7},{7,6},{8,9},{9,8},{10,11... | collective-permute-start | bytes 1769480 | tf_op jit(solution)/shard_map/ppermute | solution.py:910
  47.6 16.7 %collective-permute-start.15 = (bf16[128,1024]{1,0:T(8,128)(2,1)S(1)}, bf16[128,1024]{1,0:T(8,128)(2,1)}, u32[]{:S(2)}, u32[]{:S(2)}) collective-permute-start(bf16[128,1024]{1,0:T(8,128)(2,1)S(1)} %collective-permute-done.12.r0), channel_id=1, source_target_pairs={{0,4},{2,6},{4,0},{6,2},{8,12},{10,14},{12,8},{14,10},{16,20},{18,... | collective-permute-start | bytes 786440 | tf_op jit(solution)/shard_map/ppermute | solution.py:906
  64.3 19.8 %collective-permute-start.20 = (bf16[128,3072]{1,0:T(8,128)(2,1)}, bf16[128,3072]{1,0:T(8,128)(2,1)}, u32[]{:S(2)}, u32[]{:S(2)}) collective-permute-start(bf16[128,3072]{1,0:T(8,128)(2,1)} %shard_map.289), channel_id=1, source_target_pairs={{0,1},{1,0},{2,3},{3,2},{4,5},{5,4},{6,7},{7,6},{8,9},{9,8},{10,11... | collective-permute-start | bytes 2359304 | tf_op jit(solution)/shard_map/ppermute | solution.py:910
  84.1 19.1 %collective-permute-start.24 = (bf16[128,3072]{1,0:T(8,128)(2,1)}, bf16[128,3072]{1,0:T(8,128)(2,1)}, u32[]{:S(2)}, u32[]{:S(2)}) collective-permute-start(bf16[128,3072]{1,0:T(8,128)(2,1)} %collective-permute-done.20.r0), channel_id=1, source_target_pairs={{0,2},{2,0},{4,6},{6,4},{8,10},{10,8},{12,14},{14,12},{16,18},{18,... | collective-permute-start | bytes 2359304 | tf_op jit(solution)/shard_map/ppermute | solution.py:906
  84.1 27.0 %collective-permute-start.25 = (bf16[128,3072]{1,0:T(8,128)(2,1)}, bf16[128,3072]{1,0:T(8,128)(2,1)}, u32[]{:S(2)}, u32[]{:S(2)}) collective-permute-start(bf16[128,3072]{1,0:T(8,128)(2,1)} %shard_map.290), channel_id=1, source_target_pairs={{0,1},{1,0},{2,3},{3,2},{4,5},{5,4},{6,7},{7,6},{8,9},{9,8},{10,11... | collective-permute-start | bytes 2359304 | tf_op jit(solution)/shard_map/ppermute | solution.py:910
  84.8 26.3 %collective-permute-start.26 = (bf16[128,3072]{1,0:T(8,128)(2,1)}, bf16[128,3072]{1,0:T(8,128)(2,1)}, u32[]{:S(2)}, u32[]{:S(2)}) collective-permute-start(bf16[128,3072]{1,0:T(8,128)(2,1)} %collective-permute-done.20.r0), channel_id=1, source_target_pairs={{0,4},{2,6},{4,0},{6,2},{8,12},{10,14},{12,8},{14,10},{16,20},{18,... | collective-permute-start | bytes 2359304 | tf_op jit(solution)/shard_map/ppermute | solution.py:906
  111.1 34.5 %collective-permute-start.27 = (bf16[2,4,96,768]{3,2,1,0:T(8,128)(2,1)}, bf16[2,4,96,768]{3,2,1,0:T(8,128)(2,1)}, u32[]{:S(2)}, u32[]{:S(2)}) collective-permute-start(bf16[2,4,96,768]{3,2,1,0:T(8,128)(2,1)} %get-tuple-element.460), channel_id=1, source_target_pairs={{0,1},{1,0},{2,3},{3,2},{4,5},{5,4},{6,7},{7,6},{8,9},{9,8},{10,11... | collective-permute-start | bytes 3538952 | tf_op jit(solution)/shard_map/ppermute | solution.py:910
  112.6 23.0 %collective-permute-start.30 = (bf16[128,3072]{1,0:T(8,128)(2,1)}, bf16[128,3072]{1,0:T(8,128)(2,1)}, u32[]{:S(2)}, u32[]{:S(2)}) collective-permute-start(bf16[128,3072]{1,0:T(8,128)(2,1)} %collective-permute-done.25.r0), channel_id=1, source_target_pairs={{0,2},{2,0},{4,6},{6,4},{8,10},{10,8},{12,14},{14,12},{16,18},{18,... | collective-permute-start | bytes 2359304 | tf_op jit(solution)/shard_map/ppermute | solution.py:906
  113.1 22.5 %collective-permute-start.29 = (bf16[128,3072]{1,0:T(8,128)(2,1)}, bf16[128,3072]{1,0:T(8,128)(2,1)}, u32[]{:S(2)}, u32[]{:S(2)}) collective-permute-start(bf16[128,3072]{1,0:T(8,128)(2,1)} %collective-permute-done.25.r0), channel_id=1, source_target_pairs={{0,4},{2,6},{4,0},{6,2},{8,12},{10,14},{12,8},{14,10},{16,20},{18,... | collective-permute-start | bytes 2359304 | tf_op jit(solution)/shard_map/ppermute | solution.py:906
  147.5 42.1 %collective-permute-start.34 = (bf16[2,4,96,1024]{3,2,1,0:T(8,128)(2,1)}, bf16[2,4,96,1024]{3,2,1,0:T(8,128)(2,1)}, u32[]{:S(2)}, u32[]{:S(2)}) collective-permute-start(bf16[2,4,96,1024]{3,2,1,0:T(8,128)(2,1)} %get-tuple-element.485), channel_id=1, source_target_pairs={{0,1},{1,0},{2,3},{3,2},{4,5},{5,4},{6,7},{7,6},{8,9},{9,8},{10,11... | collective-permute-start | bytes 4718600 | tf_op jit(solution)/shard_map/ppermute | solution.py:910
  148.1 21.1 %collective-permute-start.31 = (bf16[4,96,768]{2,1,0:T(8,128)(2,1)S(1)}, bf16[4,96,768]{2,1,0:T(8,128)(2,1)S(1)}, u32[]{:S(2)}, u32[]{:S(2)}) collective-permute-start(bf16[4,96,768]{2,1,0:T(8,128)(2,1)S(1)} %fusion.7), channel_id=1, source_target_pairs={{0,4},{2,6},{4,0},{6,2},{8,12},{10,14},{12,8},{14,10},{16,20},{18,... | collective-permute-start | bytes 1769480 | tf_op jit(solution)/shard_map/ppermute | solution.py:906
  171.9 16.3 %collective-permute-start.33 = (bf16[2,96,768]{2,1,0:T(8,128)(2,1)}, bf16[2,96,768]{2,1,0:T(8,128)(2,1)}, u32[]{:S(2)}, u32[]{:S(2)}) collective-permute-start(bf16[2,96,768]{2,1,0:T(8,128)(2,1)} %fusion.15), channel_id=1, source_target_pairs={{0,8},{2,10},{4,12},{6,14},{8,0},{10,2},{12,4},{14,6},{16,24},{18,... | collective-permute-start | bytes 884744 | tf_op jit(solution)/shard_map/ppermute | solution.py:906
  192.6 33.4 %collective-permute-start.38 = (bf16[4,96,1024]{2,1,0:T(8,128)(2,1)}, bf16[4,96,1024]{2,1,0:T(8,128)(2,1)}, u32[]{:S(2)}, u32[]{:S(2)}) collective-permute-start(bf16[4,96,1024]{2,1,0:T(8,128)(2,1)} %fusion.6), channel_id=1, source_target_pairs={{0,4},{2,6},{4,0},{6,2},{8,12},{10,14},{12,8},{14,10},{16,20},{18,... | collective-permute-start | bytes 2359304 | tf_op jit(solution)/shard_map/ppermute | solution.py:906
  197.9 49.9 %collective-permute-start.41 = (bf16[2,4,96,1024]{3,2,1,0:T(8,128)(2,1)}, bf16[2,4,96,1024]{3,2,1,0:T(8,128)(2,1)}, u32[]{:S(2)}, u32[]{:S(2)}) collective-permute-start(bf16[2,4,96,1024]{3,2,1,0:T(8,128)(2,1)} %get-tuple-element.519), channel_id=1, source_target_pairs={{0,1},{1,0},{2,3},{3,2},{4,5},{5,4},{6,7},{7,6},{8,9},{9,8},{10,11... | collective-permute-start | bytes 4718600 | tf_op jit(solution)/shard_map/ppermute | solution.py:910
  228.2 17.4 %collective-permute-start.40 = (bf16[2,96,1024]{2,1,0:T(8,128)(2,1)S(1)}, bf16[2,96,1024]{2,1,0:T(8,128)(2,1)S(1)}, u32[]{:S(2)}, u32[]{:S(2)}) collective-permute-start(bf16[2,96,1024]{2,1,0:T(8,128)(2,1)S(1)} %fusion.13), channel_id=1, source_target_pairs={{0,8},{2,10},{4,12},{6,14},{8,0},{10,2},{12,4},{14,6},{16,24},{18,... | collective-permute-start | bytes 1179656 | tf_op jit(solution)/shard_map/ppermute | solution.py:906
  229.7 45.4 %collective-permute-start.45 = (bf16[2,4,32,2048]{3,2,1,0:T(8,128)(2,1)}, bf16[2,4,32,2048]{3,2,1,0:T(8,128)(2,1)}, u32[]{:S(2)}, u32[]{:S(2)}) collective-permute-start(bf16[2,4,32,2048]{3,2,1,0:T(8,128)(2,1)} %get-tuple-element.531), channel_id=1, source_target_pairs={{0,1},{1,0},{2,3},{3,2},{4,5},{5,4},{6,7},{7,6},{8,9},{9,8},{10,11... | collective-permute-start | bytes 3145736 | tf_op jit(solution)/shard_map/ppermute | solution.py:910
  250.7 22.8 %collective-permute-start.43 = (bf16[96,1024]{1,0:T(8,128)(2,1)}, bf16[96,1024]{1,0:T(8,128)(2,1)}, u32[]{:S(2)}, u32[]{:S(2)}) collective-permute-start(bf16[96,1024]{1,0:T(8,128)(2,1)} %fusion.25), channel_id=1, source_target_pairs={{0,16},{2,18},{4,20},{6,22},{8,24},{10,26},{12,28},{14,30},{16,0},... | collective-permute-start | bytes 589832 | tf_op jit(solution)/shard_map/ppermute | solution.py:906
  253.3 23.7 %collective-permute-start.44 = (bf16[4,96,1024]{2,1,0:T(8,128)(2,1)}, bf16[4,96,1024]{2,1,0:T(8,128)(2,1)}, u32[]{:S(2)}, u32[]{:S(2)}) collective-permute-start(bf16[4,96,1024]{2,1,0:T(8,128)(2,1)} %fusion.5), channel_id=1, source_target_pairs={{0,4},{2,6},{4,0},{6,2},{8,12},{10,14},{12,8},{14,10},{16,20},{18,... | collective-permute-start | bytes 2359304 | tf_op jit(solution)/shard_map/ppermute | solution.py:906
  253.9 38.3 %collective-permute-start.48 = (bf16[4,96,768]{2,1,0:T(8,128)(2,1)}, bf16[4,96,768]{2,1,0:T(8,128)(2,1)}, u32[]{:S(2)}, u32[]{:S(2)}) collective-permute-start(bf16[4,96,768]{2,1,0:T(8,128)(2,1)} %pad_maximum_fusion.2.a), channel_id=1, source_target_pairs={{0,2},{2,0},{4,6},{6,4},{8,10},{10,8},{12,14},{14,12},{16,18},{18,... | collective-permute-start | bytes 1769480 | tf_op jit(solution)/shard_map/ppermute | solution.py:906
  253.9 15.6 %collective-permute-start.5 = (bf16[2,2,4,32,2176]{4,3,2,1,0:T(8,128)(2,1)}, bf16[2,2,4,32,2176]{4,3,2,1,0:T(8,128)(2,1)}, u32[]{:S(2)}, u32[]{:S(2)}) collective-permute-start(bf16[2,2,4,32,2176]{4,3,2,1,0:T(8,128)(2,1)} %get-tuple-element.204), channel_id=1, source_target_pairs={{0,2},{2,0},{4,6},{6,4},{8,10},{10,8},{12,14},{14,12},{16,18},{18,... | collective-permute-start | bytes 6684680 | tf_op jit(solution)/shard_map/cond/branch_1_fun/ppermute | solution.py:906
  272.1 15.5 %collective-permute-start.42 = (bf16[4,96,768]{2,1,0:T(8,128)(2,1)}, bf16[4,96,768]{2,1,0:T(8,128)(2,1)S(1)}, u32[]{:S(2)}, u32[]{:S(2)}) collective-permute-start(bf16[4,96,768]{2,1,0:T(8,128)(2,1)} %pad_maximum_fusion.2.a), channel_id=1, source_target_pairs={{0,4},{2,6},{4,0},{6,2},{8,12},{10,14},{12,8},{14,10},{16,20},{18,... | collective-permute-start | bytes 1769480 | tf_op jit(solution)/shard_map/ppermute | solution.py:906
  287.6 15.7 %collective-permute-start.50 = (bf16[2,96,1024]{2,1,0:T(8,128)(2,1)S(1)}, bf16[2,96,1024]{2,1,0:T(8,128)(2,1)S(1)}, u32[]{:S(2)}, u32[]{:S(2)}) collective-permute-start(bf16[2,96,1024]{2,1,0:T(8,128)(2,1)S(1)} %fusion.11), channel_id=1, source_target_pairs={{0,8},{2,10},{4,12},{6,14},{8,0},{10,2},{12,4},{14,6},{16,24},{18,... | collective-permute-start | bytes 1179656 | tf_op jit(solution)/shard_map/ppermute | solution.py:906
  307.4 27.2 %collective-permute-start.46 = (bf16[2,4,32,2176]{3,2,1,0:T(8,128)(2,1)}, bf16[2,4,32,2176]{3,2,1,0:T(8,128)(2,1)S(1)}, u32[]{:S(2)}, u32[]{:S(2)}) collective-permute-start(bf16[2,4,32,2176]{3,2,1,0:T(8,128)(2,1)} %get-tuple-element.538), channel_id=1, source_target_pairs={{0,1},{1,0},{2,3},{3,2},{4,5},{5,4},{6,7},{7,6},{8,9},{9,8},{10,11... | collective-permute-start | bytes 3342344 | tf_op jit(solution)/shard_map/ppermute | solution.py:910
  309.0 19.6 %collective-permute-start.53 = (bf16[2,96,1024]{2,1,0:T(8,128)(2,1)S(1)}, bf16[2,96,1024]{2,1,0:T(8,128)(2,1)S(1)}, u32[]{:S(2)}, u32[]{:S(2)}) collective-permute-start(bf16[2,96,1024]{2,1,0:T(8,128)(2,1)S(1)} %pad_maximum_fusion.7), channel_id=1, source_target_pairs={{0,8},{2,10},{4,12},{6,14},{8,0},{10,2},{12,4},{14,6},{16,24},{18,... | collective-permute-start | bytes 1179656 | tf_op jit(solution)/shard_map/ppermute | solution.py:906
  340.2 15.6 %collective-permute-start.57 = (bf16[4,32,2176]{2,1,0:T(8,128)(2,1)S(1)}, bf16[4,32,2176]{2,1,0:T(8,128)(2,1)S(1)}, u32[]{:S(2)}, u32[]{:S(2)}) collective-permute-start(bf16[4,32,2176]{2,1,0:T(8,128)(2,1)S(1)} %fusion.8), channel_id=1, source_target_pairs={{0,4},{2,6},{4,0},{6,2},{8,12},{10,14},{12,8},{14,10},{16,20},{18,... | collective-permute-start | bytes 1671176 | tf_op jit(solution)/shard_map/ppermute | solution.py:906
  340.9 29.6 %collective-permute-start.58 = (bf16[4,96,1024]{2,1,0:T(8,128)(2,1)S(1)}, bf16[4,96,1024]{2,1,0:T(8,128)(2,1)S(1)}, u32[]{:S(2)}, u32[]{:S(2)}) collective-permute-start(bf16[4,96,1024]{2,1,0:T(8,128)(2,1)S(1)} %pad_maximum_fusion.a), channel_id=1, source_target_pairs={{0,4},{2,6},{4,0},{6,2},{8,12},{10,14},{12,8},{14,10},{16,20},{18,... | collective-permute-start | bytes 2359304 | tf_op jit(solution)/shard_map/ppermute | solution.py:906
  372.5 19.5 %collective-permute-start.66 = (bf16[4,96,1024]{2,1,0:T(8,128)(2,1)S(1)}, bf16[4,96,1024]{2,1,0:T(8,128)(2,1)S(1)}, u32[]{:S(2)}, u32[]{:S(2)}) collective-permute-start(bf16[4,96,1024]{2,1,0:T(8,128)(2,1)S(1)} %pad_maximum_fusion.a), channel_id=1, source_target_pairs={{0,2},{2,0},{4,6},{6,4},{8,10},{10,8},{12,14},{14,12},{16,18},{18,... | collective-permute-start | bytes 2359304 | tf_op jit(solution)/shard_map/ppermute | solution.py:906
  372.5 17.1 %collective-permute-start.63 = (bf16[2,96,1024]{2,1,0:T(8,128)(2,1)S(1)}, bf16[2,96,1024]{2,1,0:T(8,128)(2,1)S(1)}, u32[]{:S(2)}, u32[]{:S(2)}) collective-permute-start(bf16[2,96,1024]{2,1,0:T(8,128)(2,1)S(1)} %pad_maximum_fusion.8), channel_id=1, source_target_pairs={{0,8},{2,10},{4,12},{6,14},{8,0},{10,2},{12,4},{14,6},{16,24},{18,... | collective-permute-start | bytes 1179656 | tf_op jit(solution)/shard_map/ppermute | solution.py:906
  374.1 17.8 %collective-permute-start.67 = (bf16[4,96,1024]{2,1,0:T(8,128)(2,1)S(1)}, bf16[4,96,1024]{2,1,0:T(8,128)(2,1)S(1)}, u32[]{:S(2)}, u32[]{:S(2)}) collective-permute-start(bf16[4,96,1024]{2,1,0:T(8,128)(2,1)S(1)} %collective-permute-done.58.b), channel_id=1, source_target_pairs={{0,2},{2,0},{4,6},{6,4},{8,10},{10,8},{12,14},{14,12},{16,18},{18,... | collective-permute-start | bytes 2359304 | tf_op jit(solution)/shard_map/ppermute | solution.py:906
  390.1 17.7 %collective-permute-start.68 = (bf16[4,96,1024]{2,1,0:T(8,128)(2,1)S(1)}, bf16[4,96,1024]{2,1,0:T(8,128)(2,1)S(1)}, u32[]{:S(2)}, u32[]{:S(2)}) collective-permute-start(bf16[4,96,1024]{2,1,0:T(8,128)(2,1)S(1)} %pad_maximum_fusion.1.a), channel_id=1, source_target_pairs={{0,4},{2,6},{4,0},{6,2},{8,12},{10,14},{12,8},{14,10},{16,20},{18,... | collective-permute-start | bytes 2359304 | tf_op jit(solution)/shard_map/ppermute | solution.py:906
  431.0 15.8 %collective-permute-start.80 = (bf16[4,32,2176]{2,1,0:T(8,128)(2,1)S(1)}, bf16[4,32,2176]{2,1,0:T(8,128)(2,1)S(1)}, u32[]{:S(2)}, u32[]{:S(2)}) collective-permute-start(bf16[4,32,2176]{2,1,0:T(8,128)(2,1)S(1)} %pad_maximum_fusion.3.a), channel_id=1, source_target_pairs={{0,2},{2,0},{4,6},{6,4},{8,10},{10,8},{12,14},{14,12},{16,18},{18,... | collective-permute-start | bytes 1671176 | tf_op jit(solution)/shard_map/ppermute | solution.py:906
  (105 other events, 1250.5 us)

commit v3 on v2

--- a/solution.py
+++ b/solution.py
@@ -19,7 +19,7 @@
 
 F32 = jnp.float32
 BF16 = jnp.bfloat16
-VMEM_BYTES = 56 * 1024 * 1024
+MIB = 1024 * 1024
 
 ROW_EXPAND = 16
 ROW_MIXER = 32
@@ -30,6 +30,7 @@
 LANE_FEED = 32
 LANE_BIAS = 33
 LANE_HEADS = 34
+LANE_MIXER = 35
 
 
 def nn(a, b):
@@ -54,12 +55,12 @@
     )
 
 
-def call(kernel, out_shape, us=5, **kw):
+def call(kernel, out_shape, us=5, vmem=30, **kw):
     return pl.pallas_call(
         kernel,
         out_shape=out_shape,
         cost_estimate=cost(us),
-        compiler_params=pltpu.CompilerParams(vmem_limit_bytes=VMEM_BYTES),
+        compiler_params=pltpu.CompilerParams(vmem_limit_bytes=vmem * MIB),
         **kw,
     )
 
@@ -124,11 +125,11 @@
 
 def place_rows(who_ref, full_ref, own, pieces):
     x = who_ref[0]
-    q = who_ref[1]
+    q = who_ref[1] & (len(pieces) - 1)
     half = own.shape[0]
     rows = pieces[0].shape[0]
     full_ref[pl.ds(pl.multiple_of(x * half, half), half), :] = own
-    for k in range(4):
+    for k in range(len(pieces)):
         at = (1 - x) * half + (q ^ k) * rows
         full_ref[pl.ds(pl.multiple_of(at, rows), rows), :] = pieces[k]
 
@@ -286,17 +287,15 @@
 
 
 def mixer_kernel(
-    who, x, small, q, kv, pre, swish, mcol, mrow, payload, own, r0, r1, r2, r3,
-    mixed_out, states_out, gated_out, hidden_out, second_out, full,
+    small, q, kv, pre, swish, mcol, mrow, payload, mixed_out, states_out, gated_out
 ):
-    t, d = x.shape
+    t = q.shape[0]
     kd = HEADS * DK
     ones = lower_ones(WIDE)
     causal_rows = lax.broadcasted_iota(jnp.int32, (WIDE, WIDE), 0)
     causal_cols = lax.broadcasted_iota(jnp.int32, (WIDE, WIDE), 1)
     states = [payload[h * DV : (h + 1) * DV, :].astype(F32) for h in range(HEADS)]
     before = payload[HEADS * DV :, :].astype(F32)[0:1, 0:1]
-    place_rows(who, full, own[...], [r[...] for r in (r0, r1, r2, r3)])
     for i in range(t // WIDE):
         rows = slice(i * WIDE, (i + 1) * WIDE)
         marks = mcol[rows, :]
@@ -330,7 +329,22 @@
         scale = lax.rsqrt(jnp.mean(mixed * mixed, axis=-1, keepdims=True) + HEAD_FLOOR)
         pre_gate = swish[:, c]
         gated_out[:, c] = (mixed * scale * gain * (pre_gate * sigmoid(pre_gate))).astype(BF16)
-    hidden = x[...].astype(F32) + nn(gated_out[...], full[...])
+
+
+def mixer(small, q, kv, pre, swish, mcol, mrow, payload):
+    t = q.shape[0]
+    vd = HEADS * DV
+    outs = (
+        sds((t, vd), F32),
+        sds((t // WIDE, HEADS, DV, DK), BF16),
+        sds((t, vd), BF16),
+    )
+    return call(mixer_kernel, outs, us=8)(small, q, kv, pre, swish, mcol, mrow, payload)
+
+
+def reader_kernel(who, x, small, gated, own, r0, r1, hidden_out, second_out, full):
+    place_rows(who, full, own[...], [r0[...], r1[...]])
+    hidden = x[...].astype(F32) + nn(gated[...], full[...])
     hidden_out[...] = hidden
     mean_sq = jnp.mean(hidden * hidden, axis=-1, keepdims=True)
     second_out[...] = (
@@ -338,48 +352,29 @@
     ).astype(BF16)
 
 
-def mixer(who, x, small, q, kv, pre, swish, mcol, mrow, payload, own, pieces):
+def reader(who, x, small, gated, own, pieces):
     t, d = x.shape
-    vd = HEADS * DV
-    quarter = own.shape[0] // 4
-    right = pl.BlockSpec((quarter, d), lambda i: (0, 0))
-    whole = lambda a: pl.BlockSpec(a.shape, lambda i: (0,) * a.ndim)
-    outs = (
-        sds((t, vd), F32),
-        sds((t // WIDE, HEADS, DV, DK), BF16),
-        sds((t, vd), BF16),
-        sds((t, d), F32),
-        sds((t, d), BF16),
-    )
-    ins = (x, small, q, kv, pre, swish, mcol, mrow, payload, own)
+    ins = (x, small, gated, own, *pieces)
     return call(
-        mixer_kernel,
-        outs,
-        grid=(1,),
-        in_specs=[SMEM] + [whole(a) for a in ins] + [right] * 4,
-        out_specs=tuple(whole(a) for a in outs),
-        scratch_shapes=[pltpu.VMEM((vd, d), BF16)], us=11)(who, *ins, *pieces)
+        reader_kernel,
+        (sds((t, d), F32), sds((t, d), BF16)),
+        us=3,
+        in_specs=[SMEM] + [VMEM] * len(ins),
+        scratch_shapes=[pltpu.VMEM((gated.shape[1], d), BF16)],
+    )(who, *ins)
 
 
 def feed_kernel(
-    who, second, cot, g0, g1, u0, u1, down, r0, r1, r2, r3, *rest, first, blocks
+    who, second, cot, g0, g1, u0, u1, down, r0, r1, r2, r3,
+    part_out, part_ds, keep, send, wg, wu, wd, sec_t, sg_, su_, sd_, total_out, total_ds,
 ):
-    if first:
-        total_out, total_ds, keep, send, wg, wu, wd, sec_t, cot_t, sg_, su_, sd_ = rest
-    else:
-        in_out, in_ds, total_out, total_ds, keep, send, wg, wu, wd, sec_t, cot_t, sg_, su_, sd_ = rest
     j = pl.program_id(0)
 
     @pl.when(j == 0)
     def _():
-        if first:
-            total_out[...] = jnp.zeros_like(total_out)
-            total_ds[...] = jnp.zeros_like(total_ds)
-        else:
-            total_out[...] = in_out[...]
-            total_ds[...] = in_ds[...]
+        total_out[...] = jnp.zeros_like(total_out)
+        total_ds[...] = jnp.zeros_like(total_ds)
         sec_t[...] = second[...].T
-        cot_t[...] = cot[...].T
 
     x = who[0]
     q = who[1]
@@ -418,45 +413,46 @@
     place_grads(who, keep, send, su_, 32, cols)
     place_grads(who, keep, send, sd_, 64, cols)
 
-
-def feed(who, second, cot, gate_own, up_own, down_own, pieces, totals, start, blocks):
+    @pl.when(j == pl.num_programs(0) - 1)
+    def _():
+        part_out[...] = total_out[...].astype(BF16)
+        part_ds[...] = total_ds[...].astype(BF16)
+
+
+def feed(who, second, cot, gate_own, up_own, down_own, pieces, start, blocks):
     t, d = second.shape
     half = d // 2
     ff = gate_own.shape[1]
     halves = ff // 256
-    const = lambda j: (0, 0)
-    first = totals is None
     left = pl.BlockSpec((half, 128), lambda j: (0, start + j))
     right = pl.BlockSpec((half, 128), lambda j: (0, halves + start + j))
-    full = pl.BlockSpec((t, d), const)
+    full = pl.BlockSpec((t, d), lambda j: (0, 0))
     grads = pl.BlockSpec((2, 2, 4, 96, 256), lambda j: (0, 0, 0, 0, j))
     grads_shape = sds((2, 2, 4, 96, blocks * 256), BF16)
     return call(
-        functools.partial(feed_kernel, first=first, blocks=blocks),
-        (sds((t, d), F32), sds((t, d), F32), grads_shape, grads_shape),
+        feed_kernel,
+        (sds((t, d), BF16), sds((t, d), BF16), grads_shape, grads_shape),
         us=1 + 4.5 * blocks,
+        vmem=56,
         grid=(blocks,),
         in_specs=[
             SMEM, full, full, left, right, left, right,
             pl.BlockSpec((128, d), lambda j: (start + j, 0)),
         ]
-        + [pl.BlockSpec((half // 4, 768), lambda j: (0, j))] * 4
-        + ([] if first else [full, full]),
+        + [pl.BlockSpec((half // 4, 768), lambda j: (0, j))] * 4,
         out_specs=(full, full, grads, grads),
         scratch_shapes=[
             pltpu.VMEM((d, 256), BF16),
             pltpu.VMEM((d, 256), BF16),
             pltpu.VMEM((256, d), BF16),
             pltpu.VMEM((d, t), BF16),
-            pltpu.VMEM((d, t), BF16),
             pltpu.VMEM((d, 256), BF16),
             pltpu.VMEM((d, 256), BF16),
             pltpu.VMEM((d, 256), BF16),
+            pltpu.VMEM((t, d), F32),
+            pltpu.VMEM((t, d), F32),
         ],
-    )(
-        who, second, cot, gate_own, gate_own, up_own, up_own, down_own, *pieces,
-        *(() if first else totals),
-    )
+    )(who, second, cot, gate_own, gate_own, up_own, up_own, down_own, *pieces)
 
 
 def pack_kernel(who, g0, g1, u0, u1, down, out):
@@ -490,15 +486,15 @@
 
 
 def mixer_back_kernel(
-    who, small, d_second, hidden, cot, swish, mixed, q, pre, mcol, payload,
-    own, r0, r1, r2, r3,
+    who, small, s0, s1, s2, hidden, cot, swish, mixed, q, pre, mcol, payload,
+    own, r0, r1,
     d_hidden_out, low_out, d_swish_out, d_mixed_out, rows_out, back_out, full, d_gated,
 ):
     t, d = hidden.shape
     kd = HEADS * DK
-    place_rows(who, full, own[...], [r[...] for r in (r0, r1, r2, r3)])
+    place_rows(who, full, own[...], [r0[...], r1[...]])
     values = hidden[...]
-    upstream = d_second[...]
+    upstream = s0[...].astype(F32) + s1[...].astype(F32) + s2[...].astype(F32)
     scale = lax.rsqrt(jnp.mean(values * values, axis=-1, keepdims=True) + EPSILON)
     rows_out[...] = jnp.zeros_like(rows_out)
     rows_out[0:1, :] = jnp.sum(upstream * values * scale, axis=0, keepdims=True)
@@ -546,8 +542,6 @@
 def mixer_back(who, small, d_second, hidden, cot, swish, mixed, q, pre, mcol, payload, own, pieces):
     t, d = hidden.shape
     vd = HEADS * DV
-    quarter = own.shape[0] // 4
-    right = pl.BlockSpec((quarter, d), lambda i: (0, 0))
     whole = lambda a: pl.BlockSpec(a.shape, lambda i: (0,) * len(a.shape))
     outs = (
         sds((t, d), F32),
@@ -557,14 +551,14 @@
         sds((8, d), F32),
         sds((HEADS * DV, DK), BF16),
     )
-    ins = (small, d_second, hidden, cot, swish, mixed, q, pre, mcol, payload, own)
+    ins = (small, *d_second, hidden, cot, swish, mixed, q, pre, mcol, payload, own, *pieces)
     return call(
         mixer_back_kernel,
         outs,
         grid=(1,),
-        in_specs=[SMEM] + [whole(a) for a in ins] + [right] * 4,
+        in_specs=[SMEM] + [whole(a) for a in ins],
         out_specs=tuple(whole(a) for a in outs),
-        scratch_shapes=[pltpu.VMEM((vd, d), BF16), pltpu.VMEM((t, vd), F32)], us=11)(who, *ins, *pieces)
+        scratch_shapes=[pltpu.VMEM((vd, d), BF16), pltpu.VMEM((t, vd), F32)], us=11)(who, *ins)
 
 
 def gate_grads_kernel(who, normed, d_swish, gated, low, keep, send, scratch, left_t):
@@ -790,7 +784,7 @@
 
 
 def late_grads_kernel(
-    who, normed, d_qkv, d_narrow, narrow, d_pre, rows_in, bias_in,
+    who, normed, d_qkv, d_narrow, narrow, d_pre, rows_in, bias_in, mixer_in,
     keep, send, scratch, strip, left_t, rows,
 ):
     t, d = normed.shape
@@ -804,6 +798,7 @@
         place_grads(who, keep, send, scratch, 0, c)
     rows[...] = jnp.zeros_like(rows)
     rows[LANE_FEED : LANE_FEED + 1, :] = rows_in[0:1, :]
+    rows[LANE_MIXER : LANE_MIXER + 1, :] = mixer_in[0:1, :]
     part = kd // 2
     rows[LANE_BIAS : LANE_BIAS + 1, 0:part] = bias_in[0:1, 0:part]
     rows[LANE_BIAS : LANE_BIAS + 1, half : half + part] = bias_in[0:1, part:kd]
@@ -821,11 +816,11 @@
     place_grads(who, keep, send, strip, 0, slice(n * 256, n * 256 + 128))
 
 
-def late_grads(who, normed, d_qkv, d_narrow, narrow, d_pre, rows_in, bias_in):
+def late_grads(who, normed, d_qkv, d_narrow, narrow, d_pre, rows_in, bias_in, mixer_in):
     t, d = normed.shape
     shape = sds((2, 2, 4, 32, d_qkv.shape[1] + 128), BF16)
     whole = lambda a: pl.BlockSpec(a.shape, lambda i: (0,) * len(a.shape))
-    ins = (normed, d_qkv, d_narrow, narrow, d_pre, rows_in, bias_in)
+    ins = (normed, d_qkv, d_narrow, narrow, d_pre, rows_in, bias_in, mixer_in)
     return call(
         late_grads_kernel,
         (shape, shape),
@@ -901,6 +896,12 @@
     return total.astype(BF16)
 
 
+def summed(first, *rest):
+    for term in rest:
+        first = first + term.astype(F32)
+    return first.astype(BF16)
+
+
 def swap(v, bit):
     count = lax.axis_size("replica")
     return lax.ppermute(v, "replica", [(i, i ^ bit) for i in range(count)])
@@ -921,36 +922,40 @@
     return lax.cond(go, work, blank)
 
 
-class Chain:
+class Part:
     def __init__(self, keep, got):
         self.keep = keep
         self.got = got
 
+
+class Chain:
+    def __init__(self, *parts):
+        self.parts = parts
+
+    def blocks(self, y, k, *more):
+        at, sums = 0, []
+        for part in self.parts:
+            width = part.keep.shape[-1]
+            cut = [a[..., at : at + width] for a in more]
+            sums.append(added(part.keep[0, y, k], part.got[0, y, k], part.over[y, k], *cut))
+            at += width
+        return sums[0] if len(sums) == 1 else jnp.concatenate(sums, axis=-1)
+
     def to_y(self, now):
-        return added(self.keep[0, 1], self.got[0, 1], tied(self.over, now)[1])
-
-    def here(self, k, side):
-        return self.keep[0, 0, k], self.got[0, 0, k], self.over[0, k], side[k]
+        last = self.parts[-1]
+        last.over = tied(last.over, now)
+        return self.blocks(1, slice(None))
 
     def to_near(self, now):
         side = tied(self.side, now)
         odd = slice(1, 4, 2)
-        return added(*self.here(odd, side))
+        return self.blocks(0, odd, side[odd])
 
     def to_far(self, now):
-        return added(*self.here(2, self.side), tied(self.near, now)[1])
-
-    def to_line(self, now):
-        side = tied(self.side, now)
-        return [added(*self.here(k, side)) for k in range(1, 4)]
-
-    def own_of_line(self, now):
-        deep = tied(self.deep[0], now)
-        self.own = added(*self.here(0, self.side), deep, *self.deep[1:])
-        return self.own
+        return self.blocks(0, 2, self.side[2], tied(self.near, now)[1])
 
     def own_of_far(self, now):
-        self.own = added(*self.here(0, self.side), self.near[0], tied(self.far, now))
+        self.own = self.blocks(0, 0, self.side[0], self.near[0], tied(self.far, now))
         return self.own
 
     def back_near(self, now):
@@ -962,10 +967,9 @@
         self.line = jnp.stack([self.pair[0], near[0], self.pair[1], near[1]])
         return self.line
 
-    def back_y_of_line(self, now):
-        deep = tied(self.deep[0], now)
-        self.line = jnp.stack([self.own, deep, *self.deep[1:]])
-        return self.line
+    def gathered(self, now):
+        beside = tied(self.beside, now)
+        return (self.line, beside, swap(self.line, 1), swap(beside, 1))
 
 
 def over_core(keep, send):
@@ -1110,7 +1114,7 @@
     )
     kv_pieces = share((key_map, value_map))
     gate_pieces = share((query_map, swish_map))
-    read_pieces = share((readout,))
+    read_pieces = (upper(readout)[: half // 2], upper(readout)[half // 2 :])
     others = (upper(gate_map), upper(up_map), upper(down_map))
     feed_pieces = [
         tuple(
@@ -1127,21 +1131,21 @@
     local, passing = local_state(kv, pre, mcol, mrow)
     payload = chained(local, passing, marks[:1])
     queries, swish = swish_project(who, normed, query_map, swish_map, gate_pieces)
-    mixed, states, gated, hidden, second = mixer(
-        who, inputs, small, queries, kv, pre, swish, mcol, mrow, payload, readout, read_pieces
-    )
-
-    totals = None
-    feed_grads = []
+    mixed, states, gated = mixer(small, queries, kv, pre, swish, mcol, mrow, payload)
+    hidden, second = reader(who, inputs, small, gated, readout, read_pieces)
+
+    feed_grads, out_parts, second_parts = [], [], []
     for s, n, pieces in zip(starts, counts, feed_pieces):
-        *totals, keep, send = feed(
-            who, second, cotangent, gate_map, up_map, down_map, pieces, totals, s, n
+        out_part, second_part, keep, send = feed(
+            who, second, cotangent, gate_map, up_map, down_map, pieces, s, n
         )
+        out_parts.append(out_part)
+        second_parts.append(second_part)
         feed_grads.append((keep, send))
-    output = (hidden + totals[0]).astype(BF16)
+    output = summed(hidden, *out_parts)
 
     d_hidden, low, d_swish, d_mixed, rows, back = mixer_back(
-        who, small, totals[1], hidden, cotangent, swish, mixed, queries, pre, mcol, payload,
+        who, small, second_parts, hidden, cotangent, swish, mixed, queries, pre, mcol, payload,
         readout, read_pieces,
     )
     linked = marks[0] == payload[HEADS * DV, 0].astype(F32)
@@ -1154,7 +1158,9 @@
         who, inputs, small, d_hidden, d_qkv, d_swish, d_narrow,
         (query_map, key_map, value_map, swish_map), kv_pieces, gate_pieces,
     )
-    late_grad = late_grads(who, normed, d_qkv, d_narrow, narrow, d_pre, rows, bias_row)
+    late_grad = late_grads(
+        who, normed, d_qkv, d_narrow, narrow, d_pre, rows, bias_row, mixer_row
+    )
 
     gates, ups, downs = [], [], []
     for (keep, send), n in zip(feed_grads, counts):
@@ -1176,7 +1182,7 @@
     part = kd // 2
     grad_expand = jnp.concatenate([strip[:part, 16:32], strip[half : half + part, 16:32]]).T
     results = (
-        mixer_row[0], late_flat[:, :kd], late_flat[:, kd : 2 * kd],
+        joined(LANE_MIXER, half), late_flat[:, :kd], late_flat[:, kd : 2 * kd],
         late_flat[:, 2 * kd : 2 * kd + vd],
         gate_flat[:, :vd], strip[:, :16], grad_expand, joined(LANE_BIAS, part),
         joined(LANE_HEADS, DV // 2), gate_flat[:, vd:], joined(LANE_FEED, half),
@@ -1213,20 +1219,20 @@
 
     def core_step(grads, *after):
         keep, send = grads
-        ((got, out),) = fenced(tied(go, *after), lambda: over_core(keep, send))
-        return Chain(keep, got), out
+        ((got, out),) = fenced(tied(go, send, *after), lambda: over_core(keep, send))
+        return Part(keep, got), out
 
     small_other = cross(small_own)
     kv_share = share((key_map, value_map))
     kv_first = cross(kv_share)
     gate_share = share((tied(query_map, kv_share), swish_map))
-    read_share = share((tied(readout, kv_share),))
-    feed_shares = [
-        pack_feed(tied(who, gate_share, read_share), gate_map, up_map, down_map, s, n)
-        for s, n in zip(starts, counts)
-    ]
-    kv_first, small_other, gate_share, read_share, *feed_shares = together(
-        kv_first, small_other, gate_share, read_share, *feed_shares
+    read_share = lax.dynamic_slice_in_dim(tied(readout, kv_share), (q % 2) * (half // 2), half // 2, 0)
+    def pack(i, *after):
+        return pack_feed(tied(who, *after), gate_map, up_map, down_map, starts[i], counts[i])
+
+    feed_shares = [pack(0, gate_share, read_share)]
+    kv_first, small_other, gate_share, read_share, feed_shares[0] = together(
+        kv_first, small_other, gate_share, read_share, feed_shares[0]
     )
     kv_second, kv_third = swap(kv_first, 2), swap(kv_first, 1)
     gate_first = cross(gate_share)
@@ -1234,74 +1240,81 @@
         [jnp.where(x == 0, small_own, small_other), jnp.where(x == 0, small_other, small_own)],
         axis=1,
     )
-    gate_first, kv_second = together(gate_first, kv_second)
+    feed_shares += [pack(1, kv_first), pack(2, kv_first)]
+    gate_first, kv_second, kv_third, *feed_shares = together(
+        gate_first, kv_second, kv_third, *feed_shares
+    )
     kv_pieces = (kv_first, kv_third, kv_second, swap(kv_second, 1))
     gate_second, gate_third = swap(gate_first, 2), swap(gate_first, 1)
-    read_first = cross(tied(read_share, gate_first))
     f0_first = cross(tied(feed_shares[0], gate_first))
     normed, kv, pre, narrow = project(
         tied(who, gate_first), inputs, small, key_map, value_map, kv_pieces
     )
-    gate_second, read_first, normed = together(gate_second, read_first, normed)
+    gate_second, f0_first, normed = together(gate_second, f0_first, normed)
     gate_fourth = swap(gate_second, 1)
     gate_pieces = (gate_first, gate_third, gate_second, gate_fourth)
-    read_second, read_third = swap(read_first, 2), swap(read_first, 1)
+    f0_third = swap(f0_first, 1)
+    read_first = cross(tied(read_share, f0_first))
     local, _ = local_state(kv, pre, mcol, tied(mrow, normed))
-    payload, (queries, swish) = fenced(
-        tied(go, local, gate_fourth, read_third),
+    payload, (queries, swish), f0_second = fenced(
+        tied(go, local, gate_fourth, f0_third),
         lambda: lax.ppermute(local, "fsdp", [(0, 1)]),
         lambda: swish_project(who, normed, query_map, swish_map, gate_pieces),
-    )
-    f0_first, read_second, swish = together(f0_first, read_second, swish)
-    f0_second, f0_third = swap(f0_first, 2), swap(f0_first, 1)
-    read_pieces = (read_first, read_third, read_second, swap(read_second, 1))
-    f1_first = cross(tied(feed_shares[1], f0_first))
-    mixed, states, gated, hidden, second = mixer(
-        tied(who, swish), inputs, small, queries, kv, pre, swish, mcol, mrow, payload,
-        readout, read_pieces,
-    )
-    f0_second, f1_first, hidden = together(f0_second, f1_first, hidden)
+        lambda: swap(f0_first, 2),
+    )
+    read_first, swish = together(read_first, swish)
+    read_pieces = (read_first, swap(read_first, 1))
     f0_pieces = (f0_first, f0_third, f0_second, swap(f0_second, 1))
+    f1_first = cross(tied(feed_shares[1], read_first))
+    mixed, states, gated = mixer(
+        tied(small, swish), queries, kv, pre, swish, mcol, mrow, payload
+    )
+    hidden, second = reader(tied(who, gated, f0_pieces[3]), inputs, small, gated, readout, read_pieces)
+    f1_first, hidden = together(f1_first, hidden)
     f1_second, f1_third = swap(f1_first, 2), swap(f1_first, 1)
     f2_first = cross(tied(feed_shares[2], f1_first))
 
-    def feed_part(i, pieces, totals, *after):
-        *totals, keep, send = feed(
-            tied(who, *after), second, cotangent, gate_map, up_map, down_map, pieces, totals,
-            starts[i], counts[i],
+    def feed_part(i, pieces, *after):
+        out_part, second_part, keep, send = feed(
+            tied(who, *after), second, cotangent, gate_map, up_map, down_map, pieces, starts[i],
+            counts[i],
         )
-        return totals, (keep, send)
-
-    totals, grads = feed_part(0, f0_pieces, None, hidden, f1_first)
-    f0, out = core_step(grads, totals[0], f1_third)
+        out_parts.append(out_part)
+        second_parts.append(second_part)
+        return keep, send
+
+    out_parts, second_parts = [], []
+    grads = feed_part(0, f0_pieces, hidden, f1_first)
+    part0, out = core_step(grads, f1_third)
     f2_first, f1_second, out = together(f2_first, f1_second, out)
-    f0.over = cross(out)
+    part0.over = cross(out)
     f1_pieces = (f1_first, f1_third, f1_second, swap(f1_second, 1))
     f2_second, f2_third = swap(f2_first, 2), swap(f2_first, 1)
-    totals, grads = feed_part(1, f1_pieces, totals, out)
-    f1, out = core_step(grads, totals[0], f2_second, f2_third)
+    grads = feed_part(1, f1_pieces, out)
+    part1, out = core_step(grads, f2_second, f2_third)
+    f0, f1 = Chain(part0), Chain(part1)
     a = f0.to_y(out)
     a, out = together(a, out)
-    f1.over = cross(out)
+    part1.over = cross(out)
     f0.side = swap(a, 2)
     f2_pieces = (f2_first, f2_third, f2_second, swap(tied(f2_second, a), 1))
-    totals, grads = feed_part(2, f2_pieces, totals, a)
-    a = f0.to_near(totals[0])
+    keep, send = feed_part(2, f2_pieces, a)
+    a = f0.to_near(keep)
     f0.near = swap(a, 4)
-    keep, send = grads
     back_parts, (got, f2_out) = fenced(
         tied(go, a),
         lambda: mixer_back(
-            who, small, totals[1], hidden, cotangent, swish, mixed, queries, pre, mcol, payload,
-            readout, read_pieces,
+            who, small, second_parts, hidden, cotangent, swish, mixed, queries, pre, mcol,
+            payload, readout, read_pieces,
         ),
         lambda: over_core(keep, send),
     )
     d_hidden, low, d_swish, d_mixed, rows, back = back_parts
-    f2 = Chain(keep, got)
+    part2 = Part(keep, got)
+    f2 = Chain(part2)
     a, b = f0.to_far(back), f1.to_y(back)
-    a, b, back, out = together(a, b, back, f2_out)
-    f2.over = cross(out)
+    a, b, back, f2_out = together(a, b, back, f2_out)
+    part2.over = cross(f2_out)
     entering = lax.ppermute(back, "fsdp", [(1, 0)])
     f0.far = swap(a, 8)
     f1.side = swap(b, 2)
@@ -1316,72 +1329,83 @@
         ),
         lambda: over_core(keep, send),
     )
-    g = Chain(keep, got)
+    part_g = Part(keep, got)
+    g = Chain(part_g)
     a, b = f0.back_near(d_qkv), f1.to_near(d_qkv)
-    a, b, out = together(a, b, g_out)
+    a, b, g_out = together(a, b, g_out)
+    part_g.over = cross(g_out)
     f0.near, f1.near = swap(a, 4), swap(b, 4)
-    g.over = cross(out)
-    keep, send = late_grads(tied(who, a), normed, d_qkv, d_narrow, narrow, d_pre, rows, bias_row)
-    a, b, c = f0.back_y(keep), f1.to_far(keep), f2.to_y(keep)
+    grad_input, mixer_row = input_back(
+        tied(who, a), inputs, small, d_hidden, d_qkv, d_swish, d_narrow,
+        (query_map, key_map, value_map, swish_map), kv_pieces, gate_pieces,
+    )
+    a, b, c = f0.back_y(mixer_row), f1.to_far(mixer_row), f2.to_y(mixer_row)
     a, b, c = together(a, b, c)
-    f0.beside, f1.far, f2.side = swap(a, 2), swap(b, 8), swap(c, 2)
-    (grad_input, mixer_row), (got, v_out) = fenced(
-        tied(go, a),
-        lambda: input_back(
-            who, inputs, small, d_hidden, d_qkv, d_swish, d_narrow,
-            (query_map, key_map, value_map, swish_map), kv_pieces, gate_pieces,
-        ),
-        lambda: over_core(keep, send),
-    )
-    v = Chain(keep, got)
-    a, b, c = f1.own_of_far(mixer_row), f2.to_near(mixer_row), g.to_y(mixer_row)
-    f0_beside, a, b, c, out, mixer_row = together(f0.beside, a, b, c, v_out, mixer_row)
-    v.over = cross(out)
-    f1.far, f2.near, g.side = swap(a, 8), swap(b, 4), swap(c, 2)
-    f0_parts = (f0.line, f0_beside, swap(f0.line, 1), swap(f0_beside, 1))
-    mixer_half = jnp.where(x == 0, mixer_row[:, :half], mixer_row[:, half:])
-    mixer_half = mixer_half + cross(jnp.where(x == 0, mixer_row[:, half:], mixer_row[:, :half]))
-    output = (tied(hidden, b) + totals[0]).astype(BF16)
-    feeds = feed_settle(tied(who, output), f0_parts, None, starts[0], counts[0], half, ff, d)
-    a, b, c = f1.back_near(feeds[0]), f2.to_far(feeds[0]), g.to_near(feeds[0])
-    a, b, c, mixer_half = together(a, b, c, mixer_half)
-    f1.near, f2.far, g.near = swap(a, 4), swap(b, 8), swap(c, 4)
-    mixer_half = mixer_half + swap(mixer_half, 1)
-    a, b, c, e = f1.back_y(a), f2.own_of_far(a), g.to_far(a), v.to_y(a)
-    a, b, c, e, mixer_half = together(a, b, c, e, mixer_half)
-    f1.beside, f2.far, g.far, v.side = swap(a, 2), swap(b, 8), swap(c, 8), swap(e, 2)
-    mixer_half = mixer_half + swap(mixer_half, 2)
-    a, b, c = f2.back_near(a), g.own_of_far(a), v.to_near(a)
-    f1_beside, a, b, c, mixer_half = together(f1.beside, a, b, c, mixer_half)
-    f2.near, g.far, v.near = swap(a, 4), swap(b, 8), swap(c, 4)
-    f1_parts = (f1.line, f1_beside, swap(f1.line, 1), swap(f1_beside, 1))
-    a, b, c = f2.back_y(a), g.back_near(a), v.to_far(a)
-    a, b, c, mixer_half = together(a, b, c, mixer_half)
-    f2.beside, g.near, v.far = swap(a, 2), swap(b, 4), swap(c, 8)
-    feeds = feed_settle(tied(who, a), f1_parts, feeds, starts[1], counts[1], half, ff, d)
-    b, c = g.back_y(feeds[0]), v.own_of_far(feeds[0])
-    f2_beside, b, c, mixer_half = together(f2.beside, b, c, mixer_half)
-    f2_parts = (f2.line, f2_beside, swap(f2.line, 1), swap(f2_beside, 1))
-    g.beside, v.far = swap(b, 2), swap(c, 8)
-    mixer_half = mixer_half + swap(mixer_half, 4)
-    c = v.back_near(c)
-    g_beside, c, mixer_half = together(g.beside, c, mixer_half)
-    v.near = swap(c, 4)
-    g_parts = (g.line, g_beside, swap(g.line, 1), swap(g_beside, 1))
-    feeds = feed_settle(tied(who, c), f2_parts, feeds, starts[2], counts[2], half, ff, d)
-    c = v.back_y(feeds[0])
-    c, mixer_half = together(c, mixer_half)
-    v.beside = swap(c, 2)
-    mixer_half = mixer_half + swap(mixer_half, 8)
-    grad_swish, grad_readout = settle(tied(who, c), g_parts, half, (vd, vd))
-    v_beside = tied(v.beside, grad_swish)
-    v_parts = (v.line, v_beside, swap(v.line, 1), swap(v_beside, 1))
+    f2.side, f1.far, a0 = swap(c, 2), swap(b, 8), a
+    grads = late_grads(
+        tied(who, a), normed, d_qkv, d_narrow, narrow, d_pre, rows, bias_row, mixer_row
+    )
+    a = f1.own_of_far(grads[0])
+    part_v, v_out = core_step(grads, a)
+    v = Chain(part_v)
+    a, line0, v_out = together(a, a0, v_out)
+    f1.far = swap(a, 8)
+    part_v.over = cross(v_out)
+    now = f2.to_near(v_out)
+    f2.near = swap(now, 4)
+    now = g.to_y(now)
+    g.side = swap(now, 2)
+    now = f1.back_near(now)
+    f1.near = swap(now, 4)
+    f0.beside = swap(tied(line0, now), 2)
+    now = f2.to_far(now)
+    f2.far = swap(now, 8)
+    output = summed(tied(hidden, now), *out_parts)
+    now = v.to_y(output)
+    v.side = swap(now, 2)
+    now = f2.own_of_far(now)
+    f2.far = swap(now, 8)
+    now = g.to_near(now)
+    g.near = swap(now, 4)
+    now = f1.back_y(now)
+    f1.beside = swap(now, 2)
+    f0_parts = f0.gathered(now)
+    feeds = feed_settle(tied(who, now), f0_parts, None, starts[0], counts[0], half, ff, d)
+    now = f2.back_near(feeds[0])
+    f2.near = swap(now, 4)
+    now = g.to_far(now)
+    g.far = swap(now, 8)
+    now = v.to_near(now)
+    v.near = swap(now, 4)
+    now = f2.back_y(now)
+    f2.beside = swap(now, 2)
+    now = g.own_of_far(now)
+    g.far = swap(now, 8)
+    now = v.to_far(now)
+    v.far = swap(now, 8)
+    f1_parts = f1.gathered(now)
+    now = g.back_near(now)
+    g.near = swap(now, 4)
+    now = v.own_of_far(now)
+    v.far = swap(now, 8)
+    feeds = feed_settle(tied(who, now), f1_parts, feeds, starts[1], counts[1], half, ff, d)
+    now = v.back_near(feeds[0])
+    v.near = swap(now, 4)
+    now = g.back_y(now)
+    g.beside = swap(now, 2)
+    now = v.back_y(now)
+    v.beside = swap(now, 2)
+    f2_parts = f2.gathered(now)
+    feeds = feed_settle(tied(who, now), f2_parts, feeds, starts[2], counts[2], half, ff, d)
+    g_parts = g.gathered(feeds[0])
+    v_parts = v.gathered(feeds[0])
+    grad_swish, grad_readout = settle(tied(who, feeds[0]), g_parts, half, (vd, vd))
     grad_query, grad_key, grad_value, strip = settle(
         tied(who, grad_swish), v_parts, half, (kd, kd, vd, 128)
     )
     grad_gate, grad_up, grad_down = feeds
     return (
-        output, grad_input, mixer_half[0], grad_query, grad_key, grad_value, grad_swish,
+        output, grad_input, strip[:, LANE_MIXER], grad_query, grad_key, grad_value, grad_swish,
         strip[:, :16], strip[: kd // 2, LANE_EXPAND : LANE_EXPAND + 16].T,
         strip[: kd // 2, LANE_BIAS], strip[: DV // 2, LANE_HEADS], grad_readout,
         strip[:, LANE_FEED], grad_gate, grad_up, grad_down,

time: 468 us -> 420 us (0.90)
  local copies, waits for them, and re-layouts: 29.1 us -> 15.7 us
  waiting for transfers between devices: 136 us -> 123 us
  Pallas kernels: 170 us -> 160 us
  starting transfers between devices: 68.8 us -> 59.9 us
    ppermute x67 -> x61, waiting for transfers between devices: 118 us -> 106 us  [swap(): return lax.ppermute(v, 'replica', [(i, i ^ bit) for i in range(count)])]
    ppermute x67 -> x61, starting transfers between devices: 50.1 us -> 40.7 us  [swap(): return lax.ppermute(v, 'replica', [(i, i ^ bit) for i in range(count)])]
    unnamed x102 -> x88, local copies, waits for them, and re-layouts: 13 us -> 5.18 us
    pallas_call x3, Pallas kernels: 21.3 us -> 16 us  [feed_settle(): call(functools.partial(feed_settle_kernel, first=first), shapes, us=2 * b...]
    ppermute x13 -> x12, waiting for transfers between devices: 17.9 us -> 14.9 us  [cross(): return lax.ppermute(v, 'fsdp', [(0, 1), (1, 0)])]
    pallas_call x4 -> x5, Pallas kernels: 61.2 us -> 58.9 us  [the longest x3 47.6 us: feed(): call(feed_kernel, (sds((t, d), BF16), sds((t, d), BF16), grads_shape, gra...]
    ppermute x13 -> x12, starting transfers between devices: 14.1 us -> 14.7 us  [cross(): return lax.ppermute(v, 'fsdp', [(0, 1), (1, 0)])]
  transfers between devices with their start and end apart: 82 -> 75, of which waited for: 35 -> 32; matrix products, arithmetic and copies ran while one was open for 11% -> 12% of each run, Pallas kernels for 36% -> 38%
where the time goes in v3:
time: 420 us; the launch traced here: 413 us
  Pallas kernels  160 us (38%)
  waiting for transfers between devices  123 us (29%)
  starting transfers between devices  59.9 us (14%)
  other arithmetic  53.7 us (13%)
  local copies, waits for them, and re-layouts  15.7 us (4%)
    ppermute x61, waiting for transfers between devices, swap(): return lax.ppermute(v, 'replica', [(i, i ^ bit) for i in range(count)])  106 us
    pallas_call x3, Pallas kernels, feed(): call(feed_kernel, (sds((t, d), BF16), sds((t, d), BF16), grads_shape, gra...  47.6 us
    convert_element_type x25, other arithmetic, added(): return total.astype(BF16)  46.9 us
    ppermute x61, starting transfers between devices, swap(): return lax.ppermute(v, 'replica', [(i, i ^ bit) for i in range(count)])  40.7 us
    pallas_call x3, Pallas kernels, feed_settle(): call(functools.partial(feed_settle_kernel, first=first), shapes, us=2 * b...  16 us
    ppermute x12, waiting for transfers between devices, cross(): return lax.ppermute(v, 'fsdp', [(0, 1), (1, 0)])  14.9 us
    ppermute x12, starting transfers between devices, cross(): return lax.ppermute(v, 'fsdp', [(0, 1), (1, 0)])  14.7 us
    pallas_call x1, Pallas kernels, input_back(): call(input_back_kernel, (sds((t, d), BF16), sds((8, d), F32)), grid=(wn +...  14.1 us
  transfers between devices with their start and end apart: 75, of which 32 were waited for; matrix products, arithmetic and copies ran while one was open for 12% of the time, Pallas kernels for 38%

profile of v3, /device:TPU:0, one launch (start us, length us, event | category | flops | bytes accessed | tf_op | source)
XLA Modules:
  0.0 413.2 jit_solution(13352204727561728945)
XLA Ops:
  36.0 7.2 %shard_map.291 = (bf16[512,1024]{1,0:T(8,128)(2,1)}, bf16[512,1536]{1,0:T(8,128)(2,1)}, f32[512,512]{1,0:T(8,128)}, bf16[512,16]{1,0:T(8,128)(2,1)S(1)}) custom-call(s32[3]{0:T(128)S(1)} %pad_add_fusion.who, bf16[512,1024]{1,0:T(8,128)(2,1)S(1)} %copy-done, bf16[48,1024]{1,0:T(8,128)(2,1)S(1)} %pad_maximum_fusion.12.small, bf16[512,512]{1,0:T(8,128)(2,1)S(1)} %copy-done.3, ...), custom_call_target="tpu_custom_call" | custom-call | flops 50000000 | bytes 180000 | tf_op jit(solution)/shard_map/pallas_call | solution.py:188
  53.7 15.9 %conditional.6 = (bf16[1040,128]{1,0:T(8,128)(2,1)}, bf16[512,512]{1,0:T(8,128)(2,1)}, f32[512,1024]{1,0:T(8,128)S(1)}, bf16[128,2304]{1,0:T(8,128)(2,1)}) conditional(s32[]{:T(128)} %convert_element_type.612, () %tuple.147, (bf16[1040,128]{1,0:T(8,128)(2,1)S(1)}, s32[3]{0:T(128)S(1)}, bf16[512,1024]{1,0:T(8,128)(2,1)}, ...), branch_computations={%region_0.1_spmd, %region_1.2_spmd} | conditional | flops 50000000 | bytes 3604368 | solution.py:922
  58.6 6.7 %branch_1_fun.3 = (bf16[512,512]{1,0:T(8,128)(2,1)}, f32[512,1024]{1,0:T(8,128)S(1)}) custom-call(s32[3]{0:T(128)S(1)} %get-tuple-element.93.who, bf16[512,1024]{1,0:T(8,128)(2,1)} %get-tuple-element.94.normed, bf16[512,512]{1,0:T(8,128)(2,1)S(1)} %get-tuple-element.95.q_own, bf16[512,1024]{1,0:T(8,128)(2,1)} %get-tuple-element.96.s_own, ...), custom_call_target="tpu_custom_call" | custom-call | flops 50000000 | bytes 180000 | tf_op jit(solution)/shard_map/cond/branch_1_fun/pallas_call | solution.py:234
  70.4 7.0 %shard_map.293 = (f32[512,1024]{1,0:T(8,128)}, bf16[4,4,256,128]{3,2,1,0:T(8,128)(2,1)}, bf16[512,1024]{1,0:T(8,128)(2,1)S(1)}) custom-call(bf16[48,1024]{1,0:T(8,128)(2,1)} %copy-done.19, bf16[512,512]{1,0:T(8,128)(2,1)} %get-tuple-element.369.q, bf16[512,1536]{1,0:T(8,128)(2,1)} %get-tuple-element.357.kv, f32[512,512]{1,0:T(8,128)} %get-tuple-element.358.pre, ...), custom_call_target="tpu_custom_call" | custom-call | flops 80000000 | bytes 288000 | tf_op jit(solution)/shard_map/pallas_call | solution.py:342
  82.7 6.0 %collective-permute-done.19.r0 = bf16[128,3072]{1,0:T(8,128)(2,1)} collective-permute-done((bf16[128,3072]{1,0:T(8,128)(2,1)}, bf16[128,3072]{1,0:T(8,128)(2,1)}, u32[]{:S(2)}, u32[]{:S(2)}) %collective-permute-start.19) | collective-permute-done | bytes 786464 | tf_op jit(solution)/shard_map/ppermute | solution.py:911
  90.8 13.6 %shard_map.295 = (bf16[512,1024]{1,0:T(8,128)(2,1)}, bf16[512,1024]{1,0:T(8,128)(2,1)}, bf16[2,2,4,96,768]{4,3,2,1,0:T(8,128)(2,1)}, bf16[2,2,4,96,768]{4,3,2,1,0:T(8,128)(2,1)}) custom-call(s32[3]{0:T(128)S(1)} %pad_add_fusion.who, bf16[512,1024]{1,0:T(8,128)(2,1)} %copy-done.1, bf16[512,1024]{1,0:T(8,128)(2,1)S(1)} %copy-done.11, bf16[512,2816]{1,0:T(8,128)(2,1)} %g1.11, ...), custom_call_target="tpu_custom_call" | custom-call | flops 145000000 | bytes 522000 | tf_op jit(solution)/shard_map/pallas_call | solution.py:432
  104.3 7.9 %conditional.7 = (bf16[2,2,4,96,768]{4,3,2,1,0:T(8,128)(2,1)}, bf16[2,4,96,768]{3,2,1,0:T(8,128)(2,1)}) conditional(s32[]{:T(128)} %convert_element_type.614, () %tuple.156, (bf16[2,2,4,96,768]{4,3,2,1,0:T(8,128)(2,1)}, bf16[2,2,4,96,768]{4,3,2,1,0:T(8,128)(2,1)}) %tuple.157), branch_computations={%region_2.3_spmd, %region_3.4_spmd} | conditional | flops 2359296 | bytes 12976184 | solution.py:922
  104.4 4.9 %collective-permute-done.2 = bf16[2,2,4,96,768]{4,3,2,1,0:T(8,128)(2,1)} collective-permute-done((bf16[2,2,4,96,768]{4,3,2,1,0:T(8,128)(2,1)}, bf16[2,2,4,96,768]{4,3,2,1,0:T(8,128)(2,1)}, u32[]{:S(2)}, u32[]{:S(2)}) %collective-permute-start.2) | collective-permute-done | bytes 2359328 | tf_op jit(solution)/shard_map/cond/branch_1_fun/ppermute | solution.py:907
  118.3 17.1 %shard_map.296 = (bf16[512,1024]{1,0:T(8,128)(2,1)}, bf16[512,1024]{1,0:T(8,128)(2,1)}, bf16[2,2,4,96,1024]{4,3,2,1,0:T(8,128)(2,1)}, bf16[2,2,4,96,1024]{4,3,2,1,0:T(8,128)(2,1)}) custom-call(s32[3]{0:T(128)S(1)} %pad_add_fusion.who, bf16[512,1024]{1,0:T(8,128)(2,1)} %copy-done.1, bf16[512,1024]{1,0:T(8,128)(2,1)} %cot.5, bf16[512,2816]{1,0:T(8,128)(2,1)} %g1.11, ...), custom_call_target="tpu_custom_call" | custom-call | flops 190000000 | bytes 684000 | tf_op jit(solution)/shard_map/pallas_call | solution.py:432
  135.4 9.8 %conditional.8 = (bf16[2,2,4,96,1024]{4,3,2,1,0:T(8,128)(2,1)}, bf16[2,4,96,1024]{3,2,1,0:T(8,128)(2,1)}) conditional(s32[]{:T(128)} %convert_element_type.616, () %tuple.162, (bf16[2,2,4,96,1024]{4,3,2,1,0:T(8,128)(2,1)}, bf16[2,2,4,96,1024]{4,3,2,1,0:T(8,128)(2,1)}) %tuple.163), branch_computations={%region_4.5_spmd, %region_5.6_spmd} | conditional | flops 3145728 | bytes 17301560 | solution.py:922
  135.6 5.9 %collective-permute-done.3 = bf16[2,2,4,96,1024]{4,3,2,1,0:T(8,128)(2,1)} collective-permute-done((bf16[2,2,4,96,1024]{4,3,2,1,0:T(8,128)(2,1)}, bf16[2,2,4,96,1024]{4,3,2,1,0:T(8,128)(2,1)}, u32[]{:S(2)}, u32[]{:S(2)}) %collective-permute-start.3) | collective-permute-done | bytes 3145760 | tf_op jit(solution)/shard_map/cond/branch_1_fun/ppermute | solution.py:907
  150.4 16.9 %shard_map.297 = (bf16[512,1024]{1,0:T(8,128)(2,1)}, bf16[512,1024]{1,0:T(8,128)(2,1)}, bf16[2,2,4,96,1024]{4,3,2,1,0:T(8,128)(2,1)}, bf16[2,2,4,96,1024]{4,3,2,1,0:T(8,128)(2,1)}) custom-call(s32[3]{0:T(128)S(1)} %pad_add_fusion.who, bf16[512,1024]{1,0:T(8,128)(2,1)} %copy-done.1, bf16[512,1024]{1,0:T(8,128)(2,1)S(1)} %copy-done.12, bf16[512,2816]{1,0:T(8,128)(2,1)} %g1.11, ...), custom_call_target="tpu_custom_call" | custom-call | flops 190000000 | bytes 684000 | tf_op jit(solution)/shard_map/pallas_call | solution.py:432
  171.8 15.2 %conditional.9 = (f32[512,1024]{1,0:T(8,128)}, bf16[512,1024]{1,0:T(8,128)(2,1)}, bf16[512,1024]{1,0:T(8,128)(2,1)}, bf16[512,1024]{1,0:T(8,128)(2,1)}, f32[8,10...) conditional(s32[]{:T(128)} %convert_element_type.627, ...), branch_computations={%region_6.7_spmd, %region_7.8_spmd} | conditional | flops 113145728 | bytes 30284644 | solution.py:922
  172.0 11.7 %branch_1_fun.4 = (f32[512,1024]{1,0:T(8,128)}, bf16[512,1024]{1,0:T(8,128)(2,1)}, bf16[512,1024]{1,0:T(8,128)(2,1)}, bf16[512,1024]{1,0:T(8,128)(2,1)}, f32[8,1024]{1,0:T(8,128)}, /*index=5*/bf16[1024,128]{1,0:T(8,128)(2,1)}) custom-call(s32[3]{0:T(128)S(1)} %get-tuple-element.108.who, bf16[48,1024]{1,0:T(8,128)(2,1)} %get-tuple-element.109.small, ...), custom_call_target="tpu_custom_call" | custom-call | flops 110000000 | bytes 396000 | tf_op jit(solution)/shard_map/cond/branch_1_fun/pallas_call | solution.py:555
  199.2 7.9 %shard_map.298 = (bf16[2,2,4,32,2048]{4,3,2,1,0:T(8,128)(2,1)}, bf16[2,2,4,32,2048]{4,3,2,1,0:T(8,128)(2,1)}) custom-call(s32[3]{0:T(128)S(1)} %pad_add_fusion.who, bf16[512,1024]{1,0:T(8,128)(2,1)S(1)} %copy-done.13, bf16[512,1024]{1,0:T(8,128)(2,1)} %get-tuple-element.416.d_swish, bf16[512,1024]{1,0:T(8,128)(2,1)S(1)} %get-tuple-element.371.gated, ...), custom_call_target="tpu_custom_call" | custom-call | flops 90000000 | bytes 324000 | tf_op jit(solution)/shard_map/pallas_call | solution.py:594
  208.8 13.9 %conditional.10 = (bf16[512,2048]{1,0:T(8,128)(2,1)}, bf16[512,512]{1,0:T(8,128)(2,1)}, bf16[512,16]{1,0:T(8,128)(2,1)S(1)}, f32[8,512]{1,0:T(8,128)}, bf16[2,2,...) conditional(s32[]{:T(128)} %convert_element_type.653, () %tuple.179, ...), branch_computations={%region_8.9_spmd, %region_9.10_spmd} | conditional | flops 112097152 | bytes 20323156 | solution.py:922
  209.0 11.1 %branch_1_fun.5 = (bf16[512,2048]{1,0:T(8,128)(2,1)}, bf16[512,512]{1,0:T(8,128)(2,1)}, bf16[512,16]{1,0:T(8,128)(2,1)S(1)}, f32[8,512]{1,0:T(8,128)}) custom-call(bf16[48,1024]{1,0:T(8,128)(2,1)S(1)} %get-tuple-element.132.small, bf16[512,512]{1,0:T(8,128)(2,1)} %get-tuple-element.133.q, bf16[512,1536]{1,0:T(8,128)(2,1)} %get-tuple-element.134.kv, ...), custom_call_target="tpu_custom_call" | custom-call | flops 110000000 | bytes 396000 | tf_op jit(solution)/shard_map/cond/branch_1_fun/pallas_call | solution.py:690
  227.6 14.1 %shard_map.299 = (bf16[512,1024]{1,0:T(8,128)(2,1)}, f32[8,1024]{1,0:T(8,128)S(1)}) custom-call(s32[3]{0:T(128)S(1)} %pad_add_fusion.who, bf16[512,1024]{1,0:T(8,128)(2,1)S(1)} %copy-done, bf16[48,1024]{1,0:T(8,128)(2,1)S(1)} %copy-done.21, f32[512,1024]{1,0:T(8,128)} %get-tuple-element.434.d_hidden, bf16[512,2048]{1,0:T(8,128)(2,1)} %get-tuple-element.427.d_qkv, ...), custom_call_target="tpu_custom_call" | custom-call | flops 150000000 | bytes 540000 | tf_op jit(solution)/shard_map/pallas_call | solution.py:763
  252.2 4.9 %shard_map.300 = (bf16[2,2,4,32,2176]{4,3,2,1,0:T(8,128)(2,1)S(1)}, bf16[2,2,4,32,2176]{4,3,2,1,0:T(8,128)(2,1)}) custom-call(s32[3]{0:T(128)S(1)} %pad_add_fusion.who, bf16[512,1024]{1,0:T(8,128)(2,1)S(1)} %copy-done.14, bf16[512,2048]{1,0:T(8,128)(2,1)S(1)} %copy-done.10, bf16[512,16]{1,0:T(8,128)(2,1)S(1)} %copy-done.31, ...), custom_call_target="tpu_custom_call" | custom-call | flops 100000000 | bytes 360000 | tf_op jit(solution)/shard_map/pallas_call | solution.py:824
  262.7 7.2 %conditional.11 = (bf16[2,2,4,32,2176]{4,3,2,1,0:T(8,128)(2,1)}, bf16[2,4,32,2176]{3,2,1,0:T(8,128)(2,1)}) conditional(s32[]{:T(128)} %convert_element_type.692, () %tuple.192, (bf16[2,2,4,32,2176]{4,3,2,1,0:T(8,128)(2,1)}, bf16[2,2,4,32,2176]{4,3,2,1,0:T(8,128)(2,1)S(1)}) %tuple.193), branch_computations={%region_10.11_spmd, %region_11.12_spmd} | conditional | flops 2228224 | bytes 12255288 | solution.py:922
  262.7 4.7 %collective-permute-done.6 = bf16[2,2,4,32,2176]{4,3,2,1,0:T(8,128)(2,1)} collective-permute-done((bf16[2,2,4,32,2176]{4,3,2,1,0:T(8,128)(2,1)}, bf16[2,2,4,32,2176]{4,3,2,1,0:T(8,128)(2,1)}, u32[]{:S(2)}, u32[]{:S(2)}) %collective-permute-start.6) | collective-permute-done | bytes 2228256 | tf_op jit(solution)/shard_map/cond/branch_1_fun/ppermute | solution.py:907
  282.4 8.3 %collective-permute-done.42 = bf16[2,96,1024]{2,1,0:T(8,128)(2,1)S(1)} collective-permute-done((bf16[2,96,1024]{2,1,0:T(8,128)(2,1)S(1)}, bf16[2,96,1024]{2,1,0:T(8,128)(2,1)S(1)}, u32[]{:S(2)}, u32[]{:S(2)}) %collective-permute-start.42) | collective-permute-done | bytes 393248 | tf_op jit(solution)/shard_map/ppermute | solution.py:907
  301.9 7.0 %collective-permute-done.48 = bf16[96,1024]{1,0:T(8,128)(2,1)S(1)} collective-permute-done((bf16[96,1024]{1,0:T(8,128)(2,1)S(1)}, bf16[96,1024]{1,0:T(8,128)(2,1)S(1)}, u32[]{:S(2)}, u32[]{:S(2)}) %collective-permute-start.48) | collective-permute-done | bytes 196640 | tf_op jit(solution)/shard_map/ppermute | solution.py:907
  317.1 4.4 %shard_map.301 = (f32[512,2816]{1,0:T(8,128)}, f32[512,2816]{1,0:T(8,128)}, f32[1408,1024]{1,0:T(8,128)}) custom-call(s32[3]{0:T(128)S(1)} %pad_add_fusion.who, bf16[4,96,768]{2,1,0:T(8,128)(2,1)S(1)} %pad_maximum_fusion.2.a, bf16[4,96,768]{2,1,0:T(8,128)(2,1)S(1)} %collective-permute-done.52.b, bf16[4,96,768]{2,1,0:T(8,128)(2,1)S(1)} %collective-permute-done.53.c, ...), custom_call_target="tpu_custom_call" | custom-call | flops 60000000 | bytes 216000 | tf_op jit(solution)/shard_map/pallas_call | solution.py:879
  331.7 7.5 %collective-permute-done.57 = bf16[2,96,1024]{2,1,0:T(8,128)(2,1)S(1)} collective-permute-done((bf16[2,96,1024]{2,1,0:T(8,128)(2,1)S(1)}, bf16[2,96,1024]{2,1,0:T(8,128)(2,1)S(1)}, u32[]{:S(2)}, u32[]{:S(2)}) %collective-permute-start.57) | collective-permute-done | bytes 393248 | tf_op jit(solution)/shard_map/ppermute | solution.py:907
  341.2 4.4 %collective-permute-done.55 = bf16[2,32,2176]{2,1,0:T(8,128)(2,1)S(1)} collective-permute-done((bf16[2,32,2176]{2,1,0:T(8,128)(2,1)S(1)}, bf16[2,32,2176]{2,1,0:T(8,128)(2,1)S(1)}, u32[]{:S(2)}, u32[]{:S(2)}) %collective-permute-start.55) | collective-permute-done | bytes 278560 | tf_op jit(solution)/shard_map/ppermute | solution.py:907
  347.9 6.2 %collective-permute-done.58 = bf16[32,2176]{1,0:T(8,128)(2,1)S(1)} collective-permute-done((bf16[32,2176]{1,0:T(8,128)(2,1)S(1)}, bf16[32,2176]{1,0:T(8,128)(2,1)S(1)}, u32[]{:S(2)}, u32[]{:S(2)}) %collective-permute-start.58) | collective-permute-done | bytes 139296 | tf_op jit(solution)/shard_map/ppermute | solution.py:907
  358.6 5.8 %shard_map.302 = (f32[512,2816]{1,0:T(8,128)}, f32[512,2816]{1,0:T(8,128)}, f32[1408,1024]{1,0:T(8,128)}) custom-call(s32[3]{0:T(128)S(1)} %pad_add_fusion.who, bf16[4,96,1024]{2,1,0:T(8,128)(2,1)S(1)} %pad_maximum_fusion.a, bf16[4,96,1024]{2,1,0:T(8,128)(2,1)S(1)} %collective-permute-done.61.b, ...), custom_call_target="tpu_custom_call", output_to_operand_aliasing={{0}: (5, {}), {1}: (6, {}), {2}: (7, {})} | custom-call | flops 80000000 | bytes 288000 | tf_op jit(solution)/shard_map/pallas_call | solution.py:879
  368.3 5.5 %collective-permute-done.64 = bf16[2,32,2176]{2,1,0:T(8,128)(2,1)S(1)} collective-permute-done((bf16[2,32,2176]{2,1,0:T(8,128)(2,1)S(1)}, bf16[2,32,2176]{2,1,0:T(8,128)(2,1)S(1)}, u32[]{:S(2)}, u32[]{:S(2)}) %collective-permute-start.64) | collective-permute-done | bytes 278560 | tf_op jit(solution)/shard_map/ppermute | solution.py:907
  377.5 5.8 %shard_map.303 = (f32[512,2816]{1,0:T(8,128)}, f32[512,2816]{1,0:T(8,128)}, f32[1408,1024]{1,0:T(8,128)}) custom-call(s32[3]{0:T(128)S(1)} %pad_add_fusion.who, bf16[4,96,1024]{2,1,0:T(8,128)(2,1)S(1)} %pad_maximum_fusion.1.a, bf16[4,96,1024]{2,1,0:T(8,128)(2,1)S(1)} %collective-permute-done.66.b, ...), custom_call_target="tpu_custom_call", output_to_operand_aliasing={{0}: (5, {}), {1}: (6, {}), {2}: (7, {})} | custom-call | flops 80000000 | bytes 288000 | tf_op jit(solution)/shard_map/pallas_call | solution.py:879
  383.3 7.4 %collective-permute-done.72.b = bf16[4,32,2176]{2,1,0:T(8,128)(2,1)S(1)} collective-permute-done((bf16[4,32,2176]{2,1,0:T(8,128)(2,1)S(1)}, bf16[4,32,2176]{2,1,0:T(8,128)(2,1)S(1)}, u32[]{:S(2)}, u32[]{:S(2)}) %collective-permute-start.72) | collective-permute-done | bytes 557088 | tf_op jit(solution)/shard_map/ppermute | solution.py:907
  391.1 10.3 %collective-permute-done.69.b = bf16[4,32,2048]{2,1,0:T(8,128)(2,1)S(1)} collective-permute-done((bf16[4,32,2048]{2,1,0:T(8,128)(2,1)S(1)}, bf16[4,32,2048]{2,1,0:T(8,128)(2,1)S(1)}, u32[]{:S(2)}, u32[]{:S(2)}) %collective-permute-start.69) | collective-permute-done | bytes 524320 | tf_op jit(solution)/shard_map/ppermute | solution.py:907
  (304 shorter events, 199.2 us)
Async XLA Ops:
  47.1 22.4 %collective-permute-start.15 = (bf16[256,1024]{1,0:T(8,128)(2,1)}, bf16[256,1024]{1,0:T(8,128)(2,1)}, u32[]{:S(2)}, u32[]{:S(2)}) collective-permute-start(bf16[256,1024]{1,0:T(8,128)(2,1)} %constant_dynamic-slice_fusion), channel_id=1, source_target_pairs={{0,1},{1,0},{2,3},{3,2},{4,5},{5,4},{6,7},{7,6},{8,9},{9,8},{10,11... | collective-permute-start | bytes 1572872 | tf_op jit(solution)/shard_map/ppermute | solution.py:911
  53.7 15.9 %collective-permute-start.1 = (bf16[128,2304]{1,0:T(8,128)(2,1)}, bf16[128,2304]{1,0:T(8,128)(2,1)}, u32[]{:S(2)}, u32[]{:S(2)}) collective-permute-start(bf16[128,2304]{1,0:T(8,128)(2,1)} %get-tuple-element.103), channel_id=1, source_target_pairs={{0,4},{2,6},{4,0},{6,2},{8,12},{10,14},{12,8},{14,10},{16,20},{18,... | collective-permute-start | bytes 1769480 | tf_op jit(solution)/shard_map/cond/branch_1_fun/ppermute | solution.py:907
  69.5 19.2 %collective-permute-start.19 = (bf16[128,3072]{1,0:T(8,128)(2,1)}, bf16[128,3072]{1,0:T(8,128)(2,1)}, u32[]{:S(2)}, u32[]{:S(2)}) collective-permute-start(bf16[128,3072]{1,0:T(8,128)(2,1)} %shard_map.289), channel_id=1, source_target_pairs={{0,1},{1,0},{2,3},{3,2},{4,5},{5,4},{6,7},{7,6},{8,9},{9,8},{10,11... | collective-permute-start | bytes 2359304 | tf_op jit(solution)/shard_map/ppermute | solution.py:911
  88.7 15.6 %collective-permute-start.22 = (bf16[128,3072]{1,0:T(8,128)(2,1)}, bf16[128,3072]{1,0:T(8,128)(2,1)}, u32[]{:S(2)}, u32[]{:S(2)}) collective-permute-start(bf16[128,3072]{1,0:T(8,128)(2,1)} %collective-permute-done.19.r0), channel_id=1, source_target_pairs={{0,2},{2,0},{4,6},{6,4},{8,10},{10,8},{12,14},{14,12},{16,18},{18,... | collective-permute-start | bytes 2359304 | tf_op jit(solution)/shard_map/ppermute | solution.py:907
  88.7 23.5 %collective-permute-start.23 = (bf16[128,3072]{1,0:T(8,128)(2,1)}, bf16[128,3072]{1,0:T(8,128)(2,1)}, u32[]{:S(2)}, u32[]{:S(2)}) collective-permute-start(bf16[128,3072]{1,0:T(8,128)(2,1)} %shard_map.290), channel_id=1, source_target_pairs={{0,1},{1,0},{2,3},{3,2},{4,5},{5,4},{6,7},{7,6},{8,9},{9,8},{10,11... | collective-permute-start | bytes 2359304 | tf_op jit(solution)/shard_map/ppermute | solution.py:911
  89.0 23.2 %collective-permute-start.24 = (bf16[128,3072]{1,0:T(8,128)(2,1)}, bf16[128,3072]{1,0:T(8,128)(2,1)}, u32[]{:S(2)}, u32[]{:S(2)}) collective-permute-start(bf16[128,3072]{1,0:T(8,128)(2,1)} %collective-permute-done.19.r0), channel_id=1, source_target_pairs={{0,4},{2,6},{4,0},{6,2},{8,12},{10,14},{12,8},{14,10},{16,20},{18,... | collective-permute-start | bytes 2359304 | tf_op jit(solution)/shard_map/ppermute | solution.py:907
  112.2 33.0 %collective-permute-start.25 = (bf16[2,4,96,768]{3,2,1,0:T(8,128)(2,1)}, bf16[2,4,96,768]{3,2,1,0:T(8,128)(2,1)}, u32[]{:S(2)}, u32[]{:S(2)}) collective-permute-start(bf16[2,4,96,768]{3,2,1,0:T(8,128)(2,1)} %get-tuple-element.386), channel_id=1, source_target_pairs={{0,1},{1,0},{2,3},{3,2},{4,5},{5,4},{6,7},{7,6},{8,9},{9,8},{10,11... | collective-permute-start | bytes 3538952 | tf_op jit(solution)/shard_map/ppermute | solution.py:911
  113.8 21.6 %collective-permute-start.28 = (bf16[128,3072]{1,0:T(8,128)(2,1)}, bf16[128,3072]{1,0:T(8,128)(2,1)}, u32[]{:S(2)}, u32[]{:S(2)}) collective-permute-start(bf16[128,3072]{1,0:T(8,128)(2,1)} %collective-permute-done.23.r0), channel_id=1, source_target_pairs={{0,2},{2,0},{4,6},{6,4},{8,10},{10,8},{12,14},{14,12},{16,18},{18,... | collective-permute-start | bytes 2359304 | tf_op jit(solution)/shard_map/ppermute | solution.py:907
  114.3 21.1 %collective-permute-start.27 = (bf16[128,3072]{1,0:T(8,128)(2,1)}, bf16[128,3072]{1,0:T(8,128)(2,1)}, u32[]{:S(2)}, u32[]{:S(2)}) collective-permute-start(bf16[128,3072]{1,0:T(8,128)(2,1)} %collective-permute-done.23.r0), channel_id=1, source_target_pairs={{0,4},{2,6},{4,0},{6,2},{8,12},{10,14},{12,8},{14,10},{16,20},{18,... | collective-permute-start | bytes 2359304 | tf_op jit(solution)/shard_map/ppermute | solution.py:907
  147.2 41.4 %collective-permute-start.32 = (bf16[2,4,96,1024]{3,2,1,0:T(8,128)(2,1)}, bf16[2,4,96,1024]{3,2,1,0:T(8,128)(2,1)}, u32[]{:S(2)}, u32[]{:S(2)}) collective-permute-start(bf16[2,4,96,1024]{3,2,1,0:T(8,128)(2,1)} %get-tuple-element.410), channel_id=1, source_target_pairs={{0,1},{1,0},{2,3},{3,2},{4,5},{5,4},{6,7},{7,6},{8,9},{9,8},{10,11... | collective-permute-start | bytes 4718600 | tf_op jit(solution)/shard_map/ppermute | solution.py:911
  147.7 19.7 %collective-permute-start.30 = (bf16[4,96,768]{2,1,0:T(8,128)(2,1)S(1)}, bf16[4,96,768]{2,1,0:T(8,128)(2,1)S(1)}, u32[]{:S(2)}, u32[]{:S(2)}) collective-permute-start(bf16[4,96,768]{2,1,0:T(8,128)(2,1)S(1)} %fusion.7), channel_id=1, source_target_pairs={{0,4},{2,6},{4,0},{6,2},{8,12},{10,14},{12,8},{14,10},{16,20},{18,... | collective-permute-start | bytes 1769480 | tf_op jit(solution)/shard_map/ppermute | solution.py:907
  170.2 16.8 %collective-permute-start.31 = (bf16[2,96,768]{2,1,0:T(8,128)(2,1)}, bf16[2,96,768]{2,1,0:T(8,128)(2,1)}, u32[]{:S(2)}, u32[]{:S(2)}) collective-permute-start(bf16[2,96,768]{2,1,0:T(8,128)(2,1)} %fusion.15), channel_id=1, source_target_pairs={{0,8},{2,10},{4,12},{6,14},{8,0},{10,2},{12,4},{14,6},{16,24},{18,... | collective-permute-start | bytes 884744 | tf_op jit(solution)/shard_map/ppermute | solution.py:907
  191.5 32.4 %collective-permute-start.37 = (bf16[4,96,1024]{2,1,0:T(8,128)(2,1)}, bf16[4,96,1024]{2,1,0:T(8,128)(2,1)}, u32[]{:S(2)}, u32[]{:S(2)}) collective-permute-start(bf16[4,96,1024]{2,1,0:T(8,128)(2,1)} %fusion.6), channel_id=1, source_target_pairs={{0,4},{2,6},{4,0},{6,2},{8,12},{10,14},{12,8},{14,10},{16,20},{18,... | collective-permute-start | bytes 2359304 | tf_op jit(solution)/shard_map/ppermute | solution.py:907
  195.8 49.2 %collective-permute-start.33 = (bf16[2,4,96,1024]{3,2,1,0:T(8,128)(2,1)}, bf16[2,4,96,1024]{3,2,1,0:T(8,128)(2,1)}, u32[]{:S(2)}, u32[]{:S(2)}) collective-permute-start(bf16[2,4,96,1024]{3,2,1,0:T(8,128)(2,1)} %get-tuple-element.413), channel_id=1, source_target_pairs={{0,1},{1,0},{2,3},{3,2},{4,5},{5,4},{6,7},{7,6},{8,9},{9,8},{10,11... | collective-permute-start | bytes 4718600 | tf_op jit(solution)/shard_map/ppermute | solution.py:911
  225.5 16.3 %collective-permute-start.38 = (bf16[2,96,768]{2,1,0:T(8,128)(2,1)S(1)}, bf16[2,96,768]{2,1,0:T(8,128)(2,1)S(1)}, u32[]{:S(2)}, u32[]{:S(2)}) collective-permute-start(bf16[2,96,768]{2,1,0:T(8,128)(2,1)S(1)} %pad_maximum_fusion.9), channel_id=1, source_target_pairs={{0,8},{2,10},{4,12},{6,14},{8,0},{10,2},{12,4},{14,6},{16,24},{18,... | collective-permute-start | bytes 884744 | tf_op jit(solution)/shard_map/ppermute | solution.py:907
  226.0 17.4 %collective-permute-start.39 = (bf16[2,96,1024]{2,1,0:T(8,128)(2,1)S(1)}, bf16[2,96,1024]{2,1,0:T(8,128)(2,1)S(1)}, u32[]{:S(2)}, u32[]{:S(2)}) collective-permute-start(bf16[2,96,1024]{2,1,0:T(8,128)(2,1)S(1)} %fusion.13), channel_id=1, source_target_pairs={{0,8},{2,10},{4,12},{6,14},{8,0},{10,2},{12,4},{14,6},{16,24},{18,... | collective-permute-start | bytes 1179656 | tf_op jit(solution)/shard_map/ppermute | solution.py:907
  248.0 23.7 %collective-permute-start.40 = (bf16[4,96,1024]{2,1,0:T(8,128)(2,1)}, bf16[4,96,1024]{2,1,0:T(8,128)(2,1)}, u32[]{:S(2)}, u32[]{:S(2)}) collective-permute-start(bf16[4,96,1024]{2,1,0:T(8,128)(2,1)} %fusion.5), channel_id=1, source_target_pairs={{0,4},{2,6},{4,0},{6,2},{8,12},{10,14},{12,8},{14,10},{16,20},{18,... | collective-permute-start | bytes 2359304 | tf_op jit(solution)/shard_map/ppermute | solution.py:907
  249.5 27.2 %collective-permute-start.44 = (bf16[2,4,32,2048]{3,2,1,0:T(8,128)(2,1)}, bf16[2,4,32,2048]{3,2,1,0:T(8,128)(2,1)}, u32[]{:S(2)}, u32[]{:S(2)}) collective-permute-start(bf16[2,4,32,2048]{3,2,1,0:T(8,128)(2,1)} %get-tuple-element.458), channel_id=1, source_target_pairs={{0,1},{1,0},{2,3},{3,2},{4,5},{5,4},{6,7},{7,6},{8,9},{9,8},{10,11... | collective-permute-start | bytes 3145736 | tf_op jit(solution)/shard_map/ppermute | solution.py:911
  252.1 63.4 %collective-permute-start.53 = (bf16[4,96,768]{2,1,0:T(8,128)(2,1)S(1)}, bf16[4,96,768]{2,1,0:T(8,128)(2,1)S(1)}, u32[]{:S(2)}, u32[]{:S(2)}) collective-permute-start(bf16[4,96,768]{2,1,0:T(8,128)(2,1)S(1)} %pad_maximum_fusion.2.a), channel_id=1, source_target_pairs={{0,2},{2,0},{4,6},{6,4},{8,10},{10,8},{12,14},{14,12},{16,18},{18,... | collective-permute-start | bytes 1769480 | tf_op jit(solution)/shard_map/ppermute | solution.py:907
  269.9 28.1 %collective-permute-start.45 = (bf16[2,4,32,2176]{3,2,1,0:T(8,128)(2,1)}, bf16[2,4,32,2176]{3,2,1,0:T(8,128)(2,1)S(1)}, u32[]{:S(2)}, u32[]{:S(2)}) collective-permute-start(bf16[2,4,32,2176]{3,2,1,0:T(8,128)(2,1)} %get-tuple-element.454), channel_id=1, source_target_pairs={{0,1},{1,0},{2,3},{3,2},{4,5},{5,4},{6,7},{7,6},{8,9},{9,8},{10,11... | collective-permute-start | bytes 3342344 | tf_op jit(solution)/shard_map/ppermute | solution.py:911
  273.5 17.3 %collective-permute-start.42 = (bf16[2,96,1024]{2,1,0:T(8,128)(2,1)S(1)}, bf16[2,96,1024]{2,1,0:T(8,128)(2,1)S(1)}, u32[]{:S(2)}, u32[]{:S(2)}) collective-permute-start(bf16[2,96,1024]{2,1,0:T(8,128)(2,1)S(1)} %fusion.11), channel_id=1, source_target_pairs={{0,8},{2,10},{4,12},{6,14},{8,0},{10,2},{12,4},{14,6},{16,24},{18,... | collective-permute-start | bytes 1179656 | tf_op jit(solution)/shard_map/ppermute | solution.py:907
  278.3 31.9 %collective-permute-start.47 = (bf16[4,32,2048]{2,1,0:T(8,128)(2,1)S(1)}, bf16[4,32,2048]{2,1,0:T(8,128)(2,1)S(1)}, u32[]{:S(2)}, u32[]{:S(2)}) collective-permute-start(bf16[4,32,2048]{2,1,0:T(8,128)(2,1)S(1)} %fusion.9), channel_id=1, source_target_pairs={{0,4},{2,6},{4,0},{6,2},{8,12},{10,14},{12,8},{14,10},{16,20},{18,... | collective-permute-start | bytes 1572872 | tf_op jit(solution)/shard_map/ppermute | solution.py:907
  282.3 29.2 %collective-permute-start.51 = (bf16[2,96,1024]{2,1,0:T(8,128)(2,1)S(1)}, bf16[2,96,1024]{2,1,0:T(8,128)(2,1)S(1)}, u32[]{:S(2)}, u32[]{:S(2)}) collective-permute-start(bf16[2,96,1024]{2,1,0:T(8,128)(2,1)S(1)} %pad_maximum_fusion.7), channel_id=1, source_target_pairs={{0,8},{2,10},{4,12},{6,14},{8,0},{10,2},{12,4},{14,6},{16,24},{18,... | collective-permute-start | bytes 1179656 | tf_op jit(solution)/shard_map/ppermute | solution.py:907
  290.7 21.0 %collective-permute-start.52 = (bf16[4,96,768]{2,1,0:T(8,128)(2,1)S(1)}, bf16[4,96,768]{2,1,0:T(8,128)(2,1)S(1)}, u32[]{:S(2)}, u32[]{:S(2)}) collective-permute-start(bf16[4,96,768]{2,1,0:T(8,128)(2,1)S(1)} %pad_maximum_fusion.2.a), channel_id=1, source_target_pairs={{0,4},{2,6},{4,0},{6,2},{8,12},{10,14},{12,8},{14,10},{16,20},{18,... | collective-permute-start | bytes 1769480 | tf_op jit(solution)/shard_map/ppermute | solution.py:907
  315.0 15.5 %collective-permute-start.46 = (bf16[4,32,2176]{2,1,0:T(8,128)(2,1)S(1)}, bf16[4,32,2176]{2,1,0:T(8,128)(2,1)S(1)}, u32[]{:S(2)}, u32[]{:S(2)}) collective-permute-start(bf16[4,32,2176]{2,1,0:T(8,128)(2,1)S(1)} %fusion.8), channel_id=1, source_target_pairs={{0,4},{2,6},{4,0},{6,2},{8,12},{10,14},{12,8},{14,10},{16,20},{18,... | collective-permute-start | bytes 1671176 | tf_op jit(solution)/shard_map/ppermute | solution.py:907
  315.5 40.3 %collective-permute-start.62 = (bf16[4,96,1024]{2,1,0:T(8,128)(2,1)S(1)}, bf16[4,96,1024]{2,1,0:T(8,128)(2,1)S(1)}, u32[]{:S(2)}, u32[]{:S(2)}) collective-permute-start(bf16[4,96,1024]{2,1,0:T(8,128)(2,1)S(1)} %pad_maximum_fusion.a), channel_id=1, source_target_pairs={{0,2},{2,0},{4,6},{6,4},{8,10},{10,8},{12,14},{14,12},{16,18},{18,... | collective-permute-start | bytes 2359304 | tf_op jit(solution)/shard_map/ppermute | solution.py:907
  315.5 31.2 %collective-permute-start.61 = (bf16[4,96,1024]{2,1,0:T(8,128)(2,1)S(1)}, bf16[4,96,1024]{2,1,0:T(8,128)(2,1)S(1)}, u32[]{:S(2)}, u32[]{:S(2)}) collective-permute-start(bf16[4,96,1024]{2,1,0:T(8,128)(2,1)S(1)} %pad_maximum_fusion.a), channel_id=1, source_target_pairs={{0,4},{2,6},{4,0},{6,2},{8,12},{10,14},{12,8},{14,10},{16,20},{18,... | collective-permute-start | bytes 2359304 | tf_op jit(solution)/shard_map/ppermute | solution.py:907
  355.2 22.1 %collective-permute-start.67 = (bf16[4,96,1024]{2,1,0:T(8,128)(2,1)S(1)}, bf16[4,96,1024]{2,1,0:T(8,128)(2,1)S(1)}, u32[]{:S(2)}, u32[]{:S(2)}) collective-permute-start(bf16[4,96,1024]{2,1,0:T(8,128)(2,1)S(1)} %pad_maximum_fusion.1.a), channel_id=1, source_target_pairs={{0,2},{2,0},{4,6},{6,4},{8,10},{10,8},{12,14},{14,12},{16,18},{18,... | collective-permute-start | bytes 2359304 | tf_op jit(solution)/shard_map/ppermute | solution.py:907
  355.2 20.0 %collective-permute-start.66 = (bf16[4,96,1024]{2,1,0:T(8,128)(2,1)S(1)}, bf16[4,96,1024]{2,1,0:T(8,128)(2,1)S(1)}, u32[]{:S(2)}, u32[]{:S(2)}) collective-permute-start(bf16[4,96,1024]{2,1,0:T(8,128)(2,1)S(1)} %pad_maximum_fusion.1.a), channel_id=1, source_target_pairs={{0,4},{2,6},{4,0},{6,2},{8,12},{10,14},{12,8},{14,10},{16,20},{18,... | collective-permute-start | bytes 2359304 | tf_op jit(solution)/shard_map/ppermute | solution.py:907
  375.7 25.7 %collective-permute-start.69 = (bf16[4,32,2048]{2,1,0:T(8,128)(2,1)S(1)}, bf16[4,32,2048]{2,1,0:T(8,128)(2,1)S(1)}, u32[]{:S(2)}, u32[]{:S(2)}) collective-permute-start(bf16[4,32,2048]{2,1,0:T(8,128)(2,1)S(1)} %pad_maximum_fusion.4.a), channel_id=1, source_target_pairs={{0,4},{2,6},{4,0},{6,2},{8,12},{10,14},{12,8},{14,10},{16,20},{18,... | collective-permute-start | bytes 1572872 | tf_op jit(solution)/shard_map/ppermute | solution.py:907
  377.2 29.0 %collective-permute-start.73 = (bf16[4,32,2176]{2,1,0:T(8,128)(2,1)S(1)}, bf16[4,32,2176]{2,1,0:T(8,128)(2,1)S(1)}, u32[]{:S(2)}, u32[]{:S(2)}) collective-permute-start(bf16[4,32,2176]{2,1,0:T(8,128)(2,1)S(1)} %pad_maximum_fusion.3.a), channel_id=1, source_target_pairs={{0,2},{2,0},{4,6},{6,4},{8,10},{10,8},{12,14},{14,12},{16,18},{18,... | collective-permute-start | bytes 1671176 | tf_op jit(solution)/shard_map/ppermute | solution.py:907
  390.6 15.6 %collective-permute-start.74 = (bf16[4,32,2176]{2,1,0:T(8,128)(2,1)S(1)}, bf16[4,32,2176]{2,1,0:T(8,128)(2,1)S(1)}, u32[]{:S(2)}, u32[]{:S(2)}) collective-permute-start(bf16[4,32,2176]{2,1,0:T(8,128)(2,1)S(1)} %collective-permute-done.72.b), channel_id=1, source_target_pairs={{0,2},{2,0},{4,6},{6,4},{8,10},{10,8},{12,14},{14,12},{16,18},{18,... | collective-permute-start | bytes 1671176 | tf_op jit(solution)/shard_map/ppermute | solution.py:907
  (88 other events, 842.2 us)

commit v4 on v3

--- a/solution.py
+++ b/solution.py
@@ -123,9 +123,9 @@
     return jnp.concatenate([row[:, at : at + count], row[:, half + at : half + at + count]], axis=1)
 
 
-def place_rows(who_ref, full_ref, own, pieces):
+def place_rows(who_ref, full_ref, own, pieces, number=1):
     x = who_ref[0]
-    q = who_ref[1] & (len(pieces) - 1)
+    q = who_ref[number]
     half = own.shape[0]
     rows = pieces[0].shape[0]
     full_ref[pl.ds(pl.multiple_of(x * half, half), half), :] = own
@@ -134,17 +134,30 @@
         full_ref[pl.ds(pl.multiple_of(at, rows), rows), :] = pieces[k]
 
 
-def place_grads(who_ref, keep_ref, send_ref, scratch_ref, row, cols, rows=32):
+def place_grads(who_ref, outs, scratch_ref, row, cols, rows=32):
     x = who_ref[0]
     me = who_ref[2]
     half = scratch_ref.shape[0] // 2
-    for core, out_ref in ((0, keep_ref), (1, send_ref)):
+    keep, send_own, send_over = outs
+    for core in range(2):
         for xx in range(2):
+            out = (keep.at[xx], (send_own, send_over)[xx])[core]
             for yy in range(2):
                 for zz in range(4):
                     block = me ^ (core * 8 + yy * 4 + zz)
                     at = pl.multiple_of((x ^ xx) * half + block * rows, rows)
-                    out_ref[xx, yy, zz, row : row + rows, cols] = scratch_ref[pl.ds(at, rows), :]
+                    out[yy, zz, row : row + rows, cols] = scratch_ref[pl.ds(at, rows), :]
+
+
+def grads_out(rows, width, block=None, index=None):
+    shapes = [(2, 2, 4, rows, width), (2, 4, rows, width), (2, 4, rows, width)]
+    block = block or width
+    index = index or (lambda *a: 0)
+    specs = [
+        pl.BlockSpec((*shape[:-1], block), lambda *a, n=len(shape): (0,) * (n - 1) + (index(*a),))
+        for shape in shapes
+    ]
+    return [sds(shape, BF16) for shape in shapes], specs
 
 
 def project_kernel(
@@ -165,11 +178,11 @@
 
     pieces = [r[...] for r in (r0, r1, r2, r3)]
 
-    @pl.when(j < 2)
+    @pl.when(j == 0)
     def _():
         place_rows(who, full, k_own[...], pieces)
 
-    @pl.when(j >= 2)
+    @pl.when(j >= 1)
     def _():
         place_rows(who, full, v_own[...], pieces)
 
@@ -179,31 +192,28 @@
 def project(who, x, small, k_own, v_own, pieces):
     t, d = x.shape
     half = d // 2
-    kd = HEADS * DK
-    vd = HEADS * DV
-    width = kd + vd
+    wide = HEADS * DK
+    vn = HEADS * DV // wide
     const = lambda j: (0, 0)
-    qn = kd // 256
-    vn = vd // 256
     return call(
         project_kernel,
-        (sds((t, d), BF16), sds((t, width), BF16), sds((t, kd), F32), sds((t, 16), BF16)),
-        grid=(width // 256,),
+        (sds((t, d), BF16), sds((t, (1 + vn) * wide), BF16), sds((t, wide), F32), sds((t, 16), BF16)),
+        grid=(1 + vn,),
         in_specs=[
             SMEM,
             pl.BlockSpec((t, d), const),
             pl.BlockSpec(small.shape, const),
-            pl.BlockSpec((half, 256), lambda j: (0, jnp.minimum(j, qn - 1))),
-            pl.BlockSpec((half, 256), lambda j: (0, jnp.clip(j - qn, 0, vn - 1))),
+            pl.BlockSpec((half, wide), const),
+            pl.BlockSpec((half, wide), lambda j: (0, jnp.maximum(j - 1, 0))),
         ]
-        + [pl.BlockSpec((half // 4, 256), lambda j: (0, j))] * 4,
+        + [pl.BlockSpec((half // 4, wide), lambda j: (0, j))] * 4,
         out_specs=(
             pl.BlockSpec((t, d), const),
-            pl.BlockSpec((t, 256), lambda j: (0, j)),
-            pl.BlockSpec((t, kd), const),
+            pl.BlockSpec((t, wide), lambda j: (0, j)),
+            pl.BlockSpec((t, wide), const),
             pl.BlockSpec((t, 16), const),
         ),
-        scratch_shapes=[pltpu.VMEM((d, 256), BF16)],
+        scratch_shapes=[pltpu.VMEM((d, wide), BF16)],
     )(who, x, small, k_own, v_own, *pieces)
 
 
@@ -211,12 +221,12 @@
     j = pl.program_id(0)
     pieces = [r[...] for r in (r0, r1, r2, r3)]
 
-    @pl.when(j < 2)
+    @pl.when(j == 0)
     def _():
         place_rows(who, full, q_own[...], pieces)
         queries[...] = nn(normed[...], full[...]).astype(BF16)
 
-    @pl.when(j >= 2)
+    @pl.when(j >= 1)
     def _():
         place_rows(who, full, s_own[...], pieces)
         swish[...] = nn(normed[...], full[...])
@@ -225,25 +235,23 @@
 def swish_project(who, normed, q_own, s_own, pieces):
     t, d = normed.shape
     half = d // 2
-    kd = HEADS * DK
-    vd = HEADS * DV
-    qn = kd // 256
-    vn = vd // 256
-    low = lambda j: (0, jnp.minimum(j, qn - 1))
-    high = lambda j: (0, jnp.clip(j - qn, 0, vn - 1))
+    wide = HEADS * DK
+    vn = HEADS * DV // wide
+    const = lambda j: (0, 0)
+    high = lambda j: (0, jnp.maximum(j - 1, 0))
     return call(
         swish_kernel,
-        (sds((t, kd), BF16), sds((t, vd), F32)),
-        grid=(qn + vn,),
+        (sds((t, wide), BF16), sds((t, vn * wide), F32)),
+        grid=(1 + vn,),
         in_specs=[
             SMEM,
-            pl.BlockSpec((t, d), lambda j: (0, 0)),
-            pl.BlockSpec((half, 256), low),
-            pl.BlockSpec((half, 256), high),
+            pl.BlockSpec((t, d), const),
+            pl.BlockSpec((half, wide), const),
+            pl.BlockSpec((half, wide), high),
         ]
-        + [pl.BlockSpec((half // 4, 256), lambda j: (0, j))] * 4,
-        out_specs=(pl.BlockSpec((t, 256), low), pl.BlockSpec((t, 256), high)),
-        scratch_shapes=[pltpu.VMEM((d, 256), BF16)],
+        + [pl.BlockSpec((half // 4, wide), lambda j: (0, j))] * 4,
+        out_specs=(pl.BlockSpec((t, wide), const), pl.BlockSpec((t, wide), high)),
+        scratch_shapes=[pltpu.VMEM((d, wide), BF16)],
     )(who, normed, q_own, s_own, *pieces)
 
 
@@ -342,8 +350,10 @@
     return call(mixer_kernel, outs, us=8)(small, q, kv, pre, swish, mcol, mrow, payload)
 
 
-def reader_kernel(who, x, small, gated, own, r0, r1, hidden_out, second_out, full):
-    place_rows(who, full, own[...], [r0[...], r1[...]])
+def reader_kernel(
+    who, x, small, gated, own, r0, r1, r2, r3, hidden_out, second_out, full
+):
+    place_rows(who, full, own[...], [r[...] for r in (r0, r1, r2, r3)], 3)
     hidden = x[...].astype(F32) + nn(gated[...], full[...])
     hidden_out[...] = hidden
     mean_sq = jnp.mean(hidden * hidden, axis=-1, keepdims=True)
@@ -366,7 +376,7 @@
 
 def feed_kernel(
     who, second, cot, g0, g1, u0, u1, down, r0, r1, r2, r3,
-    part_out, part_ds, keep, send, wg, wu, wd, sec_t, sg_, su_, sd_, total_out, total_ds,
+    part_out, part_ds, keep, send_own, send_over, wg, wu, wd, sec_t, sg_, su_, sd_, total_out, total_ds,
 ):
     j = pl.program_id(0)
 
@@ -409,9 +419,10 @@
             at = part * half + cb * 128
             sd_[at : at + 128, :] = grad_down[part * 128 : (part + 1) * 128, cb * 256 : (cb + 1) * 256]
     cols = slice(0, 256)
-    place_grads(who, keep, send, sg_, 0, cols)
-    place_grads(who, keep, send, su_, 32, cols)
-    place_grads(who, keep, send, sd_, 64, cols)
+    outs = (keep, send_own, send_over)
+    place_grads(who, outs, sg_, 0, cols)
+    place_grads(who, outs, su_, 32, cols)
+    place_grads(who, outs, sd_, 64, cols)
 
     @pl.when(j == pl.num_programs(0) - 1)
     def _():
@@ -427,11 +438,10 @@
     left = pl.BlockSpec((half, 128), lambda j: (0, start + j))
     right = pl.BlockSpec((half, 128), lambda j: (0, halves + start + j))
     full = pl.BlockSpec((t, d), lambda j: (0, 0))
-    grads = pl.BlockSpec((2, 2, 4, 96, 256), lambda j: (0, 0, 0, 0, j))
-    grads_shape = sds((2, 2, 4, 96, blocks * 256), BF16)
+    shapes, specs = grads_out(96, blocks * 256, 256, lambda j: j)
     return call(
         feed_kernel,
-        (sds((t, d), BF16), sds((t, d), BF16), grads_shape, grads_shape),
+        (sds((t, d), BF16), sds((t, d), BF16), *shapes),
         us=1 + 4.5 * blocks,
         vmem=56,
         grid=(blocks,),
@@ -440,7 +450,7 @@
             pl.BlockSpec((128, d), lambda j: (start + j, 0)),
         ]
         + [pl.BlockSpec((half // 4, 768), lambda j: (0, j))] * 4,
-        out_specs=(full, full, grads, grads),
+        out_specs=(full, full, *specs),
         scratch_shapes=[
             pltpu.VMEM((d, 256), BF16),
             pltpu.VMEM((d, 256), BF16),
@@ -487,12 +497,12 @@
 
 def mixer_back_kernel(
     who, small, s0, s1, s2, hidden, cot, swish, mixed, q, pre, mcol, payload,
-    own, r0, r1,
+    own, r0, r1, r2, r3,
     d_hidden_out, low_out, d_swish_out, d_mixed_out, rows_out, back_out, full, d_gated,
 ):
     t, d = hidden.shape
     kd = HEADS * DK
-    place_rows(who, full, own[...], [r0[...], r1[...]])
+    place_rows(who, full, own[...], [r[...] for r in (r0, r1, r2, r3)], 3)
     values = hidden[...]
     upstream = s0[...].astype(F32) + s1[...].astype(F32) + s2[...].astype(F32)
     scale = lax.rsqrt(jnp.mean(values * values, axis=-1, keepdims=True) + EPSILON)
@@ -561,7 +571,9 @@
         scratch_shapes=[pltpu.VMEM((vd, d), BF16), pltpu.VMEM((t, vd), F32)], us=11)(who, *ins)
 
 
-def gate_grads_kernel(who, normed, d_swish, gated, low, keep, send, scratch, left_t):
+def gate_grads_kernel(
+    who, normed, d_swish, gated, low, keep, send_own, send_over, scratch, left_t
+):
     j = pl.program_id(0)
     count = d_swish.shape[1]
     half = pl.num_programs(0) // 2
@@ -582,18 +594,17 @@
     def _():
         scratch[...] = nn(left_t[...], low[...]).astype(BF16)
 
-    place_grads(who, keep, send, scratch, 0, slice(0, 256))
+    place_grads(who, (keep, send_own, send_over), scratch, 0, slice(0, 256))
 
 
 def gate_grads(who, normed, d_swish, gated, low):
     t, d = normed.shape
     n = d_swish.shape[1] // 256
     const = lambda j: (0, 0)
-    shape = sds((2, 2, 4, 32, 2 * n * 256), BF16)
-    spec = pl.BlockSpec((2, 2, 4, 32, 256), lambda j: (0, 0, 0, 0, j))
+    shapes, specs = grads_out(32, 2 * n * 256, 256, lambda j: j)
     return call(
         gate_grads_kernel,
-        (shape, shape),
+        shapes,
         grid=(2 * n,),
         in_specs=[
             SMEM,
@@ -602,7 +613,7 @@
             pl.BlockSpec((t, d), const),
             pl.BlockSpec((t, 256), lambda j: (0, jnp.maximum(j - n, 0))),
         ],
-        out_specs=(spec, spec),
+        out_specs=specs,
         scratch_shapes=[pltpu.VMEM((d, 256), BF16), pltpu.VMEM((d, t), BF16)], us=9)(who, normed, d_swish, gated, low)
 
 
@@ -703,36 +714,29 @@
 ):
     j = pl.program_id(0)
     steps = pl.num_programs(0)
-
-    @pl.when(j == 0)
-    def _():
-        total[...] = nn(d_narrow[...], small[0:ROW_EXPAND, :])
-
     first = [r[...] for r in (a0, a1, a2, a3)]
     other = [r[...] for r in (b0, b1, b2, b3)]
 
-    @pl.when(j < 2)
+    @pl.when(j == 0)
     def _():
         place_rows(who, full, q_own[...], other)
+        total[...] = nn(d_narrow[...], small[0:ROW_EXPAND, :]) + nt(d_qkv[...], full[...])
+
+    @pl.when(j == 1)
+    def _():
+        place_rows(who, full, k_own[...], first)
 
     @pl.when((j >= 2) & (j < 4))
     def _():
-        place_rows(who, full, k_own[...], first)
-
-    @pl.when((j >= 4) & (j < 8))
-    def _():
         place_rows(who, full, v_own[...], first)
 
-    @pl.when(j >= 8)
+    @pl.when((j >= 1) & (j < 4))
+    def _():
+        total[...] += nt(d_qkv[...], full[...])
+
+    @pl.when(j >= 4)
     def _():
         place_rows(who, full, s_own[...], other)
-
-    @pl.when(j < 8)
-    def _():
-        total[...] += nt(d_qkv[...], full[...])
-
-    @pl.when(j >= 8)
-    def _():
         total[...] += nt(d_swish[...], full[...])
 
     @pl.when(j == steps - 1)
@@ -752,40 +756,39 @@
 def input_back(who, x, small, d_hidden, d_qkv, d_swish, d_narrow, owns, pieces, gate_pieces):
     t, d = x.shape
     half = d // 2
-    kd = HEADS * DK
-    vd = HEADS * DV
-    qn = kd // 256
-    vn = vd // 256
-    wn = 2 * qn + vn
+    wide = HEADS * DK
+    vn = HEADS * DV // wide
     const = lambda j: (0, 0)
-    beyond = lambda j: (0, jnp.where(j < wn, jnp.minimum(j, qn - 1), j - wn + qn))
     col = lambda low, count: (lambda j: (0, jnp.clip(j - low, 0, count - 1)))
+    beyond = lambda j: (0, jnp.clip(j - 1 - vn, 0, vn))
     return call(
         input_back_kernel,
         (sds((t, d), BF16), sds((8, d), F32)),
-        grid=(wn + vn,),
+        us=10,
+        grid=(2 + 2 * vn,),
         in_specs=[
             SMEM,
             pl.BlockSpec((t, d), const),
             pl.BlockSpec(small.shape, const),
             pl.BlockSpec((t, d), const),
-            pl.BlockSpec((t, 256), col(0, wn)),
-            pl.BlockSpec((t, 256), col(wn, vn)),
+            pl.BlockSpec((t, wide), col(0, 2 + vn)),
+            pl.BlockSpec((t, wide), col(2 + vn, vn)),
             pl.BlockSpec((t, 16), const),
-            pl.BlockSpec((half, 256), col(0, qn)),
-            pl.BlockSpec((half, 256), col(qn, qn)),
-            pl.BlockSpec((half, 256), col(2 * qn, vn)),
-            pl.BlockSpec((half, 256), col(wn, vn)),
+            pl.BlockSpec((half, wide), const),
+            pl.BlockSpec((half, wide), const),
+            pl.BlockSpec((half, wide), col(2, vn)),
+            pl.BlockSpec((half, wide), col(2 + vn, vn)),
         ]
-        + [pl.BlockSpec((half // 4, 256), col(qn, qn + vn))] * 4
-        + [pl.BlockSpec((half // 4, 256), beyond)] * 4,
+        + [pl.BlockSpec((half // 4, wide), col(1, 1 + vn))] * 4
+        + [pl.BlockSpec((half // 4, wide), beyond)] * 4,
         out_specs=(pl.BlockSpec((t, d), const), pl.BlockSpec((8, d), const)),
-        scratch_shapes=[pltpu.VMEM((t, d), F32), pltpu.VMEM((d, 256), BF16)], us=15)(who, x, small, d_hidden, d_qkv, d_swish, d_narrow, *owns, *pieces, *gate_pieces)
+        scratch_shapes=[pltpu.VMEM((t, d), F32), pltpu.VMEM((d, wide), BF16)],
+    )(who, x, small, d_hidden, d_qkv, d_swish, d_narrow, *owns, *pieces, *gate_pieces)
 
 
 def late_grads_kernel(
     who, normed, d_qkv, d_narrow, narrow, d_pre, rows_in, bias_in, mixer_in,
-    keep, send, scratch, strip, left_t, rows,
+    keep, send_own, send_over, scratch, strip, left_t, rows,
 ):
     t, d = normed.shape
     half = d // 2
@@ -795,7 +798,7 @@
     for j in range(n):
         c = slice(j * 256, (j + 1) * 256)
         scratch[...] = nn(left_t[...], d_qkv[:, c]).astype(BF16)
-        place_grads(who, keep, send, scratch, 0, c)
+        place_grads(who, (keep, send_own, send_over), scratch, 0, c)
     rows[...] = jnp.zeros_like(rows)
     rows[LANE_FEED : LANE_FEED + 1, :] = rows_in[0:1, :]
     rows[LANE_MIXER : LANE_MIXER + 1, :] = mixer_in[0:1, :]
@@ -813,21 +816,21 @@
     strip[:, 0:16] = squeeze.astype(BF16)
     strip[0:part, LANE_EXPAND : LANE_EXPAND + 16] = expand[0:part].astype(BF16)
     strip[half : half + part, LANE_EXPAND : LANE_EXPAND + 16] = expand[part:kd].astype(BF16)
-    place_grads(who, keep, send, strip, 0, slice(n * 256, n * 256 + 128))
+    place_grads(who, (keep, send_own, send_over), strip, 0, slice(n * 256, n * 256 + 128))
 
 
 def late_grads(who, normed, d_qkv, d_narrow, narrow, d_pre, rows_in, bias_in, mixer_in):
     t, d = normed.shape
-    shape = sds((2, 2, 4, 32, d_qkv.shape[1] + 128), BF16)
+    shapes, specs = grads_out(32, d_qkv.shape[1] + 128)
     whole = lambda a: pl.BlockSpec(a.shape, lambda i: (0,) * len(a.shape))
     ins = (normed, d_qkv, d_narrow, narrow, d_pre, rows_in, bias_in, mixer_in)
     return call(
         late_grads_kernel,
-        (shape, shape),
+        shapes,
         us=10,
         grid=(1,),
         in_specs=[SMEM] + [whole(a) for a in ins],
-        out_specs=(whole(shape), whole(shape)),
+        out_specs=specs,
         scratch_shapes=[
             pltpu.VMEM((d, 256), BF16),
             pltpu.VMEM((d, 128), BF16),
@@ -847,6 +850,41 @@
                 count = out.shape[1]
                 out[rows, :] = part[zz, :, at : at + count].astype(F32)
                 at += count
+
+
+def last_settle_kernel(
+    who, a, b, c, d, query, key, value, squeeze, expand, feed, bias, heads, mixer, strip
+):
+    me = who[2]
+    wide = query.shape[1] + key.shape[1] + value.shape[1]
+    for k, part in enumerate((a, b, c, d)):
+        for zz in range(4):
+            rows = pl.ds(pl.multiple_of((me ^ (k * 4 + zz)) * 32, 32), 32)
+            at = 0
+            for out in (query, key, value):
+                count = out.shape[1]
+                out[rows, :] = part[zz, :, at : at + count].astype(F32)
+                at += count
+            strip[rows, :] = part[zz, :, wide:].astype(F32)
+    turned = strip[...].T
+    squeeze[...] = turned[0:16, :]
+    expand[...] = strip[0 : expand.shape[0], LANE_EXPAND : LANE_EXPAND + 16]
+    feed[...] = turned[LANE_FEED : LANE_FEED + 1, :]
+    bias[...] = turned[LANE_BIAS : LANE_BIAS + 1, 0 : bias.shape[1]]
+    heads[...] = turned[LANE_HEADS : LANE_HEADS + 1, 0 : heads.shape[1]]
+    mixer[...] = turned[LANE_MIXER : LANE_MIXER + 1, :]
+
+
+def last_settle(who, parts, half):
+    kd, vd = HEADS * DK, HEADS * DV
+    shapes = [(half, kd), (half, kd), (half, vd), (16, half), (kd // 2, 16)]
+    shapes += [(1, half), (1, kd // 2), (1, DV // 2), (1, half)]
+    return call(
+        last_settle_kernel,
+        [sds(shape, F32) for shape in shapes],
+        in_specs=[SMEM] + [VMEM] * 4,
+        scratch_shapes=[pltpu.VMEM((half, 128), F32)],
+    )(who, *parts)
 
 
 def settle(who, parts, half, widths):
@@ -937,7 +975,7 @@
         for part in self.parts:
             width = part.keep.shape[-1]
             cut = [a[..., at : at + width] for a in more]
-            sums.append(added(part.keep[0, y, k], part.got[0, y, k], part.over[y, k], *cut))
+            sums.append(added(part.keep[0, y, k], part.got[y, k], part.over[y, k], *cut))
             at += width
         return sums[0] if len(sums) == 1 else jnp.concatenate(sums, axis=-1)
 
@@ -969,16 +1007,15 @@
 
     def gathered(self, now):
         beside = tied(self.beside, now)
-        return (self.line, beside, swap(self.line, 1), swap(beside, 1))
-
-
-def over_core(keep, send):
-    got = swap(send, 1)
-    return got, added(keep[1], got[1])
-
-
-def natural(keep, send):
-    both = jnp.stack([keep, send])
+        return (self.line, beside, swap(tied(self.line, beside), 1), swap(beside, 1))
+
+
+def over_core(keep, send_over):
+    return added(keep[1], swap(send_over, 1))
+
+
+def natural(keep, send_own, send_over):
+    both = jnp.stack([keep, jnp.stack([send_own, send_over])])
     both = jnp.moveaxis(both, 0, 1)
     return both.reshape((2, 16) + keep.shape[3:])
 
@@ -1066,9 +1103,10 @@
         core, side, deep = place % 2, (place // 2) % 2, place // 4
         x = lax.axis_index("fsdp")
         q = side * 2 + core
-        who = jnp.stack([x, q, core * 8 + side * 4 + deep]).astype(jnp.int32)
+        q_deep = (deep % 2) * 2 + core
+        who = jnp.stack([x, q, core * 8 + side * 4 + deep, q_deep]).astype(jnp.int32)
     else:
-        who = jnp.zeros((3,), jnp.int32)
+        who = jnp.zeros((4,), jnp.int32)
         x = q = 0
         gather = lambda a, dim=0: lax.all_gather(a, "fsdp", axis=dim, tiled=True)
         query_map, key_map, value_map, swish_map, readout, gate_map, up_map, down_map = [
@@ -1101,7 +1139,7 @@
 
     if paired:
         return paired_device(
-            who, x, q, mcol, mrow, inputs, cotangent, query_map, key_map, value_map, swish_map,
+            who, x, q, q_deep, mcol, mrow, inputs, cotangent, query_map, key_map, value_map, swish_map,
             readout, gate_map, up_map, down_map,
             packed(squeeze, expand, mixer_gain, feed_gain, forget_bias, head_gain),
             starts, counts,
@@ -1114,11 +1152,11 @@
     )
     kv_pieces = share((key_map, value_map))
     gate_pieces = share((query_map, swish_map))
-    read_pieces = (upper(readout)[: half // 2], upper(readout)[half // 2 :])
+    read_pieces = share((readout,))
     others = (upper(gate_map), upper(up_map), upper(down_map))
     feed_pieces = [
         tuple(
-            pack_feed(jnp.full((3,), k, jnp.int32), *others, s, n) for k in range(4)
+            pack_feed(jnp.full((4,), k, jnp.int32), *others, s, n) for k in range(4)
         )
         for s, n in zip(starts, counts)
     ]
@@ -1136,12 +1174,12 @@
 
     feed_grads, out_parts, second_parts = [], [], []
     for s, n, pieces in zip(starts, counts, feed_pieces):
-        out_part, second_part, keep, send = feed(
+        out_part, second_part, *grads = feed(
             who, second, cotangent, gate_map, up_map, down_map, pieces, s, n
         )
         out_parts.append(out_part)
         second_parts.append(second_part)
-        feed_grads.append((keep, send))
+        feed_grads.append(grads)
     output = summed(hidden, *out_parts)
 
     d_hidden, low, d_swish, d_mixed, rows, back = mixer_back(
@@ -1163,8 +1201,8 @@
     )
 
     gates, ups, downs = [], [], []
-    for (keep, send), n in zip(feed_grads, counts):
-        block = natural(keep, send)
+    for grads, n in zip(feed_grads, counts):
+        block = natural(*grads)
         sides = lambda k: block[:, :, 32 * k : 32 * (k + 1), :].reshape(d, n, 2, 128)
         gates.append(sides(0))
         ups.append(sides(1))
@@ -1194,7 +1232,7 @@
 
 
 def paired_device(
-    who, x, q, mcol, mrow, inputs, cotangent, query_map, key_map, value_map, swish_map,
+    who, x, q, q_deep, mcol, mrow, inputs, cotangent, query_map, key_map, value_map, swish_map,
     readout, gate_map, up_map, down_map, small_own, starts, counts,
 ):
     t, d = inputs.shape
@@ -1217,16 +1255,20 @@
     def together(*values):
         return lax.optimization_barrier(values)
 
-    def core_step(grads, *after):
-        keep, send = grads
-        ((got, out),) = fenced(tied(go, send, *after), lambda: over_core(keep, send))
-        return Part(keep, got), out
+    def core_step(grads, *after, weights=()):
+        keep, send_own, send_over = grads
+        out, *swapped = fenced(
+            tied(go, send_over, *after),
+            lambda: over_core(keep, send_over),
+            *((lambda v=v: swap(v, 1)) for v in weights),
+        )
+        return Part(keep, swap(tied(send_own, out), 1)), out, *swapped
 
     small_other = cross(small_own)
     kv_share = share((key_map, value_map))
     kv_first = cross(kv_share)
     gate_share = share((tied(query_map, kv_share), swish_map))
-    read_share = lax.dynamic_slice_in_dim(tied(readout, kv_share), (q % 2) * (half // 2), half // 2, 0)
+    read_share = lax.dynamic_slice_in_dim(tied(readout, kv_share), q_deep * quarter, quarter, 0)
     def pack(i, *after):
         return pack_feed(tied(who, *after), gate_map, up_map, down_map, starts[i], counts[i])
 
@@ -1250,64 +1292,69 @@
     normed, kv, pre, narrow = project(
         tied(who, gate_first), inputs, small, key_map, value_map, kv_pieces
     )
-    gate_second, f0_first, normed = together(gate_second, f0_first, normed)
-    gate_fourth = swap(gate_second, 1)
+    local, _ = local_state(kv, pre, mcol, tied(mrow, normed))
+    gate_second, f0_first, local = together(gate_second, f0_first, local)
+    gate_fourth, f0_third = together(swap(gate_second, 1), swap(f0_first, 1))
     gate_pieces = (gate_first, gate_third, gate_second, gate_fourth)
-    f0_third = swap(f0_first, 1)
-    read_first = cross(tied(read_share, f0_first))
-    local, _ = local_state(kv, pre, mcol, tied(mrow, normed))
-    payload, (queries, swish), f0_second = fenced(
+    payload, (queries, swish), read_first, f0_second = fenced(
         tied(go, local, gate_fourth, f0_third),
         lambda: lax.ppermute(local, "fsdp", [(0, 1)]),
         lambda: swish_project(who, normed, query_map, swish_map, gate_pieces),
+        lambda: cross(read_share),
         lambda: swap(f0_first, 2),
     )
-    read_first, swish = together(read_first, swish)
-    read_pieces = (read_first, swap(read_first, 1))
-    f0_pieces = (f0_first, f0_third, f0_second, swap(f0_second, 1))
-    f1_first = cross(tied(feed_shares[1], read_first))
+    f0_fourth = swap(f0_second, 1)
+    f0_pieces = (f0_first, f0_third, f0_second, f0_fourth)
+    read_second, read_third = swap(read_first, 4), swap(read_first, 1)
+    f1_first = cross(tied(feed_shares[1], swish))
     mixed, states, gated = mixer(
         tied(small, swish), queries, kv, pre, swish, mcol, mrow, payload
     )
-    hidden, second = reader(tied(who, gated, f0_pieces[3]), inputs, small, gated, readout, read_pieces)
+    gated, read_second, read_third, f0_fourth = together(
+        gated, read_second, read_third, f0_fourth
+    )
+    f0_pieces = (f0_first, f0_third, f0_second, f0_fourth)
+    read_pieces = (read_first, read_third, read_second, swap(read_second, 1))
+    hidden, second = reader(tied(who, gated), inputs, small, gated, readout, read_pieces)
     f1_first, hidden = together(f1_first, hidden)
     f1_second, f1_third = swap(f1_first, 2), swap(f1_first, 1)
     f2_first = cross(tied(feed_shares[2], f1_first))
 
     def feed_part(i, pieces, *after):
-        out_part, second_part, keep, send = feed(
+        out_part, second_part, *grads = feed(
             tied(who, *after), second, cotangent, gate_map, up_map, down_map, pieces, starts[i],
             counts[i],
         )
         out_parts.append(out_part)
         second_parts.append(second_part)
-        return keep, send
+        return grads
 
     out_parts, second_parts = [], []
-    grads = feed_part(0, f0_pieces, hidden, f1_first)
-    part0, out = core_step(grads, f1_third)
-    f2_first, f1_second, out = together(f2_first, f1_second, out)
+    grads = feed_part(0, f0_pieces, hidden)
+    part0, out, f1_fourth = core_step(grads, f1_third, f1_second, weights=(f1_second,))
+    f1_pieces = (f1_first, f1_third, f1_second, f1_fourth)
+    f2_first, out = together(f2_first, out)
     part0.over = cross(out)
-    f1_pieces = (f1_first, f1_third, f1_second, swap(f1_second, 1))
     f2_second, f2_third = swap(f2_first, 2), swap(f2_first, 1)
     grads = feed_part(1, f1_pieces, out)
-    part1, out = core_step(grads, f2_second, f2_third)
+    part1, out, f2_fourth = core_step(grads, f2_second, f2_third, weights=(f2_second,))
+    f2_pieces = (f2_first, f2_third, f2_second, f2_fourth)
     f0, f1 = Chain(part0), Chain(part1)
     a = f0.to_y(out)
     a, out = together(a, out)
     part1.over = cross(out)
     f0.side = swap(a, 2)
-    f2_pieces = (f2_first, f2_third, f2_second, swap(tied(f2_second, a), 1))
-    keep, send = feed_part(2, f2_pieces, a)
+    keep, send_own, send_over = feed_part(2, f2_pieces, a)
     a = f0.to_near(keep)
     f0.near = swap(a, 4)
-    back_parts, (got, f2_out) = fenced(
+    back_parts, f2_out, got = fenced(
         tied(go, a),
         lambda: mixer_back(
             who, small, second_parts, hidden, cotangent, swish, mixed, queries, pre, mcol,
             payload, readout, read_pieces,
         ),
-        lambda: over_core(keep, send),
+        lambda: over_core(keep, send_over),
+        lambda: swap(send_own, 1),
     )
     d_hidden, low, d_swish, d_mixed, rows, back = back_parts
     part2 = Part(keep, got)
@@ -1318,16 +1365,17 @@
     entering = lax.ppermute(back, "fsdp", [(1, 0)])
     f0.far = swap(a, 8)
     f1.side = swap(b, 2)
-    keep, send = gate_grads(tied(who, a), normed, d_swish, gated, low)
+    keep, send_own, send_over = gate_grads(tied(who, a), normed, d_swish, gated, low)
     a = f0.own_of_far(keep)
     a, entering = together(a, entering)
     f0.far = swap(a, 8)
-    (d_qkv, d_pre, d_narrow, bias_row), (got, g_out) = fenced(
+    (d_qkv, d_pre, d_narrow, bias_row), g_out, got = fenced(
         tied(go, a),
         lambda: recurrence_back(
             small, queries, kv, pre, d_mixed, mcol, mrow, payload, states, entering
         ),
-        lambda: over_core(keep, send),
+        lambda: over_core(keep, send_over),
+        lambda: swap(send_own, 1),
     )
     part_g = Part(keep, got)
     g = Chain(part_g)
@@ -1345,70 +1393,67 @@
     grads = late_grads(
         tied(who, a), normed, d_qkv, d_narrow, narrow, d_pre, rows, bias_row, mixer_row
     )
-    a = f1.own_of_far(grads[0])
-    part_v, v_out = core_step(grads, a)
+    c = g.to_y(grads[0])
+    part_v, v_out = core_step(grads, c)
     v = Chain(part_v)
-    a, line0, v_out = together(a, a0, v_out)
-    f1.far = swap(a, 8)
+    a, b = f1.own_of_far(v_out), f2.to_near(v_out)
+    a, b, c, line0, v_out = together(a, b, c, a0, v_out)
     part_v.over = cross(v_out)
-    now = f2.to_near(v_out)
-    f2.near = swap(now, 4)
-    now = g.to_y(now)
-    g.side = swap(now, 2)
-    now = f1.back_near(now)
+    f1.far, f2.near, g.side = swap(a, 8), swap(b, 4), swap(c, 2)
+    now = f1.back_near(c)
     f1.near = swap(now, 4)
     f0.beside = swap(tied(line0, now), 2)
     now = f2.to_far(now)
     f2.far = swap(now, 8)
-    output = summed(tied(hidden, now), *out_parts)
-    now = v.to_y(output)
-    v.side = swap(now, 2)
-    now = f2.own_of_far(now)
-    f2.far = swap(now, 8)
     now = g.to_near(now)
     g.near = swap(now, 4)
+    output = summed(tied(hidden, now), *out_parts)
+    now = f2.own_of_far(output)
+    f2.far = swap(now, 8)
+    now = v.to_y(now)
+    v.side = swap(now, 2)
     now = f1.back_y(now)
     f1.beside = swap(now, 2)
+    now = g.to_far(now)
+    g.far = swap(now, 8)
+    now = f2.back_near(now)
+    f2.near = swap(now, 4)
     f0_parts = f0.gathered(now)
     feeds = feed_settle(tied(who, now), f0_parts, None, starts[0], counts[0], half, ff, d)
-    now = f2.back_near(feeds[0])
-    f2.near = swap(now, 4)
-    now = g.to_far(now)
+    now = v.to_near(feeds[0])
+    v.near = swap(now, 4)
+    now = g.own_of_far(now)
     g.far = swap(now, 8)
-    now = v.to_near(now)
-    v.near = swap(now, 4)
     now = f2.back_y(now)
     f2.beside = swap(now, 2)
-    now = g.own_of_far(now)
-    g.far = swap(now, 8)
     now = v.to_far(now)
     v.far = swap(now, 8)
-    f1_parts = f1.gathered(now)
     now = g.back_near(now)
     g.near = swap(now, 4)
     now = v.own_of_far(now)
     v.far = swap(now, 8)
+    f1_parts = f1.gathered(now)
     feeds = feed_settle(tied(who, now), f1_parts, feeds, starts[1], counts[1], half, ff, d)
     now = v.back_near(feeds[0])
     v.near = swap(now, 4)
     now = g.back_y(now)
     g.beside = swap(now, 2)
+    f2_parts = f2.gathered(now)
     now = v.back_y(now)
     v.beside = swap(now, 2)
-    f2_parts = f2.gathered(now)
     feeds = feed_settle(tied(who, now), f2_parts, feeds, starts[2], counts[2], half, ff, d)
     g_parts = g.gathered(feeds[0])
-    v_parts = v.gathered(feeds[0])
     grad_swish, grad_readout = settle(tied(who, feeds[0]), g_parts, half, (vd, vd))
-    grad_query, grad_key, grad_value, strip = settle(
-        tied(who, grad_swish), v_parts, half, (kd, kd, vd, 128)
-    )
+    v_parts = v.gathered(grad_swish)
+    grad_query, grad_key, grad_value, squeeze_t, expand_t, *small_grads = last_settle(
+        tied(who, grad_swish), v_parts, half
+    )
+    grad_feed, grad_bias, grad_heads, grad_mixer = [a[0] for a in small_grads]
     grad_gate, grad_up, grad_down = feeds
     return (
-        output, grad_input, strip[:, LANE_MIXER], grad_query, grad_key, grad_value, grad_swish,
-        strip[:, :16], strip[: kd // 2, LANE_EXPAND : LANE_EXPAND + 16].T,
-        strip[: kd // 2, LANE_BIAS], strip[: DV // 2, LANE_HEADS], grad_readout,
-        strip[:, LANE_FEED], grad_gate, grad_up, grad_down,
+        output, grad_input, grad_mixer, grad_query, grad_key, grad_value, grad_swish,
+        squeeze_t.T, expand_t.T, grad_bias, grad_heads, grad_readout, grad_feed,
+        grad_gate, grad_up, grad_down,
     )
 
 

time: 420 us -> 403 us (0.960)
  waiting for transfers between devices: 123 us -> 103 us
  starting transfers between devices: 59.9 us -> 73.4 us
  Pallas kernels: 160 us -> 153 us
  other arithmetic: 53.7 us -> 47.8 us
    ppermute x61 -> x68, waiting for transfers between devices: 106 us -> 90 us  [swap(): return lax.ppermute(v, 'replica', [(i, i ^ bit) for i in range(count)])]
    ppermute x61 -> x68, starting transfers between devices: 40.7 us -> 53.6 us  [swap(): return lax.ppermute(v, 'replica', [(i, i ^ bit) for i in range(count)])]
    convert_element_type x25, other arithmetic: 46.9 us -> 41 us  [added(): return total.astype(BF16)]
    pallas_call x8 -> x9, Pallas kernels: 88.4 us -> 85.6 us  [the longest x3 47.4 us: feed(): call(feed_kernel, (sds((t, d), BF16), sds((t, d), BF16), *shapes), us=1 +...]
  transfers between devices with their start and end apart: 75 -> 82, of which waited for: 32 -> 33; matrix products, arithmetic and copies ran while one was open for 12% -> 12% of each run, Pallas kernels for 38% -> 38%
where the time goes in v4:
time: 403 us; the launch traced here: 397 us
  Pallas kernels  153 us (38%)
  waiting for transfers between devices  103 us (26%)
  starting transfers between devices  73.4 us (18%)
  other arithmetic  47.8 us (12%)
  local copies, waits for them, and re-layouts  17.2 us (4%)
    ppermute x68, waiting for transfers between devices, swap(): return lax.ppermute(v, 'replica', [(i, i ^ bit) for i in range(count)])  90 us
    ppermute x68, starting transfers between devices, swap(): return lax.ppermute(v, 'replica', [(i, i ^ bit) for i in range(count)])  53.6 us
    pallas_call x3, Pallas kernels, feed(): call(feed_kernel, (sds((t, d), BF16), sds((t, d), BF16), *shapes), us=1 +...  47.4 us
    convert_element_type x25, other arithmetic, added(): return total.astype(BF16)  41 us
    pallas_call x3, Pallas kernels, feed_settle(): call(functools.partial(feed_settle_kernel, first=first), shapes, us=2 * b...  16.2 us
    ppermute x12, starting transfers between devices, cross(): return lax.ppermute(v, 'fsdp', [(0, 1), (1, 0)])  14.7 us
    ppermute x12, waiting for transfers between devices, cross(): return lax.ppermute(v, 'fsdp', [(0, 1), (1, 0)])  13.1 us
    pallas_call x1, Pallas kernels, mixer_back(): call(mixer_back_kernel, outs, grid=(1,), in_specs=[SMEM] + [whole(a) for...  11.7 us
  transfers between devices with their start and end apart: 82, of which 33 were waited for; matrix products, arithmetic and copies ran while one was open for 12% of the time, Pallas kernels for 38%

profile of v4, /device:TPU:0, one launch (start us, length us, event | category | flops | bytes accessed | tf_op | source)
XLA Modules:
  0.0 396.6 jit_solution(3183130599287454724)
XLA Ops:
  26.0 4.0 %shard_map.289 = bf16[128,3072]{1,0:T(8,128)(2,1)} custom-call(s32[4]{0:T(128)S(1)} %pad_add_fusion.who, bf16[512,2816]{1,0:T(8,128)(2,1)} %g1.11, bf16[512,2816]{1,0:T(8,128)(2,1)} %g1.11, bf16[512,2816]{1,0:T(8,128)(2,1)} %u1_.11, bf16[512,2816]{1,0:T(8,128)(2,1)} %u1_.11, bf16[1408,1024]{1,0:T(8,128)(2,1)} %down.11), custom_call_target="tpu_custom_call" | custom-call | flops 40000000 | bytes 144000 | tf_op jit(solution)/shard_map/pallas_call | solution.py:482
  38.0 5.8 %shard_map.291 = (bf16[512,1024]{1,0:T(8,128)(2,1)}, bf16[512,1536]{1,0:T(8,128)(2,1)S(1)}, f32[512,512]{1,0:T(8,128)}, bf16[512,16]{1,0:T(8,128)(2,1)S(1)}) custom-call(s32[4]{0:T(128)S(1)} %pad_add_fusion.who, bf16[512,1024]{1,0:T(8,128)(2,1)S(1)} %copy-done, bf16[48,1024]{1,0:T(8,128)(2,1)S(1)} %pad_maximum_fusion.12.small, ...), custom_call_target="tpu_custom_call" | custom-call | flops 50000000 | bytes 180000 | tf_op jit(solution)/shard_map/pallas_call | solution.py:198
  45.0 4.0 %shard_map.292 = (bf16[1040,128]{1,0:T(8,128)(2,1)}, f32[8,512]{1,0:T(8,128)}) custom-call(bf16[512,1536]{1,0:T(8,128)(2,1)S(1)} %get-tuple-element.397.kv, f32[512,512]{1,0:T(8,128)} %get-tuple-element.398.pre, f32[512,1]{1,0:T(8,128)S(1)} %copy.40.mcol, f32[1,512]{1,0:T(1,128)S(1)} %get-tuple-element.400.mrow), custom_call_target="tpu_custom_call" | custom-call | flops 50000000 | bytes 180000 | tf_op jit(solution)/shard_map/pallas_call | solution.py:292
  52.6 15.7 %conditional.6 = (bf16[1040,128]{1,0:T(8,128)(2,1)}, bf16[512,512]{1,0:T(8,128)(2,1)S(1)}, f32[512,1024]{1,0:T(8,128)S(1)}, bf16[128,1024]{1,0:T(8,128)(2,1)}, bf16[128,2304]{1,0:T(8,128)(2,1)}) conditional(s32[]{:T(128)} %convert_element_type.682, () %tuple.152, (bf16[1040,128]{1,0:T(8,128)(2,1)}, s32[4]{0:T(128)S(1)}, ...), branch_computations={%region_0.1_spmd, %region_1.2_spmd} | conditional | flops 50000000 | bytes 4652992 | solution.py:960
  57.1 4.5 %branch_1_fun.3 = (bf16[512,512]{1,0:T(8,128)(2,1)S(1)}, f32[512,1024]{1,0:T(8,128)S(1)}) custom-call(s32[4]{0:T(128)S(1)} %get-tuple-element.110.who, bf16[512,1024]{1,0:T(8,128)(2,1)S(1)} %get-tuple-element.111.normed, bf16[512,512]{1,0:T(8,128)(2,1)} %get-tuple-element.112.q_own, bf16[512,1024]{1,0:T(8,128)(2,1)} %get-tuple-element.113.s_own, ...), custom_call_target="tpu_custom_call" | custom-call | flops 50000000 | bytes 180000 | tf_op jit(solution)/shard_map/cond/branch_1_fun/pallas_call | solution.py:242
  61.6 5.7 %collective-permute-done.1 = bf16[128,1024]{1,0:T(8,128)(2,1)} collective-permute-done((bf16[128,1024]{1,0:T(8,128)(2,1)}, bf16[128,1024]{1,0:T(8,128)(2,1)}, u32[]{:S(2)}, u32[]{:S(2)}) %collective-permute-start.1) | collective-permute-done | bytes 262176 | tf_op jit(solution)/shard_map/cond/branch_1_fun/ppermute | solution.py:949
  71.8 6.8 %shard_map.293 = (f32[512,1024]{1,0:T(8,128)}, bf16[4,4,256,128]{3,2,1,0:T(8,128)(2,1)}, bf16[512,1024]{1,0:T(8,128)(2,1)S(1)}) custom-call(bf16[48,1024]{1,0:T(8,128)(2,1)} %copy-done.22, bf16[512,512]{1,0:T(8,128)(2,1)S(1)} %get-tuple-element.412.q, bf16[512,1536]{1,0:T(8,128)(2,1)} %copy-done.14, f32[512,512]{1,0:T(8,128)} %get-tuple-element.398.pre, ...), custom_call_target="tpu_custom_call" | custom-call | flops 80000000 | bytes 288000 | tf_op jit(solution)/shard_map/pallas_call | solution.py:350
  91.6 13.6 %shard_map.295 = (bf16[512,1024]{1,0:T(8,128)(2,1)}, bf16[512,1024]{1,0:T(8,128)(2,1)}, bf16[2,2,4,96,768]{4,3,2,1,0:T(8,128)(2,1)}, bf16[2,4,96,768]{3,2,1,0:T(8,128)(2,1)}, bf16[2,4,96,768]{3,2,1,0:T(8,128)(2,1)}) custom-call(s32[4]{0:T(128)S(1)} %pad_add_fusion.who, bf16[512,1024]{1,0:T(8,128)(2,1)} %copy-done.1, bf16[512,1024]{1,0:T(8,128)(2,1)S(1)} %copy-done.12, ...), custom_call_target="tpu_custom_call" | custom-call | flops 145000000 | bytes 522000 | tf_op jit(solution)/shard_map/pallas_call | solution.py:442
  109.3 6.8 %conditional.7 = (bf16[2,4,96,768]{3,2,1,0:T(8,128)(2,1)}, bf16[128,3072]{1,0:T(8,128)(2,1)}) conditional(s32[]{:T(128)} %convert_element_type.685, () %tuple.161, (bf16[2,2,4,96,768]{4,3,2,1,0:T(8,128)(2,1)}, bf16[2,4,96,768]{3,2,1,0:T(8,128)(2,1)}, bf16[128,3072]{1,0:T(8,128)(2,1)}) %tuple.272), branch_computations={%region_2.3_spmd, %region_3.4_spmd} | conditional | flops 2359296 | bytes 11403360 | solution.py:960
  119.9 17.1 %shard_map.296 = (bf16[512,1024]{1,0:T(8,128)(2,1)}, bf16[512,1024]{1,0:T(8,128)(2,1)}, bf16[2,2,4,96,1024]{4,3,2,1,0:T(8,128)(2,1)}, bf16[2,4,96,1024]{3,2,1,0:T(8,128)(2,1)}, bf16[2,4,96,1024]{3,2,1,0:T(8,128)(2,1)}) custom-call(s32[4]{0:T(128)S(1)} %pad_add_fusion.who, bf16[512,1024]{1,0:T(8,128)(2,1)} %copy-done.1, bf16[512,1024]{1,0:T(8,128)(2,1)} %cot.5, ...), custom_call_target="tpu_custom_call" | custom-call | flops 190000000 | bytes 684000 | tf_op jit(solution)/shard_map/pallas_call | solution.py:442
  138.1 8.0 %conditional.8 = (bf16[2,4,96,1024]{3,2,1,0:T(8,128)(2,1)}, bf16[128,3072]{1,0:T(8,128)(2,1)}) conditional(s32[]{:T(128)} %convert_element_type.688, () %tuple.168, (bf16[2,2,4,96,1024]{4,3,2,1,0:T(8,128)(2,1)}, bf16[2,4,96,1024]{3,2,1,0:T(8,128)(2,1)}, bf16[128,3072]{1,0:T(8,128)(2,1)}) %tuple.169), branch_computations={%region_4.5_spmd, %region_5.6_spmd} | conditional | flops 3145728 | bytes 14155872 | solution.py:960
  138.7 4.2 %collective-permute-done.5 = bf16[2,4,96,1024]{3,2,1,0:T(8,128)(2,1)S(1)} collective-permute-done((bf16[2,4,96,1024]{3,2,1,0:T(8,128)(2,1)}, bf16[2,4,96,1024]{3,2,1,0:T(8,128)(2,1)S(1)}, u32[]{:S(2)}, u32[]{:S(2)}) %collective-permute-start.5) | collective-permute-done | bytes 1572896 | tf_op jit(solution)/shard_map/cond/branch_1_fun/ppermute | solution.py:945
  150.0 16.8 %shard_map.297 = (bf16[512,1024]{1,0:T(8,128)(2,1)}, bf16[512,1024]{1,0:T(8,128)(2,1)}, bf16[2,2,4,96,1024]{4,3,2,1,0:T(8,128)(2,1)}, bf16[2,4,96,1024]{3,2,1,0:T(8,128)(2,1)}, bf16[2,4,96,1024]{3,2,1,0:T(8,128)(2,1)}) custom-call(s32[4]{0:T(128)S(1)} %pad_add_fusion.who, bf16[512,1024]{1,0:T(8,128)(2,1)} %copy-done.1, bf16[512,1024]{1,0:T(8,128)(2,1)S(1)} %copy-done.13, ...), custom_call_target="tpu_custom_call" | custom-call | flops 190000000 | bytes 684000 | tf_op jit(solution)/shard_map/pallas_call | solution.py:442
  171.2 15.7 %conditional.9 = (f32[512,1024]{1,0:T(8,128)}, bf16[512,1024]{1,0:T(8,128)(2,1)}, bf16[512,1024]{1,0:T(8,128)(2,1)}, bf16[512,1024]{1,0:T(8,128)(2,1)}, f32[8,10...) conditional(s32[]{:T(128)} %convert_element_type.708, ...), branch_computations={%region_6.7_spmd, %region_7.8_spmd} | conditional | flops 113145728 | bytes 30284684 | solution.py:960
  171.8 11.7 %branch_1_fun.4 = (f32[512,1024]{1,0:T(8,128)}, bf16[512,1024]{1,0:T(8,128)(2,1)}, bf16[512,1024]{1,0:T(8,128)(2,1)}, bf16[512,1024]{1,0:T(8,128)(2,1)}, f32[8,1024]{1,0:T(8,128)}, /*index=5*/bf16[1024,128]{1,0:T(8,128)(2,1)}) custom-call(s32[4]{0:T(128)S(1)} %get-tuple-element.128.who, bf16[48,1024]{1,0:T(8,128)(2,1)} %get-tuple-element.129.small, ...), custom_call_target="tpu_custom_call" | custom-call | flops 110000000 | bytes 396000 | tf_op jit(solution)/shard_map/cond/branch_1_fun/pallas_call | solution.py:565
  198.8 8.7 %shard_map.298 = (bf16[2,2,4,32,2048]{4,3,2,1,0:T(8,128)(2,1)}, bf16[2,4,32,2048]{3,2,1,0:T(8,128)(2,1)}, bf16[2,4,32,2048]{3,2,1,0:T(8,128)(2,1)}) custom-call(s32[4]{0:T(128)S(1)} %pad_add_fusion.who, bf16[512,1024]{1,0:T(8,128)(2,1)S(1)} %copy-done.16, bf16[512,1024]{1,0:T(8,128)(2,1)} %get-tuple-element.465.d_swish, ...), custom_call_target="tpu_custom_call" | custom-call | flops 90000000 | bytes 324000 | tf_op jit(solution)/shard_map/pallas_call | solution.py:605
  209.2 14.4 %conditional.10 = (bf16[512,2048]{1,0:T(8,128)(2,1)}, bf16[512,512]{1,0:T(8,128)(2,1)}, bf16[512,16]{1,0:T(8,128)(2,1)S(1)}, f32[8,512]{1,0:T(8,128)}, bf16[2,4,...) conditional(s32[]{:T(128)} %convert_element_type.733, () %tuple.185, (bf16[48,1024]{1,0:T(8,128)(2,1)S(1)}, ...), branch_computations={%region_8.9_spmd, %region_9.10_spmd} | conditional | flops 112097152 | bytes 20323196 | solution.py:960
  209.9 11.1 %branch_1_fun.5 = (bf16[512,2048]{1,0:T(8,128)(2,1)}, bf16[512,512]{1,0:T(8,128)(2,1)}, bf16[512,16]{1,0:T(8,128)(2,1)S(1)}, f32[8,512]{1,0:T(8,128)}) custom-call(bf16[48,1024]{1,0:T(8,128)(2,1)S(1)} %get-tuple-element.155.small, bf16[512,512]{1,0:T(8,128)(2,1)} %get-tuple-element.156.q, bf16[512,1536]{1,0:T(8,128)(2,1)} %get-tuple-element.157.kv, ...), custom_call_target="tpu_custom_call" | custom-call | flops 110000000 | bytes 396000 | tf_op jit(solution)/shard_map/cond/branch_1_fun/pallas_call | solution.py:701
  228.5 11.0 %shard_map.299 = (bf16[512,1024]{1,0:T(8,128)(2,1)}, f32[8,1024]{1,0:T(8,128)S(1)}) custom-call(s32[4]{0:T(128)S(1)} %pad_add_fusion.who, bf16[512,1024]{1,0:T(8,128)(2,1)S(1)} %copy-done, bf16[48,1024]{1,0:T(8,128)(2,1)S(1)} %copy-done.24, f32[512,1024]{1,0:T(8,128)} %get-tuple-element.486.d_hidden, bf16[512,2048]{1,0:T(8,128)(2,1)} %get-tuple-element.478.d_qkv, ...), custom_call_target="tpu_custom_call" | custom-call | flops 100000000 | bytes 360000 | tf_op jit(solution)/shard_map/pallas_call | solution.py:764
  252.8 5.3 %shard_map.300 = (bf16[2,2,4,32,2176]{4,3,2,1,0:T(8,128)(2,1)}, bf16[2,4,32,2176]{3,2,1,0:T(8,128)(2,1)S(1)}, bf16[2,4,32,2176]{3,2,1,0:T(8,128)(2,1)}) custom-call(s32[4]{0:T(128)S(1)} %pad_add_fusion.who, bf16[512,1024]{1,0:T(8,128)(2,1)S(1)} %copy-done.17, bf16[512,2048]{1,0:T(8,128)(2,1)S(1)} %copy-done.11, ...), custom_call_target="tpu_custom_call" | custom-call | flops 100000000 | bytes 360000 | tf_op jit(solution)/shard_map/pallas_call | solution.py:827
  263.3 4.5 %conditional.11 = (bf16[2,4,32,2176]{3,2,1,0:T(8,128)(2,1)S(1)}) conditional(s32[]{:T(128)} %convert_element_type.781, () %tuple.198, (bf16[2,2,4,32,2176]{4,3,2,1,0:T(8,128)(2,1)}, bf16[2,4,32,2176]{3,2,1,0:T(8,128)(2,1)}) %tuple.199), branch_computations={%region_10.11_spmd, %region_11.12_spmd} | conditional | flops 2228224 | bytes 7798832 | solution.py:960
  274.0 10.6 %collective-permute-done.51 = bf16[96,1024]{1,0:T(8,128)(2,1)S(1)} collective-permute-done((bf16[96,1024]{1,0:T(8,128)(2,1)S(1)}, bf16[96,1024]{1,0:T(8,128)(2,1)S(1)}, u32[]{:S(2)}, u32[]{:S(2)}) %collective-permute-start.51) | collective-permute-done | bytes 196640 | tf_op jit(solution)/shard_map/ppermute | solution.py:945
  294.3 4.6 %collective-permute-done.54 = bf16[96,1024]{1,0:T(8,128)(2,1)S(1)} collective-permute-done((bf16[96,1024]{1,0:T(8,128)(2,1)S(1)}, bf16[96,1024]{1,0:T(8,128)(2,1)S(1)}, u32[]{:S(2)}, u32[]{:S(2)}) %collective-permute-start.54) | collective-permute-done | bytes 196640 | tf_op jit(solution)/shard_map/ppermute | solution.py:945
  319.2 4.6 %shard_map.301 = (f32[512,2816]{1,0:T(8,128)}, f32[512,2816]{1,0:T(8,128)}, f32[1408,1024]{1,0:T(8,128)}) custom-call(s32[4]{0:T(128)S(1)} %pad_add_fusion.who, bf16[4,96,768]{2,1,0:T(8,128)(2,1)S(1)} %pad_maximum_fusion.2.a, bf16[4,96,768]{2,1,0:T(8,128)(2,1)S(1)} %collective-permute-done.59.b, bf16[4,96,768]{2,1,0:T(8,128)(2,1)S(1)} %collective-permute-done.60.c, ...), custom_call_target="tpu_custom_call" | custom-call | flops 60000000 | bytes 216000 | tf_op jit(solution)/shard_map/pallas_call | solution.py:917
  323.8 6.3 %collective-permute-done.55 = bf16[4,32,2176]{2,1,0:T(8,128)(2,1)S(1)} collective-permute-done((bf16[4,32,2176]{2,1,0:T(8,128)(2,1)S(1)}, bf16[4,32,2176]{2,1,0:T(8,128)(2,1)S(1)}, u32[]{:S(2)}, u32[]{:S(2)}) %collective-permute-start.55) | collective-permute-done | bytes 557088 | tf_op jit(solution)/shard_map/ppermute | solution.py:945
  334.1 6.0 %collective-permute-done.62 = bf16[2,32,2176]{2,1,0:T(8,128)(2,1)S(1)} collective-permute-done((bf16[2,32,2176]{2,1,0:T(8,128)(2,1)S(1)}, bf16[2,32,2176]{2,1,0:T(8,128)(2,1)S(1)}, u32[]{:S(2)}, u32[]{:S(2)}) %collective-permute-start.62) | collective-permute-done | bytes 278560 | tf_op jit(solution)/shard_map/ppermute | solution.py:945
  340.3 6.4 %collective-permute-done.65 = bf16[32,2176]{1,0:T(8,128)(2,1)S(1)} collective-permute-done((bf16[32,2176]{1,0:T(8,128)(2,1)S(1)}, bf16[32,2176]{1,0:T(8,128)(2,1)S(1)}, u32[]{:S(2)}, u32[]{:S(2)}) %collective-permute-start.65) | collective-permute-done | bytes 139296 | tf_op jit(solution)/shard_map/ppermute | solution.py:945
  351.5 5.8 %shard_map.302 = (f32[512,2816]{1,0:T(8,128)}, f32[512,2816]{1,0:T(8,128)}, f32[1408,1024]{1,0:T(8,128)}) custom-call(s32[4]{0:T(128)S(1)} %pad_add_fusion.who, bf16[4,96,1024]{2,1,0:T(8,128)(2,1)S(1)} %pad_maximum_fusion.a, bf16[4,96,1024]{2,1,0:T(8,128)(2,1)S(1)} %collective-permute-done.68.b, ...), custom_call_target="tpu_custom_call", output_to_operand_aliasing={{0}: (5, {}), {1}: (6, {}), {2}: (7, {})} | custom-call | flops 80000000 | bytes 288000 | tf_op jit(solution)/shard_map/pallas_call | solution.py:917
  357.4 4.0 %collective-permute-done.72 = bf16[2,32,2048]{2,1,0:T(8,128)(2,1)S(1)} collective-permute-done((bf16[2,32,2048]{2,1,0:T(8,128)(2,1)S(1)}, bf16[2,32,2048]{2,1,0:T(8,128)(2,1)S(1)}, u32[]{:S(2)}, u32[]{:S(2)}) %collective-permute-start.72) | collective-permute-done | bytes 262176 | tf_op jit(solution)/shard_map/ppermute | solution.py:945
  361.6 6.2 %collective-permute-done.73.b = bf16[4,96,1024]{2,1,0:T(8,128)(2,1)S(1)} collective-permute-done((bf16[4,96,1024]{2,1,0:T(8,128)(2,1)S(1)}, bf16[4,96,1024]{2,1,0:T(8,128)(2,1)S(1)}, u32[]{:S(2)}, u32[]{:S(2)}) %collective-permute-start.73) | collective-permute-done | bytes 786464 | tf_op jit(solution)/shard_map/ppermute | solution.py:945
  371.2 5.8 %shard_map.303 = (f32[512,2816]{1,0:T(8,128)}, f32[512,2816]{1,0:T(8,128)}, f32[1408,1024]{1,0:T(8,128)}) custom-call(s32[4]{0:T(128)S(1)} %pad_add_fusion.who, bf16[4,96,1024]{2,1,0:T(8,128)(2,1)S(1)} %pad_maximum_fusion.1.a, bf16[4,96,1024]{2,1,0:T(8,128)(2,1)S(1)} %collective-permute-done.73.b, ...), custom_call_target="tpu_custom_call", output_to_operand_aliasing={{0}: (5, {}), {1}: (6, {}), {2}: (7, {})} | custom-call | flops 80000000 | bytes 288000 | tf_op jit(solution)/shard_map/pallas_call | solution.py:917
  384.5 5.6 %collective-permute-done.79.b = bf16[4,32,2176]{2,1,0:T(8,128)(2,1)S(1)} collective-permute-done((bf16[4,32,2176]{2,1,0:T(8,128)(2,1)S(1)}, bf16[4,32,2176]{2,1,0:T(8,128)(2,1)S(1)}, u32[]{:S(2)}, u32[]{:S(2)}) %collective-permute-start.79) | collective-permute-done | bytes 557088 | tf_op jit(solution)/shard_map/ppermute | solution.py:945
  (323 shorter events, 198.5 us)
Async XLA Ops:
  32.2 16.8 %collective-permute-start.18 = (bf16[128,2304]{1,0:T(8,128)(2,1)}, bf16[128,2304]{1,0:T(8,128)(2,1)}, u32[]{:S(2)}, u32[]{:S(2)}) collective-permute-start(bf16[128,2304]{1,0:T(8,128)(2,1)} %shard_map.288), channel_id=1, source_target_pairs={{0,1},{1,0},{2,3},{3,2},{4,5},{5,4},{6,7},{7,6},{8,9},{9,8},{10,11... | collective-permute-start | bytes 1769480 | tf_op jit(solution)/shard_map/ppermute | solution.py:949
  68.2 20.2 %collective-permute-start.23 = (bf16[128,3072]{1,0:T(8,128)(2,1)}, bf16[128,3072]{1,0:T(8,128)(2,1)S(1)}, u32[]{:S(2)}, u32[]{:S(2)}) collective-permute-start(bf16[128,3072]{1,0:T(8,128)(2,1)} %shard_map.289), channel_id=1, source_target_pairs={{0,1},{1,0},{2,3},{3,2},{4,5},{5,4},{6,7},{7,6},{8,9},{9,8},{10,11... | collective-permute-start | bytes 2359304 | tf_op jit(solution)/shard_map/ppermute | solution.py:949
  88.4 19.1 %collective-permute-start.29 = (bf16[128,3072]{1,0:T(8,128)(2,1)S(1)}, bf16[128,3072]{1,0:T(8,128)(2,1)S(1)}, u32[]{:S(2)}, u32[]{:S(2)}) collective-permute-start(bf16[128,3072]{1,0:T(8,128)(2,1)S(1)} %collective-permute-done.23.r0), channel_id=1, source_target_pairs={{0,4},{2,6},{4,0},{6,2},{8,12},{10,14},{12,8},{14,10},{16,20},{18,... | collective-permute-start | bytes 2359304 | tf_op jit(solution)/shard_map/ppermute | solution.py:945
  89.9 17.6 %collective-permute-start.28 = (bf16[128,3072]{1,0:T(8,128)(2,1)S(1)}, bf16[128,3072]{1,0:T(8,128)(2,1)S(1)}, u32[]{:S(2)}, u32[]{:S(2)}) collective-permute-start(bf16[128,3072]{1,0:T(8,128)(2,1)S(1)} %collective-permute-done.23.r0), channel_id=1, source_target_pairs={{0,2},{2,0},{4,6},{6,4},{8,10},{10,8},{12,14},{14,12},{16,18},{18,... | collective-permute-start | bytes 2359304 | tf_op jit(solution)/shard_map/ppermute | solution.py:945
  89.9 26.3 %collective-permute-start.31 = (bf16[128,3072]{1,0:T(8,128)(2,1)}, bf16[128,3072]{1,0:T(8,128)(2,1)}, u32[]{:S(2)}, u32[]{:S(2)}) collective-permute-start(bf16[128,3072]{1,0:T(8,128)(2,1)} %shard_map.290), channel_id=1, source_target_pairs={{0,1},{1,0},{2,3},{3,2},{4,5},{5,4},{6,7},{7,6},{8,9},{9,8},{10,11... | collective-permute-start | bytes 2359304 | tf_op jit(solution)/shard_map/ppermute | solution.py:949
  116.2 30.0 %collective-permute-start.32 = (bf16[2,4,96,768]{3,2,1,0:T(8,128)(2,1)}, bf16[2,4,96,768]{3,2,1,0:T(8,128)(2,1)}, u32[]{:S(2)}, u32[]{:S(2)}) collective-permute-start(bf16[2,4,96,768]{3,2,1,0:T(8,128)(2,1)} %get-tuple-element.435), channel_id=1, source_target_pairs={{0,1},{1,0},{2,3},{3,2},{4,5},{5,4},{6,7},{7,6},{8,9},{9,8},{10,11... | collective-permute-start | bytes 3538952 | tf_op jit(solution)/shard_map/ppermute | solution.py:949
  117.9 28.3 %collective-permute-start.30 = (bf16[2,4,96,768]{3,2,1,0:T(8,128)(2,1)}, bf16[2,4,96,768]{3,2,1,0:T(8,128)(2,1)}, u32[]{:S(2)}, u32[]{:S(2)}) collective-permute-start(bf16[2,4,96,768]{3,2,1,0:T(8,128)(2,1)} %get-tuple-element.432), channel_id=1, source_target_pairs={{0,2},{2,0},{4,6},{6,4},{8,10},{10,8},{12,14},{14,12},{16,18},{18,... | collective-permute-start | bytes 3538952 | tf_op jit(solution)/shard_map/ppermute | solution.py:945
  117.9 19.1 %collective-permute-start.34 = (bf16[128,3072]{1,0:T(8,128)(2,1)}, bf16[128,3072]{1,0:T(8,128)(2,1)}, u32[]{:S(2)}, u32[]{:S(2)}) collective-permute-start(bf16[128,3072]{1,0:T(8,128)(2,1)} %collective-permute-done.31.r0), channel_id=1, source_target_pairs={{0,2},{2,0},{4,6},{6,4},{8,10},{10,8},{12,14},{14,12},{16,18},{18,... | collective-permute-start | bytes 2359304 | tf_op jit(solution)/shard_map/ppermute | solution.py:945
  118.4 19.8 %collective-permute-start.33 = (bf16[128,3072]{1,0:T(8,128)(2,1)}, bf16[128,3072]{1,0:T(8,128)(2,1)}, u32[]{:S(2)}, u32[]{:S(2)}) collective-permute-start(bf16[128,3072]{1,0:T(8,128)(2,1)} %collective-permute-done.31.r0), channel_id=1, source_target_pairs={{0,4},{2,6},{4,0},{6,2},{8,12},{10,14},{12,8},{14,10},{16,20},{18,... | collective-permute-start | bytes 2359304 | tf_op jit(solution)/shard_map/ppermute | solution.py:945
  147.9 40.3 %collective-permute-start.38 = (bf16[2,4,96,1024]{3,2,1,0:T(8,128)(2,1)}, bf16[2,4,96,1024]{3,2,1,0:T(8,128)(2,1)}, u32[]{:S(2)}, u32[]{:S(2)}) collective-permute-start(bf16[2,4,96,1024]{3,2,1,0:T(8,128)(2,1)} %get-tuple-element.460), channel_id=1, source_target_pairs={{0,1},{1,0},{2,3},{3,2},{4,5},{5,4},{6,7},{7,6},{8,9},{9,8},{10,11... | collective-permute-start | bytes 4718600 | tf_op jit(solution)/shard_map/ppermute | solution.py:949
  148.3 39.9 %collective-permute-start.37 = (bf16[2,4,96,1024]{3,2,1,0:T(8,128)(2,1)}, bf16[2,4,96,1024]{3,2,1,0:T(8,128)(2,1)}, u32[]{:S(2)}, u32[]{:S(2)}) collective-permute-start(bf16[2,4,96,1024]{3,2,1,0:T(8,128)(2,1)} %get-tuple-element.459), channel_id=1, source_target_pairs={{0,2},{2,0},{4,6},{6,4},{8,10},{10,8},{12,14},{14,12},{16,18},{18,... | collective-permute-start | bytes 4718600 | tf_op jit(solution)/shard_map/ppermute | solution.py:945
  148.3 18.5 %collective-permute-start.35 = (bf16[4,96,768]{2,1,0:T(8,128)(2,1)S(1)}, bf16[4,96,768]{2,1,0:T(8,128)(2,1)S(1)}, u32[]{:S(2)}, u32[]{:S(2)}) collective-permute-start(bf16[4,96,768]{2,1,0:T(8,128)(2,1)S(1)} %fusion.7), channel_id=1, source_target_pairs={{0,4},{2,6},{4,0},{6,2},{8,12},{10,14},{12,8},{14,10},{16,20},{18,... | collective-permute-start | bytes 1769480 | tf_op jit(solution)/shard_map/ppermute | solution.py:945
  169.6 17.3 %collective-permute-start.36 = (bf16[2,96,768]{2,1,0:T(8,128)(2,1)}, bf16[2,96,768]{2,1,0:T(8,128)(2,1)}, u32[]{:S(2)}, u32[]{:S(2)}) collective-permute-start(bf16[2,96,768]{2,1,0:T(8,128)(2,1)} %fusion.15), channel_id=1, source_target_pairs={{0,8},{2,10},{4,12},{6,14},{8,0},{10,2},{12,4},{14,6},{16,24},{18,... | collective-permute-start | bytes 884744 | tf_op jit(solution)/shard_map/ppermute | solution.py:945
  171.2 15.7 %collective-permute-start.8 = (bf16[2,4,96,1024]{3,2,1,0:T(8,128)(2,1)}, bf16[2,4,96,1024]{3,2,1,0:T(8,128)(2,1)}, u32[]{:S(2)}, u32[]{:S(2)}) collective-permute-start(bf16[2,4,96,1024]{3,2,1,0:T(8,128)(2,1)} %get-tuple-element.154), channel_id=1, source_target_pairs={{0,2},{2,0},{4,6},{6,4},{8,10},{10,8},{12,14},{14,12},{16,18},{18,... | collective-permute-start | bytes 4718600 | tf_op jit(solution)/shard_map/cond/branch_1_fun/ppermute | solution.py:945
  191.2 33.5 %collective-permute-start.42 = (bf16[4,96,1024]{2,1,0:T(8,128)(2,1)}, bf16[4,96,1024]{2,1,0:T(8,128)(2,1)}, u32[]{:S(2)}, u32[]{:S(2)}) collective-permute-start(bf16[4,96,1024]{2,1,0:T(8,128)(2,1)} %fusion.6), channel_id=1, source_target_pairs={{0,4},{2,6},{4,0},{6,2},{8,12},{10,14},{12,8},{14,10},{16,20},{18,... | collective-permute-start | bytes 2359304 | tf_op jit(solution)/shard_map/ppermute | solution.py:945
  191.6 15.9 %collective-permute-start.39 = (bf16[96,768]{1,0:T(8,128)(2,1)S(1)}, bf16[96,768]{1,0:T(8,128)(2,1)S(1)}, u32[]{:S(2)}, u32[]{:S(2)}) collective-permute-start(bf16[96,768]{1,0:T(8,128)(2,1)S(1)} %fusion.28), channel_id=1, source_target_pairs={{0,16},{2,18},{4,20},{6,22},{8,24},{10,26},{12,28},{14,30},{16,0},... | collective-permute-start | bytes 442376 | tf_op jit(solution)/shard_map/ppermute | solution.py:945
  195.5 49.9 %collective-permute-start.46 = (bf16[2,4,96,1024]{3,2,1,0:T(8,128)(2,1)}, bf16[2,4,96,1024]{3,2,1,0:T(8,128)(2,1)}, u32[]{:S(2)}, u32[]{:S(2)}) collective-permute-start(bf16[2,4,96,1024]{3,2,1,0:T(8,128)(2,1)} %get-tuple-element.493), channel_id=1, source_target_pairs={{0,1},{1,0},{2,3},{3,2},{4,5},{5,4},{6,7},{7,6},{8,9},{9,8},{10,11... | collective-permute-start | bytes 4718600 | tf_op jit(solution)/shard_map/ppermute | solution.py:949
  226.9 33.2 %collective-permute-start.43 = (bf16[2,4,32,2048]{3,2,1,0:T(8,128)(2,1)}, bf16[2,4,32,2048]{3,2,1,0:T(8,128)(2,1)S(1)}, u32[]{:S(2)}, u32[]{:S(2)}) collective-permute-start(bf16[2,4,32,2048]{3,2,1,0:T(8,128)(2,1)} %get-tuple-element.483), channel_id=1, source_target_pairs={{0,1},{1,0},{2,3},{3,2},{4,5},{5,4},{6,7},{7,6},{8,9},{9,8},{10,11... | collective-permute-start | bytes 3145736 | tf_op jit(solution)/shard_map/ppermute | solution.py:949
  226.9 17.0 %collective-permute-start.45 = (bf16[2,96,1024]{2,1,0:T(8,128)(2,1)S(1)}, bf16[2,96,1024]{2,1,0:T(8,128)(2,1)S(1)}, u32[]{:S(2)}, u32[]{:S(2)}) collective-permute-start(bf16[2,96,1024]{2,1,0:T(8,128)(2,1)S(1)} %fusion.13), channel_id=1, source_target_pairs={{0,8},{2,10},{4,12},{6,14},{8,0},{10,2},{12,4},{14,6},{16,24},{18,... | collective-permute-start | bytes 1179656 | tf_op jit(solution)/shard_map/ppermute | solution.py:945
  248.5 20.9 %collective-permute-start.48 = (bf16[4,96,1024]{2,1,0:T(8,128)(2,1)}, bf16[4,96,1024]{2,1,0:T(8,128)(2,1)}, u32[]{:S(2)}, u32[]{:S(2)}) collective-permute-start(bf16[4,96,1024]{2,1,0:T(8,128)(2,1)} %fusion.5), channel_id=1, source_target_pairs={{0,4},{2,6},{4,0},{6,2},{8,12},{10,14},{12,8},{14,10},{16,20},{18,... | collective-permute-start | bytes 2359304 | tf_op jit(solution)/shard_map/ppermute | solution.py:945
  250.2 17.6 %collective-permute-start.47 = (bf16[96,1024]{1,0:T(8,128)(2,1)S(1)}, bf16[96,1024]{1,0:T(8,128)(2,1)S(1)}, u32[]{:S(2)}, u32[]{:S(2)}) collective-permute-start(bf16[96,1024]{1,0:T(8,128)(2,1)S(1)} %fusion.25), channel_id=1, source_target_pairs={{0,16},{2,18},{4,20},{6,22},{8,24},{10,26},{12,28},{14,30},{16,0},... | collective-permute-start | bytes 589832 | tf_op jit(solution)/shard_map/ppermute | solution.py:945
  271.2 15.9 %collective-permute-start.50 = (bf16[2,96,1024]{2,1,0:T(8,128)(2,1)S(1)}, bf16[2,96,1024]{2,1,0:T(8,128)(2,1)S(1)}, u32[]{:S(2)}, u32[]{:S(2)}) collective-permute-start(bf16[2,96,1024]{2,1,0:T(8,128)(2,1)S(1)} %fusion.11), channel_id=1, source_target_pairs={{0,8},{2,10},{4,12},{6,14},{8,0},{10,2},{12,4},{14,6},{16,24},{18,... | collective-permute-start | bytes 1179656 | tf_op jit(solution)/shard_map/ppermute | solution.py:945
  272.3 17.8 %collective-permute-start.49 = (bf16[4,32,2048]{2,1,0:T(8,128)(2,1)}, bf16[4,32,2048]{2,1,0:T(8,128)(2,1)S(1)}, u32[]{:S(2)}, u32[]{:S(2)}) collective-permute-start(bf16[4,32,2048]{2,1,0:T(8,128)(2,1)} %fusion.9), channel_id=1, source_target_pairs={{0,4},{2,6},{4,0},{6,2},{8,12},{10,14},{12,8},{14,10},{16,20},{18,... | collective-permute-start | bytes 1572872 | tf_op jit(solution)/shard_map/ppermute | solution.py:945
  274.0 31.6 %collective-permute-start.52 = (bf16[2,4,32,2176]{3,2,1,0:T(8,128)(2,1)S(1)}, bf16[2,4,32,2176]{3,2,1,0:T(8,128)(2,1)S(1)}, u32[]{:S(2)}, u32[]{:S(2)}) collective-permute-start(bf16[2,4,32,2176]{3,2,1,0:T(8,128)(2,1)S(1)} %get-tuple-element.521), channel_id=1, source_target_pairs={{0,2},{2,0},{4,6},{6,4},{8,10},{10,8},{12,14},{14,12},{16,18},{18,... | collective-permute-start | bytes 3342344 | tf_op jit(solution)/shard_map/ppermute | solution.py:945
  274.0 30.1 %collective-permute-start.53 = (bf16[2,4,32,2176]{3,2,1,0:T(8,128)(2,1)S(1)}, bf16[2,4,32,2176]{3,2,1,0:T(8,128)(2,1)S(1)}, u32[]{:S(2)}, u32[]{:S(2)}) collective-permute-start(bf16[2,4,32,2176]{3,2,1,0:T(8,128)(2,1)S(1)} %get-tuple-element.700), channel_id=1, source_target_pairs={{0,1},{1,0},{2,3},{3,2},{4,5},{5,4},{6,7},{7,6},{8,9},{9,8},{10,11... | collective-permute-start | bytes 3342344 | tf_op jit(solution)/shard_map/ppermute | solution.py:949
  284.6 21.1 %collective-permute-start.58 = (bf16[2,96,1024]{2,1,0:T(8,128)(2,1)S(1)}, bf16[2,96,1024]{2,1,0:T(8,128)(2,1)S(1)}, u32[]{:S(2)}, u32[]{:S(2)}) collective-permute-start(bf16[2,96,1024]{2,1,0:T(8,128)(2,1)S(1)} %pad_maximum_fusion.7), channel_id=1, source_target_pairs={{0,8},{2,10},{4,12},{6,14},{8,0},{10,2},{12,4},{14,6},{16,24},{18,... | collective-permute-start | bytes 1179656 | tf_op jit(solution)/shard_map/ppermute | solution.py:945
  287.1 27.0 %collective-permute-start.59 = (bf16[4,96,768]{2,1,0:T(8,128)(2,1)S(1)}, bf16[4,96,768]{2,1,0:T(8,128)(2,1)S(1)}, u32[]{:S(2)}, u32[]{:S(2)}) collective-permute-start(bf16[4,96,768]{2,1,0:T(8,128)(2,1)S(1)} %pad_maximum_fusion.2.a), channel_id=1, source_target_pairs={{0,4},{2,6},{4,0},{6,2},{8,12},{10,14},{12,8},{14,10},{16,20},{18,... | collective-permute-start | bytes 1769480 | tf_op jit(solution)/shard_map/ppermute | solution.py:945
  316.7 17.2 %collective-permute-start.63 = (bf16[2,96,1024]{2,1,0:T(8,128)(2,1)S(1)}, bf16[2,96,1024]{2,1,0:T(8,128)(2,1)S(1)}, u32[]{:S(2)}, u32[]{:S(2)}) collective-permute-start(bf16[2,96,1024]{2,1,0:T(8,128)(2,1)S(1)} %pad_maximum_fusion.8), channel_id=1, source_target_pairs={{0,8},{2,10},{4,12},{6,14},{8,0},{10,2},{12,4},{14,6},{16,24},{18,... | collective-permute-start | bytes 1179656 | tf_op jit(solution)/shard_map/ppermute | solution.py:945
  317.1 29.7 %collective-permute-start.68 = (bf16[4,96,1024]{2,1,0:T(8,128)(2,1)S(1)}, bf16[4,96,1024]{2,1,0:T(8,128)(2,1)S(1)}, u32[]{:S(2)}, u32[]{:S(2)}) collective-permute-start(bf16[4,96,1024]{2,1,0:T(8,128)(2,1)S(1)} %pad_maximum_fusion.a), channel_id=1, source_target_pairs={{0,4},{2,6},{4,0},{6,2},{8,12},{10,14},{12,8},{14,10},{16,20},{18,... | collective-permute-start | bytes 2359304 | tf_op jit(solution)/shard_map/ppermute | solution.py:945
  347.4 20.4 %collective-permute-start.73 = (bf16[4,96,1024]{2,1,0:T(8,128)(2,1)S(1)}, bf16[4,96,1024]{2,1,0:T(8,128)(2,1)S(1)}, u32[]{:S(2)}, u32[]{:S(2)}) collective-permute-start(bf16[4,96,1024]{2,1,0:T(8,128)(2,1)S(1)} %pad_maximum_fusion.1.a), channel_id=1, source_target_pairs={{0,4},{2,6},{4,0},{6,2},{8,12},{10,14},{12,8},{14,10},{16,20},{18,... | collective-permute-start | bytes 2359304 | tf_op jit(solution)/shard_map/ppermute | solution.py:945
  361.5 17.5 %collective-permute-start.76 = (bf16[4,32,2048]{2,1,0:T(8,128)(2,1)S(1)}, bf16[4,32,2048]{2,1,0:T(8,128)(2,1)S(1)}, u32[]{:S(2)}, u32[]{:S(2)}) collective-permute-start(bf16[4,32,2048]{2,1,0:T(8,128)(2,1)S(1)} %pad_maximum_fusion.4.a), channel_id=1, source_target_pairs={{0,4},{2,6},{4,0},{6,2},{8,12},{10,14},{12,8},{14,10},{16,20},{18,... | collective-permute-start | bytes 1572872 | tf_op jit(solution)/shard_map/ppermute | solution.py:945
  368.4 21.7 %collective-permute-start.79 = (bf16[4,32,2176]{2,1,0:T(8,128)(2,1)S(1)}, bf16[4,32,2176]{2,1,0:T(8,128)(2,1)S(1)}, u32[]{:S(2)}, u32[]{:S(2)}) collective-permute-start(bf16[4,32,2176]{2,1,0:T(8,128)(2,1)S(1)} %pad_maximum_fusion.3.a), channel_id=1, source_target_pairs={{0,4},{2,6},{4,0},{6,2},{8,12},{10,14},{12,8},{14,10},{16,20},{18,... | collective-permute-start | bytes 1671176 | tf_op jit(solution)/shard_map/ppermute | solution.py:945
  (100 other events, 835.8 us)
